TPU v7x, 32 devices: a whole 2x2x4 slice. The times are simulated.
32 devices in a mesh: section: 4 (over x, core), dp: 8 (over z, y).
Axes of the slice: x: 2, y: 2, z: 4, core: 2. Of those that a mesh axis runs over, the one named last changes fastest.
Arguments:
- block_input: bfloat16 [2, 8, 1024, 768], P(None, 'dp'), may hold values from -6 to 6
- carried_state: float32 [4, 3, 2, 8, 768], P('section', None, None, 'dp'), may hold values from -21 to 21, as said below
- output_cotangent: bfloat16 [2, 8, 1024, 768], P(None, 'dp'), may hold values from -6 to 6
- in_weight: bfloat16 [4, 768, 3072], P('section'), may hold values from -0.21875 to 0.21875
- out_weight: bfloat16 [4, 3840, 768], P('section'), may hold values from -0.109375 to 0.109375
- norm_gain: float32 [4, 768], P('section'), may hold values from 0.5 to 1.5
- norm_bias: float32 [4, 768], P('section'), may hold values from -1.5 to 1.5
- mix_rates: float32 [4, 3, 768], P('section'), may hold values from 0.05 to 0.95
- wkv_params: float32 [4, 2, 768], P('section'), may hold values from -6 to 1, as said below
Outputs:
- section_outputs: bfloat16 [4, 2, 8, 1024, 768], P('section', None, 'dp')
- final_state: float32 [4, 2, 2, 8, 768], P('section', None, None, 'dp')
- last_normed: float32 [4, 2, 8, 768], P('section', None, 'dp')
- section_grads: bfloat16 [4, 2, 8, 1024, 768], P('section', None, 'dp')
- in_weight_grad: float32 [4, 768, 3072], P('section')
- out_weight_grad: float32 [4, 3840, 768], P('section')
- norm_gain_grad: float32 [4, 768], P('section')
- norm_bias_grad: float32 [4, 768], P('section')
- mix_rates_grad: float32 [4, 3, 768], P('section')
- wkv_params_grad: float32 [4, 2, 768], P('section')
Inputs may be any that keep to these rules, and one draw needn't show every extreme that they name: `carried_state`: row 2 (the denominator) is positive and row 1 is at most row 2 in magnitude. `wkv_params`: row 0 holds log decay rates, between -6 and -2.3; row 1 holds bonuses, between -1 and 1.
All inputs are finite; a program needn't handle non-finite values.
Results may differ from a plain program's by a relative error of at most 0.014.
Values may be sent and summed in bfloat16 or wider, within the bound.
A program may use at most 256 MiB of HBM per device.

v0:
```python
import jax
import jax.numpy as jnp
from jax import lax
from jax.sharding import PartitionSpec as P

BLOCK = 128


precise = lax.Precision.HIGHEST


def as_sent(array):

    def short(part):
        return part.astype(jnp.bfloat16) if part.dtype == jnp.float32 else part

    return jax.tree.map(short, array)


def passed_along(value, axis, steps):
    count = lax.axis_size(axis)
    leading, last = (max(0, -steps), min(count, count - steps))
    return lax.ppermute(value, axis, [(source, source + steps) for source in range(leading, last)])


def layer_norm(tokens, norm_gain, norm_bias):
    center = tokens - jnp.mean(tokens, axis=-1, keepdims=True)
    spread = jnp.mean(center * center, axis=-1, keepdims=True)
    return center * lax.rsqrt(spread + 1e-05) * norm_gain + norm_bias


def premix(tokens, norm_gain, norm_bias, mix_rates, previous):
    normed = layer_norm(tokens, norm_gain, norm_bias)
    shifted = jnp.concatenate([previous[:, None, :], normed[:, :-1, :]], axis=1)
    rate_rows = mix_rates[:, None, None, :]
    mixture = normed[None] * rate_rows + shifted[None] * (1.0 - rate_rows)
    return (mixture, normed[:, -1, :])


def project(left_operand, weight_matrix):
    return jnp.einsum(
        "xpr,rn->xpn", left_operand, weight_matrix, preferred_element_type=jnp.float32
    )


def weight_grad(left_operand, right_operand):
    return jnp.einsum(
        "ymq,ymp->qp", left_operand, right_operand, preferred_element_type=jnp.float32
    )


def back_proj(right_operand, weight_matrix):
    return jnp.einsum(
        "our,vr->ouv", right_operand, weight_matrix, preferred_element_type=jnp.float32
    )


def weighted_value_blocks(
    address_linear_map,
    content_linear_map,
    logged_fading,
    opening_item_reward,
    accruing_upper_sum,
    accruing_normalizer,
):
    seq_count, length, channels = address_linear_map.shape
    block_count = length // BLOCK
    feature_fading_speed = jnp.exp(logged_fading)
    offsets = jnp.arange(BLOCK, dtype=jnp.float32)[:, None]
    growth = jnp.exp(offsets * feature_fading_speed)
    growth_pair = jnp.concatenate([growth, growth], axis=-1)
    shrink = jnp.exp(-(offsets - 1.0) * feature_fading_speed)
    start_decay = jnp.exp(-offsets * feature_fading_speed)
    tail_decay = jnp.exp(-(BLOCK - 1.0) * feature_fading_speed)
    block_decay = jnp.exp(-BLOCK * feature_fading_speed)
    lower_mask = (offsets > offsets.T).astype(jnp.float32)
    key_blocks = address_linear_map.reshape(seq_count, block_count, BLOCK, channels).transpose(
        1, 0, 2, 3
    )
    value_blocks = content_linear_map.reshape(seq_count, block_count, BLOCK, channels).transpose(
        1, 0, 2, 3
    )

    def advance(running, blocks_in):
        present_upper_sum, present_normalizer = running
        present_address, present_content = blocks_in
        exp_keys = jnp.exp(present_address)
        exponentiated_reward = jnp.exp(opening_item_reward + present_address)
        weighted = jnp.concatenate([exp_keys * present_content, exp_keys], axis=-1) * growth_pair
        summed = jnp.einsum("ts,bsc->btc", lower_mask, weighted, precision=precise)
        prior_upper_sum = (
            shrink * summed[..., :channels] + start_decay * present_upper_sum[:, None, :]
        )
        prior_normalizer = (
            shrink * summed[..., channels:] + start_decay * present_normalizer[:, None, :]
        )
        returned_content = (prior_upper_sum + exponentiated_reward * present_content) / (
            prior_normalizer + exponentiated_reward
        )
        totals = jnp.sum(weighted, axis=1)
        present_upper_sum = tail_decay * totals[:, :channels] + block_decay * present_upper_sum
        present_normalizer = tail_decay * totals[:, channels:] + block_decay * present_normalizer
        return ((present_upper_sum, present_normalizer), returned_content)

    (accruing_upper_sum, accruing_normalizer), results = lax.scan(
        advance, (accruing_upper_sum, accruing_normalizer), (key_blocks, value_blocks)
    )
    return (
        results.transpose(1, 0, 2, 3).reshape(seq_count, length, channels),
        accruing_upper_sum,
        accruing_normalizer,
    )


def put_slot(store, value, slot, valid, axis_pos):
    previous = lax.dynamic_index_in_dim(store, slot, axis_pos, keepdims=False)
    return lax.dynamic_update_index_in_dim(store, jnp.where(valid, value, previous), slot, axis_pos)


def take_slot(store, slot, axis_pos):
    return lax.dynamic_index_in_dim(store, slot, axis_pos, keepdims=False)


def sum_grads(grad_parts):
    return (
        lax.psum_scatter(grad_parts[0], "dp", scatter_dimension=1, tiled=True),
        lax.psum_scatter(grad_parts[1], "dp", scatter_dimension=0, tiled=True),
        lax.psum_scatter(grad_parts[2], "dp", scatter_dimension=0, tiled=True),
        lax.psum_scatter(grad_parts[3], "dp", scatter_dimension=0, tiled=True),
        lax.psum_scatter(grad_parts[4], "dp", scatter_dimension=1, tiled=True),
        lax.psum_scatter(grad_parts[5], "dp", scatter_dimension=1, tiled=True),
    )


def shards(
    block_input,
    carried_state,
    output_cotangent,
    in_weight,
    out_weight,
    norm_gain,
    norm_bias,
    mix_rates,
    wkv_params,
):
    sections = lax.axis_size("section")
    section_index = lax.axis_index("section")
    section_kind = section_index % 2
    micro_count = block_input.shape[0]
    seq_count = block_input.shape[1]
    length = block_input.shape[2]
    channels = block_input.shape[3]
    hidden_width = in_weight.shape[2]
    weight_in = in_weight[0]
    weight_out = out_weight[0]
    gain_row = norm_gain[0]
    bias_row = norm_bias[0]
    rate_rows = mix_rates[0]
    wkv_rows = wkv_params[0]
    carried = carried_state[0]
    act_shape = (seq_count, length, channels)
    kept_shape = (3, seq_count, length, channels)
    state_shape = (3, seq_count, channels)
    zero_grads = (
        jnp.zeros(weight_in.shape, jnp.float32),
        jnp.zeros(weight_out.shape, jnp.float32),
        jnp.zeros(gain_row.shape, jnp.float32),
        jnp.zeros(bias_row.shape, jnp.float32),
        jnp.zeros(rate_rows.shape, jnp.float32),
        jnp.zeros(wkv_rows.shape, jnp.float32),
    )

    def spare_forward(act_in, initial_state):
        return (
            jnp.zeros(act_shape, jnp.bfloat16),
            jnp.zeros(kept_shape, jnp.float32),
            jnp.zeros(state_shape, jnp.float32),
        )

    def time_forward(act_in, initial_state):
        tokens = act_in.astype(jnp.float32)
        mixture, last_row = premix(tokens, gain_row, bias_row, rate_rows, initial_state[0])
        low_mix = mixture.astype(jnp.bfloat16)
        address_linear_map = project(low_mix[0], weight_in[:, :channels])
        content_linear_map = project(low_mix[2], weight_in[:, channels : 2 * channels])
        recept = project(low_mix[1], weight_in[:, 2 * channels : 3 * channels])
        weighted_avg, accruing_upper_sum, accruing_normalizer = weighted_value_blocks(
            address_linear_map,
            content_linear_map,
            wkv_rows[0],
            wkv_rows[1],
            initial_state[1],
            initial_state[2],
        )
        gated_mix = (jax.nn.sigmoid(recept) * weighted_avg).astype(jnp.bfloat16)
        branch = project(gated_mix, weight_in[:, 3 * channels :])
        returned_content = (tokens + branch).astype(jnp.bfloat16)
        kept_proj = jnp.stack([address_linear_map, content_linear_map, recept])
        return (
            returned_content,
            kept_proj,
            jnp.stack([last_row, accruing_upper_sum, accruing_normalizer]),
        )

    def channel_forward(act_in, initial_state):
        tokens = act_in.astype(jnp.float32)
        mixture, last_row = premix(tokens, gain_row, bias_row, rate_rows, initial_state[0])
        low_mix = mixture.astype(jnp.bfloat16)
        pre_act = project(low_mix[0], weight_in)
        hidden = jnp.square(jnp.maximum(pre_act, 0.0)).astype(jnp.bfloat16)
        key_value = project(hidden, weight_out[:hidden_width])
        recept = project(low_mix[1], weight_out[hidden_width:])
        returned_content = (tokens + jax.nn.sigmoid(recept) * key_value).astype(jnp.bfloat16)
        zero_rows = jnp.zeros_like(last_row)
        kept_proj = jnp.stack([key_value, recept, jnp.zeros_like(recept)])
        return (returned_content, kept_proj, jnp.stack([last_row, zero_rows, zero_rows]))

    def spare_backward(act_in, kept_in, upstream, initial_state):
        return (jnp.zeros(act_shape, jnp.bfloat16), zero_grads)

    def time_backward(act_in, kept_in, upstream, initial_state):
        tokens = act_in.astype(jnp.float32)

        def time_local_premix(tokens_in, gain_in, bias_in, rates_in):
            return premix(tokens_in, gain_in, bias_in, rates_in, initial_state[0])

        (mixture, last_row), premix_back = jax.vjp(
            time_local_premix, tokens, gain_row, bias_row, rate_rows
        )
        low_mix = mixture.astype(jnp.bfloat16)
        address_linear_map = kept_in[0]
        content_linear_map = kept_in[1]
        recept = kept_in[2]

        def here_scaled_content(
            address_arguments, content_arguments, fading_argument, reward_argument
        ):
            return weighted_value_blocks(
                address_arguments,
                content_arguments,
                fading_argument,
                reward_argument,
                initial_state[1],
                initial_state[2],
            )

        (weighted_avg, accruing_upper_sum, accruing_normalizer), scaled_content_reverse_pass = (
            jax.vjp(
                here_scaled_content,
                address_linear_map,
                content_linear_map,
                wkv_rows[0],
                wkv_rows[1],
            )
        )
        sig_recept = jax.nn.sigmoid(recept)
        gated_mix = (sig_recept * weighted_avg).astype(jnp.bfloat16)
        grad_output_w = weight_grad(gated_mix, upstream)
        grad_gated = back_proj(upstream, weight_in[:, 3 * channels :])
        grad_avg = grad_gated * sig_recept
        grad_recept = (grad_gated * weighted_avg * sig_recept * (1.0 - sig_recept)).astype(
            jnp.bfloat16
        )
        address_cotangent, content_cotangent, fading_cotangent_sum, reward_cotangent_sum = (
            scaled_content_reverse_pass(
                (grad_avg, jnp.zeros_like(accruing_upper_sum), jnp.zeros_like(accruing_normalizer))
            )
        )
        address_cotangent = address_cotangent.astype(jnp.bfloat16)
        content_cotangent = content_cotangent.astype(jnp.bfloat16)
        grad_in = jnp.concatenate(
            [
                weight_grad(low_mix[0], address_cotangent),
                weight_grad(low_mix[2], content_cotangent),
                weight_grad(low_mix[1], grad_recept),
                grad_output_w,
            ],
            axis=1,
        )
        grad_mix = jnp.stack(
            [
                back_proj(address_cotangent, weight_in[:, :channels]),
                back_proj(grad_recept, weight_in[:, 2 * channels : 3 * channels]),
                back_proj(content_cotangent, weight_in[:, channels : 2 * channels]),
            ]
        )
        grad_tokens, grad_gain, grad_bias, grad_rates = premix_back(
            (grad_mix, jnp.zeros_like(last_row))
        )
        grad_entry = (upstream.astype(jnp.float32) + grad_tokens).astype(jnp.bfloat16)
        return (
            grad_entry,
            (
                grad_in,
                jnp.zeros(weight_out.shape, jnp.float32),
                grad_gain,
                grad_bias,
                grad_rates,
                jnp.stack([fading_cotangent_sum, reward_cotangent_sum]),
            ),
        )

    def channel_backward(act_in, kept_in, upstream, initial_state):
        tokens = act_in.astype(jnp.float32)

        def channel_local_premix(tokens_in, gain_in, bias_in, rates_in):
            return premix(tokens_in, gain_in, bias_in, rates_in, initial_state[0])

        (mixture, last_row), premix_back = jax.vjp(
            channel_local_premix, tokens, gain_row, bias_row, rate_rows
        )
        low_mix = mixture.astype(jnp.bfloat16)
        pre_act = project(low_mix[0], weight_in)
        hidden = jnp.square(jnp.maximum(pre_act, 0.0)).astype(jnp.bfloat16)
        key_value = kept_in[0]
        recept = kept_in[1]
        sig_recept = jax.nn.sigmoid(recept)
        upstream_wide = upstream.astype(jnp.float32)
        grad_kv = (upstream_wide * sig_recept).astype(jnp.bfloat16)
        grad_recept = (upstream_wide * key_value * sig_recept * (1.0 - sig_recept)).astype(
            jnp.bfloat16
        )
        grad_value_w = weight_grad(hidden, grad_kv)
        grad_hidden = back_proj(grad_kv, weight_out[:hidden_width])
        grad_pre = (grad_hidden * 2.0 * jnp.maximum(pre_act, 0.0)).astype(jnp.bfloat16)
        grad_in = weight_grad(low_mix[0], grad_pre)
        grad_recept_w = weight_grad(low_mix[1], grad_recept)
        grad_key_mix = back_proj(grad_pre, weight_in)
        grad_mix = jnp.stack(
            [
                grad_key_mix,
                back_proj(grad_recept, weight_out[hidden_width:]),
                jnp.zeros_like(grad_key_mix),
            ]
        )
        grad_tokens, grad_gain, grad_bias, grad_rates = premix_back(
            (grad_mix, jnp.zeros_like(last_row))
        )
        grad_entry = (upstream_wide + grad_tokens).astype(jnp.bfloat16)
        return (
            grad_entry,
            (
                grad_in,
                jnp.concatenate([grad_value_w, grad_recept_w], axis=0),
                grad_gain,
                grad_bias,
                grad_rates,
                jnp.zeros(wkv_rows.shape, jnp.float32),
            ),
        )

    base_tick = micro_count + sections - 1
    tick_count = base_tick + micro_count + sections - 1

    def tick(moment, running):
        recv_act, recv_grad, stash_in, kept_store, outputs, entry_grads, finals, grad_total = (
            running
        )
        fwd_micro = moment - section_index
        fwd_valid = (fwd_micro >= 0) & (fwd_micro < micro_count)
        fwd_slot = jnp.clip(fwd_micro, 0, micro_count - 1)
        fresh = take_slot(block_input, fwd_slot, 0)
        act_in = jnp.where(section_index == 0, fresh, recv_act)
        initial_state = take_slot(carried, fwd_slot, 1)
        fwd_branch = jnp.where(fwd_valid, 1 + section_kind, 0)
        returned_content, kept_new, final_new = lax.switch(
            fwd_branch, [spare_forward, time_forward, channel_forward], act_in, initial_state
        )
        stash_in = put_slot(stash_in, act_in, fwd_slot, fwd_valid, 0)
        kept_store = put_slot(kept_store, kept_new, fwd_slot, fwd_valid, 0)
        outputs = put_slot(outputs, returned_content, fwd_slot, fwd_valid, 0)
        finals = put_slot(finals, final_new, fwd_slot, fwd_valid, 1)
        sent_act = jax.tree.map(
            lambda part, own: part.astype(own.dtype),
            passed_along(as_sent(returned_content), "section", 1),
            returned_content,
        )
        back_micro = moment - base_tick - (sections - 1 - section_index)
        back_valid = (back_micro >= 0) & (back_micro < micro_count)
        back_slot = jnp.clip(back_micro, 0, micro_count - 1)
        cotangent = take_slot(output_cotangent, back_slot, 0)
        upstream = jnp.where(section_index == sections - 1, cotangent, recv_grad)
        back_branch = jnp.where(back_valid, 1 + section_kind, 0)
        grad_entry, grad_parts = lax.switch(
            back_branch,
            [spare_backward, time_backward, channel_backward],
            take_slot(stash_in, back_slot, 0),
            take_slot(kept_store, back_slot, 0),
            upstream,
            take_slot(carried, back_slot, 1),
        )
        grad_total = jax.tree.map(jnp.add, grad_total, grad_parts)
        entry_grads = put_slot(entry_grads, grad_entry, back_slot, back_valid, 0)
        sent_grad = jax.tree.map(
            lambda part, own: part.astype(own.dtype),
            passed_along(as_sent(grad_entry), "section", -1),
            grad_entry,
        )
        return (sent_act, sent_grad, stash_in, kept_store, outputs, entry_grads, finals, grad_total)

    running = (
        jnp.zeros(act_shape, jnp.bfloat16),
        jnp.zeros(act_shape, jnp.bfloat16),
        jnp.zeros((micro_count,) + act_shape, jnp.bfloat16),
        jnp.zeros((micro_count,) + kept_shape, jnp.float32),
        jnp.zeros((micro_count,) + act_shape, jnp.bfloat16),
        jnp.zeros((micro_count,) + act_shape, jnp.bfloat16),
        jnp.zeros(carried.shape, jnp.float32),
        zero_grads,
    )
    running = lax.fori_loop(0, tick_count, tick, running)
    reduced = sum_grads(running[7])
    gathered = (
        lax.all_gather(reduced[0].astype(jnp.bfloat16), "dp", axis=1, tiled=True).astype(
            jnp.float32
        ),
        lax.all_gather(reduced[1].astype(jnp.bfloat16), "dp", axis=0, tiled=True).astype(
            jnp.float32
        ),
        lax.all_gather(reduced[2].astype(jnp.bfloat16), "dp", axis=0, tiled=True).astype(
            jnp.float32
        ),
        lax.all_gather(reduced[3].astype(jnp.bfloat16), "dp", axis=0, tiled=True).astype(
            jnp.float32
        ),
        lax.all_gather(reduced[4].astype(jnp.bfloat16), "dp", axis=1, tiled=True).astype(
            jnp.float32
        ),
        lax.all_gather(reduced[5].astype(jnp.bfloat16), "dp", axis=1, tiled=True).astype(
            jnp.float32
        ),
    )
    outputs = running[4]
    entry_grads = running[5]
    finals = running[6]
    return (
        outputs[None],
        finals[1:][None],
        finals[0][None],
        entry_grads[None],
        gathered[0][None],
        gathered[1][None],
        gathered[2][None],
        gathered[3][None],
        gathered[4][None],
        gathered[5][None],
    )


def solution(mesh):
    return jax.shard_map(
        shards,
        mesh=mesh,
        in_specs=(
            P(None, "dp", None, None),
            P("section", None, None, "dp", None),
            P(None, "dp", None, None),
            P("section", None, None),
            P("section", None, None),
            P("section", None),
            P("section", None),
            P("section", None, None),
            P("section", None, None),
        ),
        out_specs=(
            P("section", None, "dp", None, None),
            P("section", None, None, "dp", None),
            P("section", None, "dp", None),
            P("section", None, "dp", None, None),
            P("section", None, None),
            P("section", None, None),
            P("section", None),
            P("section", None),
            P("section", None, None),
            P("section", None, None),
        ),
        check_vma=False,
    )
```

profile of v0, /device:TPU:0, one launch (start us, length us, event | category | flops | bytes accessed | tf_op | source)
XLA Modules:
  0.0 3394.4 jit_solution(17901491923954245081)
XLA Ops:
  23.9 2674.6 %while.141 = (s32[]{:T(128)}, bf16[1,1024,768]{2,1,0:T(8,128)(2,1)}, bf16[1,1024,768]{2,1,0:T(8,128)(2,1)}, bf16[2,1,1024,768]{3,2,1,0:T(8,128)(2,1)S(1)}, f32[2...) while((s32[]{:T(128)}, bf16[1,1024,768]{2,1,0:T(8,128)(2,1)}, ...), condition=%wide.region_45.46_spmd.clone.clone, body=%wide.region_0.45_spmd.clone.sunk.clone | while | flops 37607399424 | bytes 787352320 | solution.py:411
  37.0 63.0 %conditional.8 = (bf16[1,1024,768]{2,1,0:T(8,128)(2,1)}, f32[3,1,1024,768]{3,2,1,0:T(8,128)}, f32[3,1,768]{2,1,0:T(1,128)S(1)}) conditional(s32[]{:T(128)} %clamp.26, () %tuple.343, (bf16[1,1024,768]{2,1,0:T(8,128)(2,1)S(1)}, f32[1,768]{1,0:T(1,128)S(1)}, f32[1,768]{1,0:T(1,128)S(1)}, f32[1,3,768]{2,1,0:T(4,128)S(1)}, ...), branch_computations={%region_1.1_spmd, %region_2.7_spmd, %region_8.10_spmd} | conditional | flops 10910174208 | bytes 173242368 | solution.py:366
  48.5 34.0 %while.138 = (s32[]{:T(128)}, f32[1,768]{1,0:T(1,128)S(1)}, f32[1,768]{1,0:T(1,128)S(1)}, f32[8,1,128,768]{3,2,0,1:T(8,128)}, f32[768]{0:T(1024)S(1)}, /*index=5...) while((s32[]{:T(128)}, f32[1,768]{1,0:T(1,128)S(1)}, ...), condition=%wide.region_7.6_spmd.clone.clone.clone, body=%wide.region_5.5_spmd.clone.clone.sunk.clone | while | flops 304385024 | bytes 12652165 | solution.py:105
  124.2 16.1 conditional.9
  151.1 12.4 select_add_fusion.23
  187.9 62.6 %conditional.8 = (bf16[1,1024,768]{2,1,0:T(8,128)(2,1)}, f32[3,1,1024,768]{3,2,1,0:T(8,128)}, f32[3,1,768]{2,1,0:T(1,128)S(1)}) conditional(s32[]{:T(128)} %clamp.26, () %tuple.343, (bf16[1,1024,768]{2,1,0:T(8,128)(2,1)S(1)}, f32[1,768]{1,0:T(1,128)S(1)}, f32[1,768]{1,0:T(1,128)S(1)}, f32[1,3,768]{2,1,0:T(4,128)S(1)}, ...), branch_computations={%region_1.1_spmd, %region_2.7_spmd, %region_8.10_spmd} | conditional | flops 10910174208 | bytes 173242368 | solution.py:366
  199.5 34.0 %while.138 = (s32[]{:T(128)}, f32[1,768]{1,0:T(1,128)S(1)}, f32[1,768]{1,0:T(1,128)S(1)}, f32[8,1,128,768]{3,2,0,1:T(8,128)}, f32[768]{0:T(1024)S(1)}, /*index=5...) while((s32[]{:T(128)}, f32[1,768]{1,0:T(1,128)S(1)}, ...), condition=%wide.region_7.6_spmd.clone.clone.clone, body=%wide.region_5.5_spmd.clone.clone.sunk.clone | while | flops 304385024 | bytes 12652165 | solution.py:105
  274.8 16.4 conditional.9
  301.9 15.4 select_add_fusion.23
  378.0 16.1 conditional.9
  395.7 30.9 collective-permute-start
  430.1 15.4 select_add_fusion.23
  447.9 11.5 select_add_fusion.22
  506.2 16.4 conditional.9
  524.2 17.4 collective-permute-start
  545.1 15.4 select_add_fusion.23
  621.1 16.1 conditional.9
  638.8 59.7 %collective-permute-start = (bf16[1,1024,768]{2,1,0:T(8,128)(2,1)}, bf16[1,1024,768]{2,1,0:T(8,128)(2,1)}, u32[]{:S(2)}, u32[]{:S(2)}) collective-permute-start(bf16[1,1024,768]{2,1,0:T(8,128)(2,1)} %get-tuple-element.4146), channel_id=1, source_target_pairs={{0,8},{8,16},{16,24},{1,9},{9,17},{17,25},{2,10},{10,18},{18,26},{... | collective-permute-start | bytes 4718600 | tf_op jit(solution)/shard_map/while/body/eval_jaxpr/ppermute | solution.py:23
  702.1 15.4 select_add_fusion.23
  719.8 11.5 select_add_fusion.22
  778.1 16.4 conditional.9
  806.1 15.4 select_add_fusion.23
  882.1 16.1 conditional.9
  899.8 30.0 collective-permute-start
  933.3 15.4 select_add_fusion.23
  951.1 11.5 select_add_fusion.22
  1009.4 16.4 conditional.9
  1027.3 571.0 %collective-permute-start = (bf16[1,1024,768]{2,1,0:T(8,128)(2,1)}, bf16[1,1024,768]{2,1,0:T(8,128)(2,1)}, u32[]{:S(2)}, u32[]{:S(2)}) collective-permute-start(bf16[1,1024,768]{2,1,0:T(8,128)(2,1)} %get-tuple-element.4146), channel_id=1, source_target_pairs={{0,8},{8,16},{16,24},{1,9},{9,17},{17,25},{2,10},{10,18},{18,26},{... | collective-permute-start | bytes 4718600 | tf_op jit(solution)/shard_map/while/body/eval_jaxpr/ppermute | solution.py:23
  1601.9 15.4 select_add_fusion.23
  1619.7 11.5 select_add_fusion.22
  1678.0 442.7 %conditional.9 = (bf16[1,1024,768]{2,1,0:T(8,128)(2,1)}, f32[768,3072]{0,1:T(8,128)}, f32[3840,768]{1,0:T(8,128)}, f32[768]{0:T(1024)}, f32[768]{0:T(1024)}, /*index=5*/f32[3,768]{1,0:T(4,128)}, f32[2,768]{1,0:T(2,128)}) conditional(s32[]{:T(128)} %clamp.27, () %tuple.346, (bf16[1,1024,768]{2,1,0:T(8,128)(2,1)}, ...), branch_computations={%region_11.11_spmd, %region_12.33_spmd, %region_34.44_spmd} | conditional | flops 26680301568 | bytes 335687072 | solution.py:384
  1691.5 161.4 %while.139 = (s32[]{:T(128)}, f32[1,768]{1,0:T(1,128)S(1)}, f32[1,768]{1,0:T(1,128)S(1)}, f32[8,1,128,768]{3,2,0,1:T(8,128)}, f32[8,1,128,768]{2,3,1,0:T(8,128)}...) while((s32[]{:T(128)}, f32[1,768]{1,0:T(1,128)S(1)}, ...), condition=%wide.region_15.14_spmd.clone.clone.clone, body=%wide.region_13.13_spmd.clone.clone.sunk.clone | while | flops 304974848 | bytes 19403552 | solution.py:105
  1863.1 192.6 %while.140 = (s32[]{:T(128)}, f32[768]{0:T(1024)}, f32[128,1536]{0,1:T(8,128)}, f32[128,768]{0,1:T(8,128)}, f32[128,768]{0,1:T(8,128)}, /*index=5*/f32[768]{0:T(...) while((s32[]{:T(128)}, f32[768]{0:T(1024)}, ...), condition=%wide.region_20.19_spmd.clone.clone.clone.clone, body=%wide.region_16.18_spmd.clone.clone.clone.sunk.clone | while | flops 306657536 | bytes 26908196 | solution.py:105
  2136.0 15.4 select_add_fusion.23
  2212.0 443.0 %conditional.9 = (bf16[1,1024,768]{2,1,0:T(8,128)(2,1)}, f32[768,3072]{0,1:T(8,128)}, f32[3840,768]{1,0:T(8,128)}, f32[768]{0:T(1024)}, f32[768]{0:T(1024)}, /*index=5*/f32[3,768]{1,0:T(4,128)}, f32[2,768]{1,0:T(2,128)}) conditional(s32[]{:T(128)} %clamp.27, () %tuple.346, (bf16[1,1024,768]{2,1,0:T(8,128)(2,1)}, ...), branch_computations={%region_11.11_spmd, %region_12.33_spmd, %region_34.44_spmd} | conditional | flops 26680301568 | bytes 335687072 | solution.py:384
  2225.7 161.4 %while.139 = (s32[]{:T(128)}, f32[1,768]{1,0:T(1,128)S(1)}, f32[1,768]{1,0:T(1,128)S(1)}, f32[8,1,128,768]{3,2,0,1:T(8,128)}, f32[8,1,128,768]{2,3,1,0:T(8,128)}...) while((s32[]{:T(128)}, f32[1,768]{1,0:T(1,128)S(1)}, ...), condition=%wide.region_15.14_spmd.clone.clone.clone, body=%wide.region_13.13_spmd.clone.clone.sunk.clone | while | flops 304974848 | bytes 19403552 | solution.py:105
  2397.3 192.8 %while.140 = (s32[]{:T(128)}, f32[768]{0:T(1024)}, f32[128,1536]{0,1:T(8,128)}, f32[128,768]{0,1:T(8,128)}, f32[128,768]{0,1:T(8,128)}, /*index=5*/f32[768]{0:T(...) while((s32[]{:T(128)}, f32[768]{0:T(1024)}, ...), condition=%wide.region_20.19_spmd.clone.clone.clone.clone, body=%wide.region_16.18_spmd.clone.clone.clone.sunk.clone | while | flops 306657536 | bytes 26908196 | solution.py:105
  2665.8 15.4 select_add_fusion.23
  2711.1 162.4 %reduce-scatter.9.cloned.1.call-done = f32[768,384]{1,0:T(8,128)} async-done(((f32[768,3072]{1,0:T(8,128)}), f32[768,384]{1,0:T(8,128)}) %reduce-scatter.9.cloned.1.call-update) | async-done | bytes 1179664 | tf_op jit(solution)/shard_map/reduce_scatter | solution.py:126
  2875.7 197.5 %reduce-scatter.11.cloned.1.call-done = f32[480,768]{1,0:T(8,128)} async-done(((f32[3840,768]{1,0:T(8,128)}), f32[480,768]{1,0:T(8,128)}) %reduce-scatter.11.cloned.1.call-update) | async-done | bytes 1474576 | tf_op jit(solution)/shard_map/reduce_scatter | solution.py:127
  3076.8 19.9 all-reduce.11
  3097.9 17.1 all-reduce.12
  3117.4 19.9 reduce-scatter.15.cloned.1.call-done
  3138.2 18.5 all-gather.1
  3157.3 43.8 %reduce-scatter.13.cloned.1.call-done = f32[96,3]{1,0:T(8,128)} async-done(((f32[768,3]{1,0:T(8,128)}), f32[96,3]{1,0:T(8,128)}) %reduce-scatter.13.cloned.1.call-update) | async-done | bytes 1168
  3202.0 18.7 all-gather
  3221.4 62.5 %all-gather.5.cloned.1.call-done = bf16[768,3072]{1,0:T(8,128)(2,1)} async-done(((bf16[768,384]{1,0:T(8,128)(2,1)}), bf16[768,3072]{1,0:T(8,128)(2,1)}) %all-gather.5.cloned.1.call-update) | async-done | bytes 4718608 | tf_op jit(solution)/shard_map/all_gather | solution.py:414
  3291.3 87.9 %all-gather.7.cloned.1.call-done = bf16[3840,768]{1,0:T(8,128)(2,1)} async-done(((bf16[480,768]{1,0:T(8,128)(2,1)}), bf16[3840,768]{1,0:T(8,128)(2,1)}) %all-gather.7.cloned.1.call-update) | async-done | bytes 5898256 | tf_op jit(solution)/shard_map/all_gather | solution.py:417
  (2253 shorter events, 1796.0 us)
Async XLA Ops:
  7.2 2866.3 %reduce-scatter.9.cloned.1.call-start = ((), (), s32[]{:S(2)}) async-start(), calls=%async_computation.4 | async-start | bytes 10616832 | tf_op jit(solution)/shard_map/reduce_scatter | solution.py:126
  24.2 100.0 %copy-start.32 = (f32[1,3,768]{2,1,0:T(4,128)}, f32[1,3,768]{2,1,0:T(4,128)S(1)}, u32[]{:S(2)}) copy-start(f32[1,3,768]{2,1,0:T(4,128)S(1)} %get-tuple-element.4520) | copy-start | bytes 27652 | tf_op jit(solution)/shard_map/while
  140.3 34.2 %collective-permute-start.1 = (bf16[1,1024,768]{2,1,0:T(8,128)(2,1)}, bf16[1,1024,768]{2,1,0:T(8,128)(2,1)}, u32[]{:S(2)}, u32[]{:S(2)}) collective-permute-start(bf16[1,1024,768]{2,1,0:T(8,128)(2,1)} %get-tuple-element.4150), channel_id=1, source_target_pairs={{8,0},{16,8},{24,16},{9,1},{17,9},{25,17},{10,2},{18,10},{26,18},{... | collective-permute-start | bytes 4718600 | tf_op jit(solution)/shard_map/while/body/eval_jaxpr/ppermute | solution.py:23
  141.9 32.7 collective-permute-start
  175.1 99.7 %copy-start.32 = (f32[1,3,768]{2,1,0:T(4,128)}, f32[1,3,768]{2,1,0:T(4,128)S(1)}, u32[]{:S(2)}) copy-start(f32[1,3,768]{2,1,0:T(4,128)S(1)} %get-tuple-element.4520) | copy-start | bytes 27652 | tf_op jit(solution)/shard_map/while
  291.2 40.0 %collective-permute-start.1 = (bf16[1,1024,768]{2,1,0:T(8,128)(2,1)}, bf16[1,1024,768]{2,1,0:T(8,128)(2,1)}, u32[]{:S(2)}, u32[]{:S(2)}) collective-permute-start(bf16[1,1024,768]{2,1,0:T(8,128)(2,1)} %get-tuple-element.4150), channel_id=1, source_target_pairs={{8,0},{16,8},{24,16},{9,1},{17,9},{25,17},{10,2},{18,10},{26,18},{... | collective-permute-start | bytes 4718600 | tf_op jit(solution)/shard_map/while/body/eval_jaxpr/ppermute | solution.py:23
  292.8 38.5 %collective-permute-start = (bf16[1,1024,768]{2,1,0:T(8,128)(2,1)}, bf16[1,1024,768]{2,1,0:T(8,128)(2,1)}, u32[]{:S(2)}, u32[]{:S(2)}) collective-permute-start(bf16[1,1024,768]{2,1,0:T(8,128)(2,1)} %get-tuple-element.4146), channel_id=1, source_target_pairs={{0,8},{8,16},{16,24},{1,9},{9,17},{17,25},{2,10},{10,18},{18,26},{... | collective-permute-start | bytes 4718600 | tf_op jit(solution)/shard_map/while/body/eval_jaxpr/ppermute | solution.py:23
  301.9 17.0 copy-start.65
  331.5 46.5 %copy-start.32 = (f32[1,3,768]{2,1,0:T(4,128)}, f32[1,3,768]{2,1,0:T(4,128)S(1)}, u32[]{:S(2)}) copy-start(f32[1,3,768]{2,1,0:T(4,128)S(1)} %get-tuple-element.4520) | copy-start | bytes 27652 | tf_op jit(solution)/shard_map/while
  394.1 34.1 %copy-start.30 = (bf16[2,1,1024,768]{3,2,1,0:T(8,128)(2,1)S(1)}, bf16[2,1,1024,768]{3,2,1,0:T(8,128)(2,1)}, u32[]{:S(2)}) copy-start(bf16[2,1,1024,768]{3,2,1,0:T(8,128)(2,1)} %get-tuple-element.4477) | copy-start | bytes 9437188 | tf_op jit(solution)/shard_map/while
  394.1 65.3 %collective-permute-start.1 = (bf16[1,1024,768]{2,1,0:T(8,128)(2,1)}, bf16[1,1024,768]{2,1,0:T(8,128)(2,1)}, u32[]{:S(2)}, u32[]{:S(2)}) collective-permute-start(bf16[1,1024,768]{2,1,0:T(8,128)(2,1)} %get-tuple-element.4150), channel_id=1, source_target_pairs={{8,0},{16,8},{24,16},{9,1},{17,9},{25,17},{10,2},{18,10},{26,18},{... | collective-permute-start | bytes 4718600 | tf_op jit(solution)/shard_map/while/body/eval_jaxpr/ppermute | solution.py:23
  395.7 63.8 %collective-permute-start = (bf16[1,1024,768]{2,1,0:T(8,128)(2,1)}, bf16[1,1024,768]{2,1,0:T(8,128)(2,1)}, u32[]{:S(2)}, u32[]{:S(2)}) collective-permute-start(bf16[1,1024,768]{2,1,0:T(8,128)(2,1)} %get-tuple-element.4146), channel_id=1, source_target_pairs={{0,8},{8,16},{16,24},{1,9},{9,17},{17,25},{2,10},{10,18},{18,26},{... | collective-permute-start | bytes 4718600 | tf_op jit(solution)/shard_map/while/body/eval_jaxpr/ppermute | solution.py:23
  430.1 17.0 copy-start.65
  459.9 46.3 %copy-start.32 = (f32[1,3,768]{2,1,0:T(4,128)}, f32[1,3,768]{2,1,0:T(4,128)S(1)}, u32[]{:S(2)}) copy-start(f32[1,3,768]{2,1,0:T(4,128)S(1)} %get-tuple-element.4520) | copy-start | bytes 27652 | tf_op jit(solution)/shard_map/while
  522.6 20.6 copy-start.30
  522.6 51.8 %collective-permute-start.1 = (bf16[1,1024,768]{2,1,0:T(8,128)(2,1)}, bf16[1,1024,768]{2,1,0:T(8,128)(2,1)}, u32[]{:S(2)}, u32[]{:S(2)}) collective-permute-start(bf16[1,1024,768]{2,1,0:T(8,128)(2,1)} %get-tuple-element.4150), channel_id=1, source_target_pairs={{8,0},{16,8},{24,16},{9,1},{17,9},{25,17},{10,2},{18,10},{26,18},{... | collective-permute-start | bytes 4718600 | tf_op jit(solution)/shard_map/while/body/eval_jaxpr/ppermute | solution.py:23
  524.2 50.2 %collective-permute-start = (bf16[1,1024,768]{2,1,0:T(8,128)(2,1)}, bf16[1,1024,768]{2,1,0:T(8,128)(2,1)}, u32[]{:S(2)}, u32[]{:S(2)}) collective-permute-start(bf16[1,1024,768]{2,1,0:T(8,128)(2,1)} %get-tuple-element.4146), channel_id=1, source_target_pairs={{0,8},{8,16},{16,24},{1,9},{9,17},{17,25},{2,10},{10,18},{18,26},{... | collective-permute-start | bytes 4718600 | tf_op jit(solution)/shard_map/while/body/eval_jaxpr/ppermute | solution.py:23
  545.1 17.0 copy-start.65
  574.7 46.5 %copy-start.32 = (f32[1,3,768]{2,1,0:T(4,128)}, f32[1,3,768]{2,1,0:T(4,128)S(1)}, u32[]{:S(2)}) copy-start(f32[1,3,768]{2,1,0:T(4,128)S(1)} %get-tuple-element.4520) | copy-start | bytes 27652 | tf_op jit(solution)/shard_map/while
  637.3 62.9 %copy-start.30 = (bf16[2,1,1024,768]{3,2,1,0:T(8,128)(2,1)S(1)}, bf16[2,1,1024,768]{3,2,1,0:T(8,128)(2,1)}, u32[]{:S(2)}) copy-start(bf16[2,1,1024,768]{3,2,1,0:T(8,128)(2,1)} %get-tuple-element.4477) | copy-start | bytes 9437188 | tf_op jit(solution)/shard_map/while
  637.3 94.1 %collective-permute-start.1 = (bf16[1,1024,768]{2,1,0:T(8,128)(2,1)}, bf16[1,1024,768]{2,1,0:T(8,128)(2,1)}, u32[]{:S(2)}, u32[]{:S(2)}) collective-permute-start(bf16[1,1024,768]{2,1,0:T(8,128)(2,1)} %get-tuple-element.4150), channel_id=1, source_target_pairs={{8,0},{16,8},{24,16},{9,1},{17,9},{25,17},{10,2},{18,10},{26,18},{... | collective-permute-start | bytes 4718600 | tf_op jit(solution)/shard_map/while/body/eval_jaxpr/ppermute | solution.py:23
  638.8 92.5 %collective-permute-start = (bf16[1,1024,768]{2,1,0:T(8,128)(2,1)}, bf16[1,1024,768]{2,1,0:T(8,128)(2,1)}, u32[]{:S(2)}, u32[]{:S(2)}) collective-permute-start(bf16[1,1024,768]{2,1,0:T(8,128)(2,1)} %get-tuple-element.4146), channel_id=1, source_target_pairs={{0,8},{8,16},{16,24},{1,9},{9,17},{17,25},{2,10},{10,18},{18,26},{... | collective-permute-start | bytes 4718600 | tf_op jit(solution)/shard_map/while/body/eval_jaxpr/ppermute | solution.py:23
  731.9 46.3 %copy-start.32 = (f32[1,3,768]{2,1,0:T(4,128)}, f32[1,3,768]{2,1,0:T(4,128)S(1)}, u32[]{:S(2)}) copy-start(f32[1,3,768]{2,1,0:T(4,128)S(1)} %get-tuple-element.4520) | copy-start | bytes 27652 | tf_op jit(solution)/shard_map/while
  794.5 40.8 %collective-permute-start.1 = (bf16[1,1024,768]{2,1,0:T(8,128)(2,1)}, bf16[1,1024,768]{2,1,0:T(8,128)(2,1)}, u32[]{:S(2)}, u32[]{:S(2)}) collective-permute-start(bf16[1,1024,768]{2,1,0:T(8,128)(2,1)} %get-tuple-element.4150), channel_id=1, source_target_pairs={{8,0},{16,8},{24,16},{9,1},{17,9},{25,17},{10,2},{18,10},{26,18},{... | collective-permute-start | bytes 4718600 | tf_op jit(solution)/shard_map/while/body/eval_jaxpr/ppermute | solution.py:23
  796.1 39.3 %collective-permute-start = (bf16[1,1024,768]{2,1,0:T(8,128)(2,1)}, bf16[1,1024,768]{2,1,0:T(8,128)(2,1)}, u32[]{:S(2)}, u32[]{:S(2)}) collective-permute-start(bf16[1,1024,768]{2,1,0:T(8,128)(2,1)} %get-tuple-element.4146), channel_id=1, source_target_pairs={{0,8},{8,16},{16,24},{1,9},{9,17},{17,25},{2,10},{10,18},{18,26},{... | collective-permute-start | bytes 4718600 | tf_op jit(solution)/shard_map/while/body/eval_jaxpr/ppermute | solution.py:23
  835.6 46.5 %copy-start.32 = (f32[1,3,768]{2,1,0:T(4,128)}, f32[1,3,768]{2,1,0:T(4,128)S(1)}, u32[]{:S(2)}) copy-start(f32[1,3,768]{2,1,0:T(4,128)S(1)} %get-tuple-element.4520) | copy-start | bytes 27652 | tf_op jit(solution)/shard_map/while
  898.2 33.2 copy-start.30
  898.2 64.4 %collective-permute-start.1 = (bf16[1,1024,768]{2,1,0:T(8,128)(2,1)}, bf16[1,1024,768]{2,1,0:T(8,128)(2,1)}, u32[]{:S(2)}, u32[]{:S(2)}) collective-permute-start(bf16[1,1024,768]{2,1,0:T(8,128)(2,1)} %get-tuple-element.4150), channel_id=1, source_target_pairs={{8,0},{16,8},{24,16},{9,1},{17,9},{25,17},{10,2},{18,10},{26,18},{... | collective-permute-start | bytes 4718600 | tf_op jit(solution)/shard_map/while/body/eval_jaxpr/ppermute | solution.py:23
  899.8 62.8 %collective-permute-start = (bf16[1,1024,768]{2,1,0:T(8,128)(2,1)}, bf16[1,1024,768]{2,1,0:T(8,128)(2,1)}, u32[]{:S(2)}, u32[]{:S(2)}) collective-permute-start(bf16[1,1024,768]{2,1,0:T(8,128)(2,1)} %get-tuple-element.4146), channel_id=1, source_target_pairs={{0,8},{8,16},{16,24},{1,9},{9,17},{17,25},{2,10},{10,18},{18,26},{... | collective-permute-start | bytes 4718600 | tf_op jit(solution)/shard_map/while/body/eval_jaxpr/ppermute | solution.py:23
  963.1 46.3 %copy-start.32 = (f32[1,3,768]{2,1,0:T(4,128)}, f32[1,3,768]{2,1,0:T(4,128)S(1)}, u32[]{:S(2)}) copy-start(f32[1,3,768]{2,1,0:T(4,128)S(1)} %get-tuple-element.4520) | copy-start | bytes 27652 | tf_op jit(solution)/shard_map/while
  1025.7 574.3 %copy-start.30 = (bf16[2,1,1024,768]{3,2,1,0:T(8,128)(2,1)S(1)}, bf16[2,1,1024,768]{3,2,1,0:T(8,128)(2,1)}, u32[]{:S(2)}) copy-start(bf16[2,1,1024,768]{3,2,1,0:T(8,128)(2,1)} %get-tuple-element.4477) | copy-start | bytes 9437188 | tf_op jit(solution)/shard_map/while
  1025.8 605.5 %collective-permute-start.1 = (bf16[1,1024,768]{2,1,0:T(8,128)(2,1)}, bf16[1,1024,768]{2,1,0:T(8,128)(2,1)}, u32[]{:S(2)}, u32[]{:S(2)}) collective-permute-start(bf16[1,1024,768]{2,1,0:T(8,128)(2,1)} %get-tuple-element.4150), channel_id=1, source_target_pairs={{8,0},{16,8},{24,16},{9,1},{17,9},{25,17},{10,2},{18,10},{26,18},{... | collective-permute-start | bytes 4718600 | tf_op jit(solution)/shard_map/while/body/eval_jaxpr/ppermute | solution.py:23
  1027.3 603.9 %collective-permute-start = (bf16[1,1024,768]{2,1,0:T(8,128)(2,1)}, bf16[1,1024,768]{2,1,0:T(8,128)(2,1)}, u32[]{:S(2)}, u32[]{:S(2)}) collective-permute-start(bf16[1,1024,768]{2,1,0:T(8,128)(2,1)} %get-tuple-element.4146), channel_id=1, source_target_pairs={{0,8},{8,16},{16,24},{1,9},{9,17},{17,25},{2,10},{10,18},{18,26},{... | collective-permute-start | bytes 4718600 | tf_op jit(solution)/shard_map/while/body/eval_jaxpr/ppermute | solution.py:23
  1631.5 46.5 %copy-start.32 = (f32[1,3,768]{2,1,0:T(4,128)}, f32[1,3,768]{2,1,0:T(4,128)S(1)}, u32[]{:S(2)}) copy-start(f32[1,3,768]{2,1,0:T(4,128)S(1)} %get-tuple-element.4520) | copy-start | bytes 27652 | tf_op jit(solution)/shard_map/while
  2120.7 44.6 %collective-permute-start.1 = (bf16[1,1024,768]{2,1,0:T(8,128)(2,1)}, bf16[1,1024,768]{2,1,0:T(8,128)(2,1)}, u32[]{:S(2)}, u32[]{:S(2)}) collective-permute-start(bf16[1,1024,768]{2,1,0:T(8,128)(2,1)} %get-tuple-element.4150), channel_id=1, source_target_pairs={{8,0},{16,8},{24,16},{9,1},{17,9},{25,17},{10,2},{18,10},{26,18},{... | collective-permute-start | bytes 4718600 | tf_op jit(solution)/shard_map/while/body/eval_jaxpr/ppermute | solution.py:23
  2122.2 43.0 %collective-permute-start = (bf16[1,1024,768]{2,1,0:T(8,128)(2,1)}, bf16[1,1024,768]{2,1,0:T(8,128)(2,1)}, u32[]{:S(2)}, u32[]{:S(2)}) collective-permute-start(bf16[1,1024,768]{2,1,0:T(8,128)(2,1)} %get-tuple-element.4146), channel_id=1, source_target_pairs={{0,8},{8,16},{16,24},{1,9},{9,17},{17,25},{2,10},{10,18},{18,26},{... | collective-permute-start | bytes 4718600 | tf_op jit(solution)/shard_map/while/body/eval_jaxpr/ppermute | solution.py:23
  2165.8 46.3 %copy-start.32 = (f32[1,3,768]{2,1,0:T(4,128)}, f32[1,3,768]{2,1,0:T(4,128)S(1)}, u32[]{:S(2)}) copy-start(f32[1,3,768]{2,1,0:T(4,128)S(1)} %get-tuple-element.4520) | copy-start | bytes 27652 | tf_op jit(solution)/shard_map/while
  2655.0 40.0 %collective-permute-start.1 = (bf16[1,1024,768]{2,1,0:T(8,128)(2,1)}, bf16[1,1024,768]{2,1,0:T(8,128)(2,1)}, u32[]{:S(2)}, u32[]{:S(2)}) collective-permute-start(bf16[1,1024,768]{2,1,0:T(8,128)(2,1)} %get-tuple-element.4150), channel_id=1, source_target_pairs={{8,0},{16,8},{24,16},{9,1},{17,9},{25,17},{10,2},{18,10},{26,18},{... | collective-permute-start | bytes 4718600 | tf_op jit(solution)/shard_map/while/body/eval_jaxpr/ppermute | solution.py:23
  2656.6 38.5 %collective-permute-start = (bf16[1,1024,768]{2,1,0:T(8,128)(2,1)}, bf16[1,1024,768]{2,1,0:T(8,128)(2,1)}, u32[]{:S(2)}, u32[]{:S(2)}) collective-permute-start(bf16[1,1024,768]{2,1,0:T(8,128)(2,1)} %get-tuple-element.4146), channel_id=1, source_target_pairs={{0,8},{8,16},{16,24},{1,9},{9,17},{17,25},{2,10},{10,18},{18,26},{... | collective-permute-start | bytes 4718600 | tf_op jit(solution)/shard_map/while/body/eval_jaxpr/ppermute | solution.py:23
  2708.2 365.0 %reduce-scatter.11.cloned.1.call-start = ((), (), s32[]{:S(2)}) async-start(), calls=%async_computation.6 | async-start | bytes 13271040 | tf_op jit(solution)/shard_map/reduce_scatter | solution.py:127
  2708.9 428.3 %reduce-scatter.15.cloned.1.call-start = ((), (), s32[]{:S(2)}) async-start(), calls=%async_computation.9 | async-start | bytes 442368
  2710.0 365.5 %copy-start.74 = (u32[32]{0:T(128)S(1)}, u32[32]{0:T(128)}, u32[]{:S(2)}) copy-start(u32[32]{0:T(128)} %constant.376) | copy-start | bytes 388
  2710.0 366.8 %copy-start.70 = (f32[768]{0:T(1024)S(1)}, f32[768]{0:T(1024)}, u32[]{:S(2)}) copy-start(f32[768]{0:T(1024)} %get-tuple-element.4660) | copy-start | bytes 9220
  2710.0 366.8 %copy-start.73 = (f32[768]{0:T(1024)S(1)}, f32[768]{0:T(1024)}, u32[]{:S(2)}) copy-start(f32[768]{0:T(1024)} %get-tuple-element.4661) | copy-start | bytes 9220
  2710.0 406.2 %copy-start.63 = (f32[3,2,1,768]{3,2,1,0:T(1,128)S(1)}, f32[3,2,1,768]{3,2,1,0:T(1,128)}, u32[]{:S(2)}) copy-start(f32[3,2,1,768]{3,2,1,0:T(1,128)} %get-tuple-element.4657) | copy-start | bytes 55300
  2710.0 491.1 %reduce-scatter.13.cloned.1.call-start = ((), (), s32[]{:S(2)}) async-start(), calls=%async_computation.8 | async-start | bytes 442368
  2711.0 572.9 %all-gather.5.cloned.1.call-start = ((), (), s32[]{:S(2)}) async-start(), calls=%async_computation.5 | async-start | bytes 5308416 | tf_op jit(solution)/shard_map/all_gather | solution.py:414
  2875.7 503.5 %all-gather.7.cloned.1.call-start = ((), (), s32[]{:S(2)}) async-start(), calls=%async_computation.7 | async-start | bytes 6635520 | tf_op jit(solution)/shard_map/all_gather | solution.py:417
  (437 other events, 3482.4 us)
Sparse Core Ops, SparseCore 0:
  2708.3 165.1 reduce-scatter.8
  2877.7 195.4 reduce-scatter.10
  3076.8 60.4 reduce-scatter.14
  3140.8 60.3 reduce-scatter.12
  3203.8 80.0 all-gather.4
  3286.7 92.4 all-gather.6
where the time goes:
time: 3410 us; the launch traced here: 3390 us
  other arithmetic  964 us (28%)
  local copies, waits for them, and re-layouts  758 us (22%)
  starting transfers between devices  752 us (22%)
  waiting for transfers between devices  575 us (17%)
  matrix products  152 us (4%)
  loops' own time  102 us (3%)
  blocking collectives  74.1 us (2%)
    ppermute x20, starting transfers between devices, passed_along(): lax.ppermute(value, axis, [(source, source + steps) for source in range(l...  752 us
    add x50, other arithmetic, tick(): grad_total = jax.tree.map(jnp.add, grad_total, grad_parts)  285 us
    dynamic_update_slice x176, local copies, waits for them, and re-layouts, weighted_value_blocks(): lax.scan(advance, (accruing_upper_sum, accruing_normalizer), (key_blocks,...  199 us
    reduce_scatter x1, waiting for transfers between devices, sum_grads(): lax.psum_scatter(grad_parts[1], 'dp', scatter_dimension=0, tiled=True)  197 us
    reduce_scatter x1, waiting for transfers between devices, sum_grads(): lax.psum_scatter(grad_parts[0], 'dp', scatter_dimension=1, tiled=True)  162 us
    dynamic_update_slice x40, other arithmetic, put_slot(): lax.dynamic_update_index_in_dim(store, jnp.where(valid, value, previous),...  147 us
    another operation x71, local copies, waits for them, and re-layouts  127 us
    dynamic_slice x50, local copies, waits for them, and re-layouts, put_slot(): previous = lax.dynamic_index_in_dim(store, slot, axis_pos, keepdims=False)  99 us
  transfers between devices with their start and end apart: 26, of which 6 were waited for; matrix products, arithmetic and copies ran while one was open for 10% of the time, Pallas kernels for 0%

commit v1 on v0

v1 whole, which is shorter than its diff:
```python
import functools

import jax
import jax.numpy as jnp
from jax import lax
from jax.experimental import pallas as pl
from jax.experimental.pallas import tpu as pltpu
from jax.sharding import PartitionSpec as P

MESH = pl.DeviceIdType.MESH
F32 = jnp.float32
BF16 = jnp.bfloat16
CHUNK = 256
ROWS = 32
UNROLL = 4
VMEM_BYTES = 63 << 20

T_MIX0, T_MIX2, T_MIX1, T_GATED, C_MIX0, C_MIX1 = 0, 1, 2, 3, 4, 5
EARLY = 6
T_DK, T_DV, T_DQ, T_G, C_DKV, C_DQ, C_HID, C_DPRE = 0, 1, 2, 3, 4, 5, 6, 10
LATE = 14
KEPT = EARLY + LATE
GAIN, BIAS, RATES, DECAY, BONUS = 0, 1, 2, 5, 6


def nn(left, right):
    return jnp.dot(left, right, preferred_element_type=F32)


def nt(left, right):
    return lax.dot_general(left, right, (((1,), (1,)), ((), ())), preferred_element_type=F32)


def tn(left, right):
    return lax.dot_general(left, right, (((0,), (0,)), ((), ())), preferred_element_type=F32)


def folded(rows):
    total = rows[0:8]
    for start in range(8, rows.shape[0], 8):
        total = total + rows[start : start + 8]
    return total


def chain_kernel(
    sections,
    length,
    channels,
    hidden_blocks,
    x_hbm,
    cot_hbm,
    w_in_hbm,
    w_out_hbm,
    gain_hbm,
    bias_hbm,
    rates_hbm,
    wkv_hbm,
    state_hbm,
    outs_hbm,
    grads_hbm,
    fin_hbm,
    sums_hbm,
    kept_hbm,
    weights,
    early,
    kept,
    entry,
    hs,
    states,
    upstream,
    wide,
    pairs,
    tables,
    triangles,
    gains,
    biases,
    rates,
    wkvs,
    starts,
    previous,
    carry,
    carry_next,
    fin,
    sums,
    totals,
    weight_sem,
    weight_send,
    small_sem,
    small_send,
    entry_sem,
    entry_send,
    up_sem,
    up_send,
    out_sem,
    out_send,
    out_recv,
    early_sem,
    kept_sem,
):
    section = lax.axis_index("section")
    core = section % 2
    stage = section // 2
    stages = sections // 2
    partner = {"section": section + 1 - 2 * core}
    chunks = length // CHUNK
    blocks = CHUNK // ROWS
    time_blocks = 4
    last_stage = stage == stages - 1

    barrier = pltpu.get_barrier_semaphore()
    pl.semaphore_signal(barrier, inc=1, device_id=partner, device_id_type=MESH)

    @pl.when(stage > 0)
    def _():
        pl.semaphore_signal(
            barrier, inc=1, device_id={"section": section - 2}, device_id_type=MESH
        )

    @pl.when(stage < stages - 1)
    def _():
        pl.semaphore_signal(
            barrier, inc=1, device_id={"section": section + 2}, device_id_type=MESH
        )

    def entry_copy(chunk):
        rows = pl.ds(chunk * CHUNK, CHUNK)
        return pltpu.make_async_copy(
            x_hbm.at[core, 0, rows], entry.at[rows], entry_sem.at[chunk]
        )

    def up_copy(chunk):
        rows = pl.ds(chunk * CHUNK, CHUNK)
        return pltpu.make_async_copy(
            cot_hbm.at[core, 0, rows], upstream.at[rows], up_sem.at[chunk]
        )

    @pl.when(stage == 0)
    def _():
        for chunk in range(chunks):
            entry_copy(chunk).start()

    @pl.when(last_stage)
    def _():
        for chunk in range(chunks):
            up_copy(chunk).start()

    small_pairs = (
        (gain_hbm, gains.at[core]),
        (bias_hbm, biases.at[core]),
        (rates_hbm, rates.at[core]),
        (wkv_hbm.at[0], wkvs.at[core]),
        (state_hbm.at[0], starts.at[core]),
    )
    small_copies = [
        pltpu.make_async_copy(source, target, small_sem.at[0, at])
        for at, (source, target) in enumerate(small_pairs)
    ]
    for copy in small_copies:
        copy.start()

    def in_block(index):
        return w_in_hbm.at[0, :, pl.ds(index * channels, channels)]

    def out_block(index):
        return w_out_hbm.at[0, pl.ds(index * channels, channels), :]

    for index in range(4):
        slot = core * time_blocks + index
        pltpu.make_async_copy(in_block(index), weights.at[slot], weight_sem.at[slot]).start()

    @pl.when(core == 1)
    def _():
        for index in range(hidden_blocks + 1):
            slot = 8 + index
            pltpu.make_async_copy(
                out_block(index), weights.at[slot], weight_sem.at[slot]
            ).start()

    has_previous = jnp.where(stage > 0, 1, 0)
    has_next = jnp.where(stage < stages - 1, 1, 0)
    pl.semaphore_wait(barrier, 1 + has_previous + has_next)

    small_remotes = [
        pltpu.make_async_remote_copy(
            src_ref=source,
            dst_ref=target,
            send_sem=small_send.at[at],
            recv_sem=small_sem.at[1, at],
            device_id=partner,
            device_id_type=MESH,
        )
        for at, (source, target) in enumerate(small_pairs)
    ]

    def in_remote(index):
        slot = core * time_blocks + index
        return pltpu.make_async_remote_copy(
            src_ref=in_block(index),
            dst_ref=weights.at[slot],
            send_sem=weight_send.at[slot],
            recv_sem=weight_sem.at[slot],
            device_id=partner,
            device_id_type=MESH,
        )

    def out_remote(index):
        slot = 8 + index
        return pltpu.make_async_remote_copy(
            src_ref=out_block(index),
            dst_ref=weights.at[slot],
            send_sem=weight_send.at[slot],
            recv_sem=weight_sem.at[slot],
            device_id=partner,
            device_id_type=MESH,
        )

    for copy in small_remotes:
        copy.start()
    for index in range(4):
        in_remote(index).start()

    @pl.when(core == 1)
    def _():
        for index in (hidden_blocks, *range(hidden_blocks)):
            out_remote(index).start()

    row_at = lax.broadcasted_iota(jnp.int32, (CHUNK, 2 * CHUNK), 0)
    column_at = lax.broadcasted_iota(jnp.int32, (CHUNK, 2 * CHUNK), 1)
    column_at = jnp.where(column_at >= CHUNK, column_at - CHUNK, column_at)
    triangles[0] = jnp.where(row_at > column_at, 1.0, 0.0).astype(BF16)
    triangles[1] = jnp.where(row_at < column_at, 1.0, 0.0).astype(BF16)
    sums[...] = jnp.zeros_like(sums)
    fin[...] = jnp.zeros_like(fin)

    for copy in small_copies:
        copy.wait()
    for copy in small_remotes:
        copy.wait_recv()

    rate = jnp.exp(wkvs[0, 0:1, :])
    step = jnp.exp(-rate)
    lift = jnp.exp(wkvs[0, 1:2, :])

    def table_rows(index, _):
        start = pl.multiple_of(index * ROWS, ROWS)
        place = (lax.broadcasted_iota(jnp.int32, (ROWS, channels), 0) + start).astype(F32)
        tables[0, pl.ds(start, ROWS), :] = jnp.exp(-(CHUNK - 1.0 - place) * rate)
        tables[1, pl.ds(start, ROWS), :] = jnp.exp(-place * rate)
        return 0

    lax.fori_loop(0, blocks, table_rows, 0)

    for row in range(3):
        carry[row : row + 1] = starts[0, row, core]
    carry[3:4] = starts[1, 0, core]

    def weight_wait(slot):
        pltpu.make_async_copy(weights.at[slot], weights.at[slot], weight_sem.at[slot]).wait()

    def stats(tokens):
        center = tokens - jnp.mean(tokens, axis=-1, keepdims=True)
        spread = jnp.mean(center * center, axis=-1, keepdims=True)
        root = lax.rsqrt(spread + 1e-05)
        return center * root, root

    row_index = lax.broadcasted_iota(jnp.int32, (ROWS, channels), 0)

    def token_mix(kind, source, base, side, slots, carry_row):
        gain, bias = gains[kind], biases[kind]

        def body(index, before):
            start = pl.multiple_of(base + index * ROWS, ROWS)
            rows = pl.ds(start, ROWS)
            unit, _ = stats(source[rows, :].astype(F32))
            normed = unit * gain + bias
            previous[kind, pl.ds(start // ROWS, 1), :] = before
            shifted = jnp.where(
                row_index == 0, jnp.broadcast_to(before, normed.shape), pltpu.roll(normed, 1, 0)
            )
            gap = normed - shifted
            for rate_row, slot in slots:
                early[side, slot, pl.ds(pl.multiple_of(index * ROWS, ROWS), ROWS), :] = (
                    shifted + gap * rates[kind, rate_row]
                ).astype(BF16)
            return normed[ROWS - 1 : ROWS, :]

        carry[carry_row : carry_row + 1] = lax.fori_loop(
            0, blocks, body, carry[carry_row : carry_row + 1], unroll=UNROLL
        )

    def early_copy(chunk):
        rows = pl.ds(pl.multiple_of(chunk * CHUNK, CHUNK), CHUNK)
        side = chunk % 2
        return pltpu.make_async_copy(
            early.at[side], kept_hbm.at[pl.ds(0, EARLY), rows], early_sem.at[side]
        )

    def forward_chunk(chunk, _):
        base = pl.multiple_of(chunk * CHUNK, CHUNK)
        rows = pl.ds(base, CHUNK)
        side = chunk % 2

        @pl.when(chunk >= 2)
        def _():
            early_copy(chunk - 2).wait()

        pltpu.make_async_copy(entry.at[rows], entry.at[rows], entry_sem.at[chunk]).wait()

        token_mix(0, entry, base, side, ((0, T_MIX0), (2, T_MIX2), (1, T_MIX1)), 0)

        for slot in range(3):

            @pl.when(chunk == 0)
            def _():
                weight_wait(slot)

            wide[slot] = nn(early[side, slot], weights[slot])

        def weighted(index, _):
            start = pl.multiple_of(index * ROWS, ROWS)
            local = pl.ds(start, ROWS)
            whole = pl.ds(pl.multiple_of(base + start, ROWS), ROWS)
            value = wide[1, local, :]
            power = jnp.exp(wide[0, local, :])
            wide[0, local, :] = power
            scaled = power * tables[0, local, :]
            pairs[local, pl.ds(0, channels)] = (scaled * value).astype(BF16)
            pairs[local, pl.ds(channels, channels)] = scaled.astype(BF16)
            kept[T_DK, whole, :] = power.astype(BF16)
            kept[T_DV, whole, :] = value.astype(BF16)
            return 0

        lax.fori_loop(0, blocks, weighted, 0)
        wide[3] = nn(triangles[0, :, pl.ds(0, CHUNK)], pairs[pl.ds(0, CHUNK), pl.ds(0, channels)])
        wide[4] = nn(
            triangles[0, :, pl.ds(0, CHUNK)], pairs[pl.ds(0, CHUNK), pl.ds(channels, channels)]
        )
        upper, lower = carry[1:2], carry[2:3]

        def averaged(index, _):
            start = pl.multiple_of(index * ROWS, ROWS)
            local = pl.ds(start, ROWS)
            whole = pl.ds(pl.multiple_of(base + start, ROWS), ROWS)
            place = (row_index + start).astype(F32)
            grown = jnp.exp((CHUNK - place) * rate)
            faded = tables[1, local, :]
            power, value = wide[0, local, :], wide[1, local, :]
            before_upper = grown * wide[3, local, :] + faded * upper
            before_lower = grown * wide[4, local, :] + faded * lower
            now = power * lift
            average = (before_upper + now * value) / (before_lower + now)
            gate = jax.nn.sigmoid(wide[2, local, :])
            states[0, whole, :] = before_upper
            states[1, whole, :] = before_lower
            kept[T_DQ, whole, :] = gate.astype(BF16)
            early[side, T_GATED, local, :] = (gate * average).astype(BF16)
            tail = slice(ROWS - 8, ROWS)
            after_upper = step * before_upper[tail] + power[tail] * value[tail]
            after_lower = step * before_lower[tail] + power[tail]
            carry_next[0:1] = after_upper[7:8]
            carry_next[1:2] = after_lower[7:8]
            return 0

        lax.fori_loop(0, blocks, averaged, 0)
        carry[1:3] = carry_next[0:2]

        @pl.when(chunk == 0)
        def _():
            weight_wait(3)

        hs[0, rows, :] = (
            entry[rows, :].astype(F32) + nn(early[side, T_GATED], weights[3])
        ).astype(BF16)

        token_mix(1, hs.at[0], base, side, ((0, C_MIX0), (1, C_MIX1)), 3)

        for index in range(hidden_blocks):

            @pl.when(chunk == 0)
            def _():
                weight_wait(4 + index)

            pre = nn(early[side, C_MIX0], weights[4 + index])
            kept[C_HID + index, rows, :] = jnp.square(jnp.maximum(pre, 0.0)).astype(BF16)

        @pl.when(chunk == 0)
        def _():
            weight_wait(8 + hidden_blocks)

        early_copy(chunk).start()
        wide[1] = nn(early[side, C_MIX1], weights[8 + hidden_blocks])

        @pl.when(chunk == 0)
        def _():
            for index in range(hidden_blocks):
                weight_wait(8 + index)

        total = nn(kept[C_HID, rows, :], weights[8])
        for index in range(1, hidden_blocks):
            total = total + nn(kept[C_HID + index, rows, :], weights[8 + index])
        wide[0] = total

        def joined(index, _):
            start = pl.multiple_of(index * ROWS, ROWS)
            local = pl.ds(start, ROWS)
            whole = pl.ds(pl.multiple_of(base + start, ROWS), ROWS)
            gate = jax.nn.sigmoid(wide[1, local, :])
            value = wide[0, local, :]
            kept[C_DKV, whole, :] = gate.astype(BF16)
            kept[C_DQ, whole, :] = value.astype(BF16)
            hs[1, whole, :] = (hs[0, whole, :].astype(F32) + gate * value).astype(BF16)
            return 0

        lax.fori_loop(0, blocks, joined, 0)

        @pl.when(stage < stages - 1)
        def _():
            entry_remote(chunk).start()

        return 0

    def entry_remote(chunk):
        rows = pl.ds(pl.multiple_of(chunk * CHUNK, CHUNK), CHUNK)
        return pltpu.make_async_remote_copy(
            src_ref=hs.at[1, rows],
            dst_ref=entry.at[rows],
            send_sem=entry_send.at[chunk],
            recv_sem=entry_sem.at[chunk],
            device_id={"section": section + 2},
            device_id_type=MESH,
        )

    def up_remote(chunk):
        rows = pl.ds(pl.multiple_of(chunk * CHUNK, CHUNK), CHUNK)
        return pltpu.make_async_remote_copy(
            src_ref=upstream.at[rows],
            dst_ref=upstream.at[rows],
            send_sem=up_send.at[chunk],
            recv_sem=up_sem.at[chunk],
            device_id={"section": section - 2},
            device_id_type=MESH,
        )

    lax.fori_loop(0, chunks, forward_chunk, 0)
    early_copy(chunks - 2).wait()
    early_copy(chunks - 1).wait()
    fin[0, 0:1] = carry[0:1]
    fin[0, 1:3] = carry[1:3]
    fin[1, 0:1] = carry[3:4]

    def to_owner(index, own_src, other_src, dst):
        own = pltpu.make_async_copy(own_src, dst, out_sem.at[index])
        other = pltpu.make_async_remote_copy(
            src_ref=other_src,
            dst_ref=dst,
            send_sem=out_send.at[index],
            recv_sem=out_recv.at[index],
            device_id=partner,
            device_id_type=MESH,
        )
        return own, other

    outs_copies = to_owner(0, hs.at[core], hs.at[1 - core], outs_hbm.at[core])
    fin_copies = to_owner(1, fin.at[core], fin.at[1 - core], fin_hbm.at[core])
    for copy in outs_copies + fin_copies:
        copy.start()

    carry[0:4] = jnp.zeros((4, channels), F32)

    def norm_back(kind, source, base, mixes, above, target, carry_row):
        gain, bias = gains[kind], biases[kind]

        def body(index, after):
            back = blocks - 1 - index
            local = pl.ds(pl.multiple_of(back * ROWS, ROWS), ROWS)
            start = pl.multiple_of(base + back * ROWS, ROWS)
            rows = pl.ds(start, ROWS)
            unit, root = stats(source[rows, :].astype(F32))
            normed = unit * gain + bias
            before = previous[kind, pl.ds(start // ROWS, 1), :]
            shifted = jnp.where(
                row_index == 0, jnp.broadcast_to(before, normed.shape), pltpu.roll(normed, 1, 0)
            )
            gap = normed - shifted
            straight = jnp.zeros_like(normed)
            total = jnp.zeros_like(normed)
            for rate_row, slot in mixes:
                mix = wide[slot, local, :]
                straight = straight + mix * rates[kind, rate_row]
                total = total + mix
                sums[kind, RATES + rate_row] += folded(mix * gap)
            late = total - straight
            moved = jnp.where(
                row_index == ROWS - 1,
                jnp.broadcast_to(after, late.shape),
                pltpu.roll(late, ROWS - 1, 0),
            )
            d_normed = straight + moved
            sums[kind, GAIN] += folded(d_normed * unit)
            sums[kind, BIAS] += folded(d_normed)
            d_unit = d_normed * gain
            d_tokens = (
                d_unit
                - jnp.mean(d_unit, axis=-1, keepdims=True)
                - unit * jnp.mean(d_unit * unit, axis=-1, keepdims=True)
            ) * root
            target[rows, :] = (above[rows, :].astype(F32) + d_tokens).astype(BF16)
            return late[0:1, :]

        carry[carry_row : carry_row + 1] = lax.fori_loop(
            0, blocks, body, carry[carry_row : carry_row + 1], unroll=UNROLL
        )

    def late_copy(chunk, part):
        rows = pl.ds(pl.multiple_of(chunk * CHUNK, CHUNK), CHUNK)
        begin, count = ((C_DKV, LATE - C_DKV), (T_DK, C_DKV))[part]
        return pltpu.make_async_copy(
            kept.at[pl.ds(begin, count), rows],
            kept_hbm.at[pl.ds(EARLY + begin, count), rows],
            kept_sem.at[part, chunk],
        )

    def grad_copies(chunk, kind):
        rows = pl.ds(pl.multiple_of(chunk * CHUNK, CHUNK), CHUNK)
        sources = (upstream.at[rows], kept.at[T_G, rows])
        return to_owner(
            2 + chunk, sources[kind], sources[1 - kind], grads_hbm.at[core, rows]
        )

    def backward_chunk(turn, _):
        chunk = chunks - 1 - turn
        base = pl.multiple_of(chunk * CHUNK, CHUNK)
        rows = pl.ds(base, CHUNK)
        pltpu.make_async_copy(upstream.at[rows], upstream.at[rows], up_sem.at[chunk]).wait()

        def split(index, _):
            whole = pl.ds(pl.multiple_of(base + index * ROWS, ROWS), ROWS)
            above = upstream[whole, :].astype(F32)
            gate = kept[C_DKV, whole, :].astype(F32)
            value = kept[C_DQ, whole, :].astype(F32)
            d_value = above * gate
            kept[C_DKV, whole, :] = d_value.astype(BF16)
            kept[C_DQ, whole, :] = (d_value * value * (1.0 - gate)).astype(BF16)
            return 0

        lax.fori_loop(0, blocks, split, 0)

        for index in range(hidden_blocks):
            d_hidden = nt(kept[C_DKV, rows, :], weights[8 + index])
            slope = jnp.sqrt(kept[C_HID + index, rows, :].astype(F32))
            kept[C_DPRE + index, rows, :] = (d_hidden * (2.0 * slope)).astype(BF16)
        total = nt(kept[C_DPRE, rows, :], weights[4])
        for index in range(1, hidden_blocks):
            total = total + nt(kept[C_DPRE + index, rows, :], weights[4 + index])
        wide[0] = total
        wide[1] = nt(kept[C_DQ, rows, :], weights[8 + hidden_blocks])
        late_copy(chunk, 0).start()
        norm_back(1, hs.at[0], base, ((0, 0), (1, 1)), upstream, kept.at[T_G], 3)

        wide[0] = nt(kept[T_G, rows, :], weights[3])

        def inputs(index, _):
            start = pl.multiple_of(index * ROWS, ROWS)
            local = pl.ds(start, ROWS)
            whole = pl.ds(pl.multiple_of(base + start, ROWS), ROWS)
            power = kept[T_DK, whole, :].astype(F32)
            value = kept[T_DV, whole, :].astype(F32)
            gate = kept[T_DQ, whole, :].astype(F32)
            now = power * lift
            inverse = 1.0 / (states[1, whole, :] + now)
            average = (states[0, whole, :] + now * value) * inverse
            d_average = wide[0, local, :] * gate
            kept[T_DQ, whole, :] = (d_average * average * (1.0 - gate)).astype(BF16)
            unit = d_average * inverse
            wide[1, local, :] = unit
            wide[2, local, :] = average
            scaled = unit * tables[1, local, :]
            for column, term in ((0, scaled), (channels, -scaled * average)):
                high = term.astype(BF16)
                pairs[local, pl.ds(column, channels)] = high
                pairs[pl.ds(pl.multiple_of(CHUNK + start, ROWS), ROWS), pl.ds(column, channels)] = (
                    term - high.astype(F32)
                ).astype(BF16)
            return 0

        lax.fori_loop(0, blocks, inputs, 0)
        wide[3] = nn(triangles[1], pairs[:, pl.ds(0, channels)])
        wide[4] = nn(triangles[1], pairs[:, pl.ds(channels, channels)])
        alpha_after, beta_after = carry[1:2], carry[2:3]

        def outputs(index, _):
            start = pl.multiple_of((blocks - 1 - index) * ROWS, ROWS)
            local = pl.ds(start, ROWS)
            whole = pl.ds(pl.multiple_of(base + start, ROWS), ROWS)
            place = (row_index + start).astype(F32)
            grown = jnp.exp((place + 1.0) * rate)
            faded = tables[0, local, :]
            alpha = grown * wide[3, local, :] + faded * alpha_after
            beta = grown * wide[4, local, :] + faded * beta_after
            unit, average = wide[1, local, :], wide[2, local, :]
            power = kept[T_DK, whole, :].astype(F32)
            value = kept[T_DV, whole, :].astype(F32)
            weighed = unit * (power * lift)
            own = weighed * (value - average)
            kept[T_DK, whole, :] = (own + power * (alpha * value + beta)).astype(BF16)
            kept[T_DV, whole, :] = (weighed + power * alpha).astype(BF16)
            sums[0, BONUS] += folded(own)
            sums[0, DECAY] += folded(
                alpha * states[0, whole, :] + beta * states[1, whole, :]
            )
            carry_next[0:1] = unit[0:1] + step * alpha[0:1]
            carry_next[1:2] = step * beta[0:1] - unit[0:1] * average[0:1]
            return 0

        lax.fori_loop(0, blocks, outputs, 0)
        carry[1:3] = carry_next[0:2]
        wide[0] = nt(kept[T_DK, rows, :], weights[0])
        wide[1] = nt(kept[T_DQ, rows, :], weights[2])
        wide[2] = nt(kept[T_DV, rows, :], weights[1])
        norm_back(
            0, entry, base, ((0, 0), (1, 1), (2, 2)), kept.at[T_G], upstream, 0
        )

        @pl.when(stage > 0)
        def _():
            up_remote(chunk).start()

        late_copy(chunk, 1).start()
        for kind in range(2):

            @pl.when(core == kind)
            def _():
                for copy in grad_copies(chunk, kind):
                    copy.start()

        return 0

    lax.fori_loop(0, chunks, backward_chunk, 0)

    sums[0, DECAY] = sums[0, DECAY] * (-rate * step)
    for kind in range(2):
        for row in range(7):
            totals[kind, row : row + 1] = jnp.sum(sums[kind, row], axis=0, keepdims=True)
        totals[kind, 7:8] = jnp.zeros((1, channels), F32)
    sums_copy = pltpu.make_async_copy(totals, sums_hbm, kept_sem.at[0, chunks])
    sums_copy.start()
    for copy in (sums_copy,) + outs_copies + fin_copies:
        copy.wait()
    for chunk in range(chunks):
        for part in range(2):
            late_copy(chunk, part).wait()
        for copy in grad_copies(chunk, 0):
            copy.wait()
    for copy in small_remotes:
        copy.wait_send()
    for index in range(4):
        in_remote(index).wait_send()

    @pl.when(core == 1)
    def _():
        for index in range(hidden_blocks + 1):
            out_remote(index).wait_send()

    @pl.when(stage < stages - 1)
    def _():
        for chunk in range(chunks):
            entry_remote(chunk).wait_send()

    @pl.when(stage > 0)
    def _():
        for chunk in range(chunks):
            up_remote(chunk).wait_send()


def chain(sections, x, cotangent, w_in, w_out, gain, bias, rates, wkv, state):
    length, channels = x.shape[2:]
    hidden_blocks = w_in.shape[2] // channels
    chunks = length // CHUNK
    anywhere = pl.BlockSpec(memory_space=pl.ANY)
    dma = pltpu.SemaphoreType.DMA
    slots = 9 + hidden_blocks
    return pl.pallas_call(
        functools.partial(chain_kernel, sections, length, channels, hidden_blocks),
        out_shape=(
            jax.ShapeDtypeStruct((2, length, channels), BF16),
            jax.ShapeDtypeStruct((2, length, channels), BF16),
            jax.ShapeDtypeStruct((2, 8, channels), F32),
            jax.ShapeDtypeStruct((2, 8, channels), F32),
            jax.ShapeDtypeStruct((KEPT, length, channels), BF16),
        ),
        in_specs=[anywhere] * 9,
        out_specs=(anywhere,) * 5,
        scratch_shapes=[
            pltpu.VMEM((slots, channels, channels), BF16),
            pltpu.VMEM((2, EARLY, CHUNK, channels), BF16),
            pltpu.VMEM((LATE, length, channels), BF16),
            pltpu.VMEM((length, channels), BF16),
            pltpu.VMEM((2, length, channels), BF16),
            pltpu.VMEM((2, length, channels), F32),
            pltpu.VMEM((length, channels), BF16),
            pltpu.VMEM((5, CHUNK, channels), F32),
            pltpu.VMEM((2 * CHUNK, 2 * channels), BF16),
            pltpu.VMEM((2, CHUNK, channels), F32),
            pltpu.VMEM((2, CHUNK, 2 * CHUNK), BF16),
            pltpu.VMEM((2, 1, channels), F32),
            pltpu.VMEM((2, 1, channels), F32),
            pltpu.VMEM((2, 3, 1, channels), F32),
            pltpu.VMEM((2, 2, channels), F32),
            pltpu.VMEM((2, 3, 2, 1, channels), F32),
            pltpu.VMEM((2, length // ROWS, channels), F32),
            pltpu.VMEM((8, channels), F32),
            pltpu.VMEM((8, channels), F32),
            pltpu.VMEM((2, 8, channels), F32),
            pltpu.VMEM((2, 8, 8, channels), F32),
            pltpu.VMEM((2, 8, channels), F32),
            dma((slots,)),
            dma((slots,)),
            dma((2, 5)),
            dma((5,)),
            dma((chunks,)),
            dma((chunks,)),
            dma((chunks,)),
            dma((chunks,)),
            dma((2 + chunks,)),
            dma((2 + chunks,)),
            dma((2 + chunks,)),
            dma((2,)),
            dma((2, chunks + 1)),
        ],
        compiler_params=pltpu.CompilerParams(
            collective_id=0, has_side_effects=True, vmem_limit_bytes=VMEM_BYTES
        ),
    )(x, cotangent, w_in, w_out, gain, bias, rates, wkv, state)


C_BLOCKS = 9
T_BLOCKS = 4
BLOCKS = C_BLOCKS + T_BLOCKS
PLACES = (8, 9, 0, 1, 2, 3, 10, 4, 5, 6, 11, 12, 7)
PAIRED = 8


def lookup(index, table):
    value = jnp.int32(table[0])
    for at, entry in enumerate(table[1:], 1):
        value = jnp.where(index == at, entry, value)
    return value


def reduce_plan(line, half):
    pieces = (max(16, half // (2 * line)), max(16, half // line))
    sizes = (2 * line * pieces[0], line * pieces[1])
    counts = (-(-PAIRED * half // sizes[0]), -(-(BLOCKS - PAIRED) * half // sizes[1]))
    return pieces, sizes, counts


def ready_times(first, size, count, half):
    made = {place: time for time, place in enumerate(PLACES)}
    times = []
    for group in range(count):
        begin, end = first + group * size, first + (group + 1) * size
        times.append(
            max(made[place] for place in range(BLOCKS) if place * half < end and begin < (place + 1) * half)
        )
    return tuple(times)


COMPUTE = 2
FETCHED_AHEAD = 3
ORDER_OF_FOUR = (
    2000, 1000, 2010, 2020, 1001, 1010, 2030, 2040, 1002, 2050, 30, 1011, 2060, 1020, 2070, 1003,
    2080, 1012, 31, 1021, 2090, 0, 2100, 1004, 1013, 2110, 1022, 2120, 32, 1, 1005, 50,
    1014, 1023, 1006, 2, 33, 1040, 1015, 1007, 51, 3, 60, 1016, 1041, 52, 34, 1017,
    61, 70, 1042, 53, 35, 62, 20, 1024, 71, 1043, 4, 36, 1030, 63, 1025, 21,
    40, 5, 72, 37, 1044, 1026, 1031, 6, 22, 64, 41, 73, 1027, 1045, 7, 1032,
    10, 23, 65, 42, 1046, 1033, 11, 24, 66, 43, 1047, 12, 25, 67, 44, 13,
    26, 45, 14, 27, 46, 15, 47, 16, 54, 74, 17, 55, 75, 1034, 56, 76,
    1035, 77, 57, 1036, 1037,
)


def event_order(line, half):
    _, sizes, counts = reduce_plan(line, half)
    if line == 4 and counts == (8, 5):
        return [(code // 1000, code // 10 % 100, code % 10) for code in ORDER_OF_FOUR]
    firsts = (0, counts[0] * sizes[0])
    steps = [(block, 0, (COMPUTE, block, 0)) for block in range(BLOCKS)]
    for kind in range(2):
        times = ready_times(firsts[kind], sizes[kind], counts[kind], half)
        for group, time in enumerate(times):
            steps += [(time + turn, 1 + kind, (kind, group, turn)) for turn in range(2 * line)]
    return [step for _, _, step in sorted(steps)]


def reduce_kernel(
    count,
    length,
    channels,
    kept_hbm,
    sums_hbm,
    in_hbm,
    out_hbm,
    total_hbm,
    kept,
    mine,
    theirs,
    pair_landing,
    cross_landing,
    right0,
    left0,
    right1,
    left1,
    small,
    kept_sem,
    pair_sem,
    pair_send,
    y_sem,
    y_send,
    sum_sem0,
    sum_send0,
    sum_sem1,
    sum_send1,
    spread_sem0,
    spread_send0,
    spread_sem1,
    spread_send1,
    give_sem,
    give_send,
    give_recv,
    small_sem,
    small_send,
):
    section = lax.axis_index("section")
    dp_index = lax.axis_index("dp")
    core = section % 2
    line = count // 2
    z, y = dp_index // 2, dp_index % 2
    half = channels // 2
    pieces, sizes, counts = reduce_plan(line, half)
    firsts = (0, counts[0] * sizes[0])
    partner = {"section": section + 1 - 2 * core}
    across = {"dp": dp_index + 1 - 2 * y}

    def peer(offset):
        return {"dp": lax.rem(dp_index + offset, count)}

    late = EARLY

    def operands(block):
        turn = block - C_BLOCKS
        left = jnp.where(block < 8, late + C_HID + block - 4, jnp.where(block == 8, C_MIX1, T_MIX0 + turn))
        left = jnp.where(block < 4, C_MIX0, left)
        right = jnp.where(block == 8, late + C_DQ, late + T_DK + turn)
        right = jnp.where(block < 8, late + C_DKV, right)
        right = jnp.where(block < 4, late + C_DPRE + block, right)
        return (left, (block == 0) | (block >= 4)), (right, (block <= 4) | (block >= 8))

    def kept_copy(slot):
        return pltpu.make_async_copy(kept_hbm.at[slot], kept.at[slot], kept_sem.at[slot])

    def fetch(block):
        for slot, first in operands(block):
            pl.when(first & (block < BLOCKS))(lambda: kept_copy(slot).start())

    for block in range(FETCHED_AHEAD):
        fetch(jnp.int32(block))
    own_small = pltpu.make_async_copy(sums_hbm.at[core], small.at[0], small_sem.at[0])
    own_small.start()

    barrier = pltpu.get_barrier_semaphore()
    diagonal = {"section": section + 1 - 2 * core, "dp": dp_index + 1 - 2 * y}
    for device in (partner, diagonal):
        pl.semaphore_signal(barrier, inc=1, device_id=device, device_id_type=MESH)

    def greet(offset, _):
        pl.semaphore_signal(barrier, inc=1, device_id=peer(offset), device_id_type=MESH)
        return 0

    lax.fori_loop(1, count, greet, 0)

    small_pair = pltpu.make_async_remote_copy(
        src_ref=sums_hbm.at[1 - core],
        dst_ref=small.at[1],
        send_sem=small_send.at[0],
        recv_sem=small_sem.at[1],
        device_id=partner,
        device_id_type=MESH,
    )

    def small_copy(offset):
        return pltpu.make_async_remote_copy(
            src_ref=small.at[0],
            dst_ref=small.at[1 + offset],
            send_sem=small_send.at[offset],
            recv_sem=small_sem.at[1 + offset],
            device_id=peer(offset),
            device_id_type=MESH,
        )

    def small_start(offset, _):
        small_copy(offset).start()
        return 0

    def small_add(offset, total):
        small_copy(offset).wait()
        return total + small[1 + offset]

    def product(block, which):
        (left, _), (right, _) = operands(block)
        columns = pl.ds(pl.multiple_of(which * half, 128), half)
        return tn(kept[left, :, columns], kept[right])

    def block_rows(block):
        return pl.ds(pl.multiple_of(lookup(block, PLACES) * half, half), half)

    def sent_rows(block):
        return pl.ds(pl.multiple_of(block * half, half), half)

    def pair_copy(block):
        return pltpu.make_async_remote_copy(
            src_ref=theirs.at[sent_rows(block)],
            dst_ref=mine.at[block_rows(block)],
            send_sem=pair_send.at[block],
            recv_sem=pair_sem.at[block],
            device_id=partner,
            device_id_type=MESH,
        )

    def for_partner(block):
        for slot, first in operands(block):
            pl.when(first)(lambda: kept_copy(slot).wait())
        fetch(block + FETCHED_AHEAD)
        theirs[sent_rows(block), :] = product(block, 1 - core).astype(BF16)

        @pl.when(block == 0)
        def _():
            pl.semaphore_wait(barrier, count + 1)
            small_pair.start()

        pair_copy(block).start()

    def for_me(block):
        rows = block_rows(block)
        own = product(block, core)
        pair_copy(block).wait_recv()
        mine[rows, :] = (own + mine[rows, :].astype(F32)).astype(BF16)

    blocks_at = tuple(PLACES.index(place) for place in range(BLOCKS))

    def give(kind, group, start):
        size = pieces[kind]
        rows = pl.ds(pl.multiple_of(start, size), size)
        place = start // half if half % sizes[kind] else firsts[kind] // half + group * sizes[kind] // half
        block = lookup(place, blocks_at)
        row = core * half + start - place * half

        def copies(owner, target):
            @pl.when(owner == core)
            def _():
                pltpu.make_async_copy(mine.at[rows], target, give_sem.at[0]).start()

            def remote(device):
                return pltpu.make_async_remote_copy(
                    src_ref=mine.at[rows],
                    dst_ref=target,
                    send_sem=give_send.at[0],
                    recv_sem=give_recv.at[0],
                    device_id=device,
                    device_id_type=MESH,
                )

            @pl.when(owner != core)
            def _():
                remote(partner).start()

            if kind == 0:
                remote({"section": section - core + owner, "dp": dp_index + 1 - 2 * y}).start()

        def to_in(owner, column):
            columns = pl.ds(pl.multiple_of(column * channels, channels), channels)
            copies(owner, in_hbm.at[pl.ds(pl.multiple_of(row, size), size), columns])

        def to_out():
            within = (block - 4) * channels + row
            copies(1, out_hbm.at[pl.ds(pl.multiple_of(within, size), size)])

        of_time = block >= C_BLOCKS
        pl.when((block < 4) | (of_time & (place < BLOCKS)))(
            lambda: to_in(jnp.where(of_time, 0, 1), jnp.where(of_time, block - C_BLOCKS, block))
        )
        pl.when((block >= 4) & ~of_time)(to_out)

    right_peer, left_peer = {"dp": dp_index + 2}, {"dp": dp_index - 2}
    landings = ((right0, left0), (right1, left1))
    sum_sems = ((sum_sem0, sum_send0), (sum_sem1, sum_send1))
    spread_sems = ((spread_sem0, spread_send0), (spread_sem1, spread_send1))

    def piece_rows(kind, group, index):
        start = firsts[kind] + group * sizes[kind] + index * pieces[kind]
        if kind == 0:
            start = start + y * (sizes[0] // 2)
        return start, pl.ds(pl.multiple_of(start, pieces[kind]), pieces[kind])

    def sum_copy(kind, group, direction, step):
        place = landings[kind][direction].at[group, step]
        receive, send = sum_sems[kind]
        return pltpu.make_async_remote_copy(
            src_ref=place,
            dst_ref=place,
            send_sem=send.at[group, direction, step],
            recv_sem=receive.at[group, direction, step],
            device_id=(right_peer, left_peer)[direction],
            device_id_type=MESH,
        )

    def spread_copy(kind, group, direction, step, index):
        _, rows = piece_rows(kind, group, index)
        receive, send = spread_sems[kind]
        return pltpu.make_async_remote_copy(
            src_ref=mine.at[rows],
            dst_ref=mine.at[rows],
            send_sem=send.at[group, direction, step],
            recv_sem=receive.at[group, direction, step],
            device_id=(right_peer, left_peer)[direction],
            device_id_type=MESH,
        )

    def passing(kind, group, turn):
        for direction in range(2):
            behind = z if direction == 0 else line - 1 - z
            step = turn - behind
            index = line - 1 - step if direction == 0 else step
            place = landings[kind][direction].at[group, step]
            _, rows = piece_rows(kind, group, index)

            @pl.when((step >= 0) & (behind == 0) & (step < line - 1))
            def _():
                place[...] = mine[rows, :]
                sum_copy(kind, group, direction, step).start()

            @pl.when((step >= 0) & (behind > 0))
            def _():
                sum_copy(kind, group, direction, step).wait_recv()

                @pl.when(turn < line - 1)
                def _():
                    place[...] = (place[...].astype(F32) + mine[rows, :].astype(F32)).astype(BF16)
                    sum_copy(kind, group, direction, step).start()

    def arrived(kind, group):
        _, rows = piece_rows(kind, group, z)
        total = mine[rows, :].astype(F32)
        from_left = landings[kind][0].at[group, jnp.minimum(line - 1 - z, line - 2)]
        from_right = landings[kind][1].at[group, jnp.minimum(z, line - 2)]
        mine[rows, :] = total.astype(BF16)

        @pl.when(z == 0)
        def _():
            mine[rows, :] = (total + from_right[...].astype(F32)).astype(BF16)

        @pl.when(z == line - 1)
        def _():
            mine[rows, :] = (total + from_left[...].astype(F32)).astype(BF16)

        @pl.when((z > 0) & (z < line - 1))
        def _():
            mine[rows, :] = (
                total + from_left[...].astype(F32) + from_right[...].astype(F32)
            ).astype(BF16)

    def finished(kind, group, index):
        start, _ = piece_rows(kind, group, index)
        give(kind, group, start)

    def spread_own(kind, group):
        @pl.when(z < line - 1)
        def _():
            spread_copy(kind, group, 0, 0, z).start()

        @pl.when(z > 0)
        def _():
            spread_copy(kind, group, 1, 0, z).start()

        finished(kind, group, z)

    def spreading(kind, group, hop):
        for direction in range(2):
            index = z - hop if direction == 0 else z + hop
            onward = z < line - 1 if direction == 0 else z > 0
            exists = index >= 0 if direction == 0 else index < line

            @pl.when(exists)
            def _():
                spread_copy(kind, group, direction, hop - 1, index).wait_recv()

                @pl.when(onward)
                def _():
                    spread_copy(kind, group, direction, hop, index).start()

                finished(kind, group, index)

    def over(group):
        start = group * sizes[0] + (1 - y) * (sizes[0] // 2)
        return pltpu.make_async_remote_copy(
            src_ref=mine.at[pl.ds(pl.multiple_of(start, pieces[0]), sizes[0] // 2)],
            dst_ref=pair_landing.at[group],
            send_sem=y_send.at[group],
            recv_sem=y_sem.at[group],
            device_id=across,
            device_id_type=MESH,
        )

    def swap(group):
        _, rows = piece_rows(1, group, z)
        return pltpu.make_async_remote_copy(
            src_ref=mine.at[rows],
            dst_ref=cross_landing.at[group],
            send_sem=y_send.at[counts[0] + group],
            recv_sem=y_sem.at[counts[0] + group],
            device_id=across,
            device_id_type=MESH,
        )

    def event0(group, turn):
        @pl.when(turn == 0)
        def _():
            over(group).start()

        @pl.when(turn == 1)
        def _():
            over(group).wait_recv()

            def add(index, _):
                _, rows = piece_rows(0, group, index)
                local = pl.ds(pl.multiple_of(index * pieces[0], pieces[0]), pieces[0])
                mine[rows, :] = (
                    mine[rows, :].astype(F32) + pair_landing[group, local, :].astype(F32)
                ).astype(BF16)
                return 0

            lax.fori_loop(0, line, add, 0)

        @pl.when((turn >= 1) & (turn <= line))
        def _():
            passing(0, group, turn - 1)

        @pl.when(turn == line)
        def _():
            arrived(0, group)
            spread_own(0, group)

        @pl.when(turn > line)
        def _():
            spreading(0, group, turn - line)

    def event1(group, turn):
        @pl.when(turn < line)
        def _():
            passing(1, group, turn)

        @pl.when(turn == line - 1)
        def _():
            arrived(1, group)
            swap(group).start()

        @pl.when(turn == line)
        def _():
            swap(group).wait()
            _, rows = piece_rows(1, group, z)
            mine[rows, :] = (
                mine[rows, :].astype(F32) + cross_landing[group].astype(F32)
            ).astype(BF16)
            spread_own(1, group)

        @pl.when(turn > line)
        def _():
            spreading(1, group, turn - line)

    spare = firsts[1] + counts[1] * sizes[1] - BLOCKS * half
    if spare:
        mine[pl.ds(BLOCKS * half, spare), :] = jnp.zeros((spare, channels), BF16)
    order = [(COMPUTE, 0, 0)]
    for kind, group, turn in event_order(line, half):
        if kind == COMPUTE:
            order += [(COMPUTE, group + 1, 0)] * (group + 1 < BLOCKS) + [(COMPUTE, group, 1)]
        else:
            order.append((kind, group, turn))
    codes = [kind * 1024 + group * 64 + turn for kind, group, turn in order]
    steps = len(codes)
    words = tuple(a + 4096 * b for a, b in zip(codes[::2], (codes + [0])[1::2], strict=True))

    def take(index, _):
        word = lookup(index // 2, words)
        code = jnp.where(index % 2 == 0, word % 4096, word // 4096)
        kind, group, turn = code // 1024, code // 64 % 16, code % 64

        @pl.when(kind == COMPUTE)
        def _():
            pl.when(turn == 0)(lambda: for_partner(group))
            pl.when(turn == 1)(lambda: for_me(group))

            @pl.when((turn == 1) & (group == BLOCKS // 2))
            def _():
                own_small.wait()
                small_pair.wait()
                small[0] = small[0] + small[1]
                lax.fori_loop(1, count, small_start, 0)

        pl.when(kind == 0)(lambda: event0(group, turn))
        pl.when(kind == 1)(lambda: event1(group, turn))
        return 0

    lax.fori_loop(0, steps, take, 0)
    small[0] = lax.fori_loop(1, count, small_add, small[0])
    total_copy = pltpu.make_async_copy(small.at[0], total_hbm, small_sem.at[0])
    total_copy.start()

    def pair_done(block, _):
        pair_copy(block).wait_send()
        return 0

    def over_done(group, _):
        over(group).wait_send()
        return 0

    lax.fori_loop(0, BLOCKS, pair_done, 0)
    lax.fori_loop(0, counts[0], over_done, 0)
    for kind in range(2):

        def group_done(group, _):
            def step_done(step, _):
                for direction in range(2):
                    behind = z if direction == 0 else line - 1 - z

                    @pl.when(step < line - 1 - behind)
                    def _():
                        sum_copy(kind, group, direction, step).wait_send()

                    @pl.when((step <= behind) & (behind < line - 1))
                    def _():
                        spread_copy(kind, group, direction, step, 0).wait_send()

                return 0

            return lax.fori_loop(0, line - 1, step_done, 0)

        lax.fori_loop(0, counts[kind], group_done, 0)

    def taken(rows, sem):
        if rows:
            ref = mine.at[pl.ds(0, rows)]
            pltpu.make_async_copy(ref, ref, sem.at[0]).wait()

    paired = [PLACES[block] < PAIRED for block in range(BLOCKS)]
    whole = [half // 2 if pair else half for pair in paired]
    by_kind = (range(C_BLOCKS, BLOCKS), range(C_BLOCKS))
    for own in range(2):

        @pl.when(core == own)
        def _():
            local = sum(whole[block] for block in by_kind[own])
            crossed = sum(half // 2 for block in range(BLOCKS) if paired[block])
            other = sum(whole[block] for block in by_kind[1 - own])
            taken(local, give_sem)
            taken(other + crossed, give_send)
            taken(len(by_kind[own]) * channels - local, give_recv)

    total_copy.wait()


def reduced(count, kept, sums):
    length, channels = kept.shape[1:]
    half = channels // 2
    line = count // 2
    pieces, sizes, counts = reduce_plan(line, half)
    anywhere = pl.BlockSpec(memory_space=pl.ANY)
    dma = pltpu.SemaphoreType.DMA
    hops = [dma((counts[kind], 2, line - 1)) for kind in range(2)]
    landings = [pltpu.VMEM((counts[kind], line - 1, pieces[kind], channels), BF16) for kind in range(2)]
    return pl.pallas_call(
        functools.partial(reduce_kernel, count, length, channels),
        out_shape=(
            jax.ShapeDtypeStruct((channels, 4 * channels), BF16),
            jax.ShapeDtypeStruct(((C_BLOCKS - 4) * channels, channels), BF16),
            jax.ShapeDtypeStruct((8, channels), F32),
        ),
        in_specs=[anywhere] * 2,
        out_specs=(anywhere,) * 3,
        scratch_shapes=[
            pltpu.VMEM((KEPT, length, channels), BF16),
            pltpu.VMEM((counts[0] * sizes[0] + counts[1] * sizes[1], channels), BF16),
            pltpu.VMEM((BLOCKS * half, channels), BF16),
            pltpu.VMEM((counts[0], sizes[0] // 2, channels), BF16),
            pltpu.VMEM((counts[1], pieces[1], channels), BF16),
            landings[0],
            landings[0],
            landings[1],
            landings[1],
            pltpu.VMEM((count + 1, 8, channels), F32),
            dma((KEPT,)),
            dma((BLOCKS,)),
            dma((BLOCKS,)),
            dma((sum(counts),)),
            dma((sum(counts),)),
            hops[0],
            hops[0],
            hops[1],
            hops[1],
            hops[0],
            hops[0],
            hops[1],
            hops[1],
            dma((1,)),
            dma((1,)),
            dma((1,)),
            dma((count + 1,)),
            dma((count + 1,)),
        ],
        compiler_params=pltpu.CompilerParams(
            collective_id=1, has_side_effects=True, vmem_limit_bytes=VMEM_BYTES
        ),
    )(kept, sums)


def finish_kernel(
    steps,
    in_short,
    out_short,
    outs_in,
    grads_in,
    fin,
    total,
    in_wide,
    out_wide,
    outs,
    grads,
    states,
    normed,
    gain,
    bias,
    rates,
    wkv,
):
    holds_channel_mix = lax.axis_index("section") % 2 == 1
    step = pl.program_id(0)

    @pl.when(step == 0)
    def _():
        for micro in range(2):
            normed[0, micro] = fin[micro, 0:1]
            for row in range(2):
                states[0, row, micro] = fin[micro, 1 + row : 2 + row]
        gain[...] = total[GAIN : GAIN + 1]
        bias[...] = total[BIAS : BIAS + 1]
        for row in range(3):
            rates[row] = total[RATES + row : RATES + row + 1]
        wkv[0] = total[DECAY : DECAY + 2]

    in_wide[...] = in_short[...].astype(F32)
    out_wide[...] = jnp.where(holds_channel_mix, out_short[...].astype(F32), 0.0)
    outs[0, :, 0] = outs_in[...]
    grads[0, :, 0] = grads_in[...]


def finished_outputs(in_short, out_short, outs, grads, fin, total):
    steps = 8
    length, channels = outs.shape[1:]
    whole = pl.BlockSpec(memory_space=pltpu.VMEM)
    kept = pl.BlockSpec((2, length // steps, channels), lambda i: (0, i, 0))
    placed = pl.BlockSpec((1, 2, 1, length // steps, channels), lambda i: (0, 0, 0, i, 0))

    def spec(array):
        rows, columns = array.shape
        return pl.BlockSpec((rows // steps, columns), lambda i: (i, 0))

    def shape(*sizes, dtype=F32):
        return jax.ShapeDtypeStruct(sizes, dtype)

    in_wide, out_wide, *rest = pl.pallas_call(
        functools.partial(finish_kernel, steps),
        grid=(steps,),
        out_shape=(
            shape(*in_short.shape),
            shape(*out_short.shape),
            shape(1, 2, 1, length, channels, dtype=BF16),
            shape(1, 2, 1, length, channels, dtype=BF16),
            shape(1, 2, 2, 1, channels),
            shape(1, 2, 1, channels),
            shape(1, channels),
            shape(1, channels),
            shape(3, 1, channels),
            shape(1, 2, channels),
        ),
        in_specs=[spec(in_short), spec(out_short), kept, kept, whole, whole],
        out_specs=(spec(in_short), spec(out_short), placed, placed) + (whole,) * 6,
        compiler_params=pltpu.CompilerParams(vmem_limit_bytes=VMEM_BYTES),
    )(in_short, out_short, outs, grads, fin, total)
    *rest, rates, wkv = rest
    return in_wide, out_wide, *rest, jnp.swapaxes(rates, 0, 1), wkv


def shards(
    block_input,
    carried_state,
    output_cotangent,
    in_weight,
    out_weight,
    norm_gain,
    norm_bias,
    mix_rates,
    wkv_params,
):
    sections = lax.axis_size("section")
    outs, grads, fin, sums, kept = chain(
        sections,
        block_input,
        output_cotangent,
        in_weight,
        out_weight,
        norm_gain,
        norm_bias,
        jnp.swapaxes(mix_rates, 0, 1),
        wkv_params,
        carried_state,
    )
    in_short, out_short, total = reduced(lax.axis_size("dp"), kept, sums)
    in_grad, out_grad, outs, grads, states, normed, gain, bias, rates, wkv = finished_outputs(
        in_short, out_short, outs, grads, fin, total
    )
    return outs, states, normed, grads, in_grad[None], out_grad[None], gain, bias, rates, wkv


def solution(mesh):
    return jax.shard_map(
        shards,
        mesh=mesh,
        in_specs=(
            P(None, "dp", None, None),
            P("section", None, None, "dp", None),
            P(None, "dp", None, None),
            P("section", None, None),
            P("section", None, None),
            P("section", None),
            P("section", None),
            P("section", None, None),
            P("section", None, None),
        ),
        out_specs=(
            P("section", None, "dp", None, None),
            P("section", None, None, "dp", None),
            P("section", None, "dp", None),
            P("section", None, "dp", None, None),
            P("section", None, None),
            P("section", None, None),
            P("section", None),
            P("section", None),
            P("section", None, None),
            P("section", None, None),
        ),
        check_vma=False,
    )
```

time: 3410 us -> 298 us (0.09)
  other arithmetic: 964 us -> 0 us
  local copies, waits for them, and re-layouts: 758 us -> 0 us
  starting transfers between devices: 752 us -> 0 us
  waiting for transfers between devices: 575 us -> 0 us
  Pallas kernels: 0 us -> 297 us
  matrix products: 152 us -> 0 us
  loops' own time: 102 us -> 0 us
  blocking collectives: 74.1 us -> 0 us
    ppermute x20 -> x0, starting transfers between devices: 752 us -> none  [passed_along(): lax.ppermute(value, axis, [(source, source + steps) for source in range(l...]
    reduce_scatter x2 -> x0, waiting for transfers between devices: 360 us -> none  [the longest x1 197 us: sum_grads(): lax.psum_scatter(grad_parts[1], 'dp', scatter_dimension=0, tiled=True)]
    add x114 -> x0, other arithmetic: 308 us -> none  [the longest x50 285 us: tick(): grad_total = jax.tree.map(jnp.add, grad_total, grad_parts)]
    pallas_call x0 -> x3, Pallas kernels: none -> 297 us  [the longest x1 154 us: reduced(): pl.pallas_call(functools.partial(reduce_kernel, count, length, channels),...]
    dynamic_update_slice x72 -> x0, other arithmetic: 213 us -> none  [the longest x40 147 us: put_slot(): lax.dynamic_update_index_in_dim(store, jnp.where(valid, value, previous),...]
    dynamic_update_slice x176 -> x0, local copies, waits for them, and re-layouts: 199 us -> none  [weighted_value_blocks(): lax.scan(advance, (accruing_upper_sum, accruing_normalizer), (key_blocks,...]
    dynamic_slice x178 -> x0, local copies, waits for them, and re-layouts: 172 us -> none  [the longest x50 99 us: put_slot(): previous = lax.dynamic_index_in_dim(store, slot, axis_pos, keepdims=False)]
    dot_general x72 -> x0, matrix products: 152 us -> none  [the longest x48 68.1 us: advance(): summed = jnp.einsum('ts,bsc->btc', lower_mask, weighted, precision=precise)]
  transfers between devices with their start and end apart: 26 -> 0, of which waited for: 6 -> 0; matrix products, arithmetic and copies ran while one was open for 10% -> 0% of each run, Pallas kernels for 0% -> 0%
where the time goes in v1:
time: 298 us
  Pallas kernels  297 us (100%)
    pallas_call x1, Pallas kernels, reduced(): pl.pallas_call(functools.partial(reduce_kernel, count, length, channels),...  154 us
    pallas_call x1, Pallas kernels, chain(): pl.pallas_call(functools.partial(chain_kernel, sections, length, channels...  127 us
    pallas_call x1, Pallas kernels, finished_outputs(): pl.pallas_call(functools.partial(finish_kernel, steps), grid=(steps,), ou...  15.9 us

profile of v1, /device:TPU:0, one launch (start us, length us, event | category | flops | bytes accessed | tf_op | source)
XLA Modules:
  0.0 297.7 jit_solution(8460955022058183341)
XLA Ops:
  0.6 127.0 %shard_map.168 = (bf16[2,1024,768]{2,1,0:T(8,128)(2,1)}, bf16[2,1024,768]{2,1,0:T(8,128)(2,1)}, f32[2,8,768]{2,1,0:T(8,128)}, f32[2,8,768]{2,1,0:T(8,128)}, bf16[20,1024,768]{2,1,0:T(8,128)(2,1)}) custom-call(bf16[2,1,1024,768]{3,2,1,0:T(8,128)(2,1)} %x_hbm.1, bf16[2,1,1024,768]{3,2,1,0:T(8,128)(2,1)} %cot_hbm.1, bf16[1,768,3072]{2,1,0:T(8,128)(2,1)} %w_in_hbm.1, ...), custom_call_target="tpu_custom_call" | custom-call | tf_op jit(solution)/shard_map/pallas_call | solution.py:682
  127.7 153.9 %shard_map.169 = (bf16[768,3072]{1,0:T(8,128)(2,1)}, bf16[3840,768]{1,0:T(8,128)(2,1)}, f32[8,768]{1,0:T(8,128)}) custom-call(bf16[20,1024,768]{2,1,0:T(8,128)(2,1)} %get-tuple-element.28.kept_hbm, f32[2,8,768]{2,1,0:T(8,128)} %get-tuple-element.29.sums_hbm), custom_call_target="tpu_custom_call" | custom-call | tf_op jit(solution)/shard_map/pallas_call | solution.py:1280
  281.6 15.9 %shard_map.170 = (f32[768,3072]{1,0:T(8,128)}, f32[3840,768]{1,0:T(8,128)}, bf16[1,2,1,1024,768]{4,3,2,1,0:T(8,128)(2,1)}, bf16[1,2,1,1024,768]{4,3,2,1,0:T(8,12...) custom-call(bf16[768,3072]{1,0:T(8,128)(2,1)} %get-tuple-element.30., ...), custom_call_target="tpu_custom_call" | custom-call | tf_op jit(solution)/shard_map/pallas_call | solution.py:1379

commit v2 on v1

v2 whole, which is shorter than its diff:
```python
import functools

import jax
import jax.numpy as jnp
from jax import lax
from jax.experimental import pallas as pl
from jax.experimental.pallas import tpu as pltpu
from jax.sharding import PartitionSpec as P

MESH = pl.DeviceIdType.MESH
F32 = jnp.float32
BF16 = jnp.bfloat16
CHUNK = 256
ROWS = 32
UNROLL = 4
VMEM_BYTES = (64 << 20) - (128 << 10)

T_MIX0, T_MIX2, T_MIX1, T_GATED, C_MIX0, C_MIX1 = 0, 1, 2, 3, 4, 5
EARLY = 6
T_DK, T_DV, T_DQ, T_G, C_DKV, C_DQ, C_HID, C_DPRE = 0, 1, 2, 3, 4, 5, 6, 10
LATE = 14
GAIN, BIAS, RATES, DECAY, BONUS = 0, 1, 2, 5, 6


def nn(left, right):
    return jnp.dot(left, right, preferred_element_type=F32)


def nt(left, right):
    return lax.dot_general(left, right, (((1,), (1,)), ((), ())), preferred_element_type=F32)


def tn(left, right):
    return lax.dot_general(left, right, (((0,), (0,)), ((), ())), preferred_element_type=F32)


class Stack:
    def __init__(self, buffer, start, *heights):
        self.buffer, self.start, self.heights = buffer, start, heights

    @property
    def at(self):
        return Places(self)

    def __getitem__(self, index):
        return self.at[index][...]


class Places:
    def __init__(self, stack):
        self.stack = stack

    def __getitem__(self, index):
        index = index if isinstance(index, tuple) else (index,)
        start, height = self.stack.start, self.stack.heights[-1]
        for place, tall in zip(index, self.stack.heights, strict=True):
            start = start + place * tall
        if not isinstance(start, int):
            start = pl.multiple_of(start, 16)
        return self.stack.buffer.at[pl.ds(start, height)]


def folded(rows):
    total = rows[0:8]
    for start in range(8, rows.shape[0], 8):
        total = total + rows[start : start + 8]
    return total


def chain_kernel(
    sections,
    length,
    channels,
    hidden_blocks,
    count,
    x_hbm,
    cot_hbm,
    w_in_hbm,
    w_out_hbm,
    gain_hbm,
    bias_hbm,
    rates_hbm,
    wkv_hbm,
    state_hbm,
    outs_hbm,
    grads_hbm,
    fin_hbm,
    early_hbm,
    in_hbm,
    out_hbm,
    total_hbm,
    pool,
    early,
    kept,
    states,
    upstream,
    wide,
    pairs,
    tables,
    triangles,
    gains,
    biases,
    rates,
    wkvs,
    starts,
    previous,
    carry,
    carry_next,
    fin,
    sums,
    totals,
    weight_sem,
    weight_send,
    small_sem,
    small_send,
    entry_sem,
    entry_send,
    up_sem,
    up_send,
    out_sem,
    out_send,
    out_recv,
    early_sem,
    *reducing,
):
    section = lax.axis_index("section")
    dp_index = lax.axis_index("dp")
    core = section % 2
    stage = section // 2
    stages = sections // 2
    partner = {"section": section + 1 - 2 * core}
    chunks = length // CHUNK
    blocks = CHUNK // ROWS
    time_blocks = 4
    last_stage = stage == stages - 1
    weights = Stack(pool, 0, channels)
    after_weights = (9 + hidden_blocks) * channels
    entry = pool.at[pl.ds(after_weights, length)]
    hs = Stack(pool, after_weights + length, length)
    mid, top = hs.at[0], hs.at[1]

    barrier = pltpu.get_barrier_semaphore()
    across = {"dp": dp_index + 1 - 2 * (dp_index % 2)}
    for device in (partner, partner | across):
        pl.semaphore_signal(barrier, inc=1, device_id=device, device_id_type=MESH)

    def greet(offset, _):
        peer = {"dp": lax.rem(dp_index + offset, count)}
        pl.semaphore_signal(barrier, inc=1, device_id=peer, device_id_type=MESH)
        return 0

    lax.fori_loop(1, count, greet, 0)

    @pl.when(stage > 0)
    def _():
        pl.semaphore_signal(
            barrier, inc=1, device_id={"section": section - 2}, device_id_type=MESH
        )

    @pl.when(stage < stages - 1)
    def _():
        pl.semaphore_signal(
            barrier, inc=1, device_id={"section": section + 2}, device_id_type=MESH
        )

    def entry_copy(chunk):
        rows = pl.ds(chunk * CHUNK, CHUNK)
        return pltpu.make_async_copy(
            x_hbm.at[core, 0, rows], entry.at[rows], entry_sem.at[chunk]
        )

    def up_copy(chunk):
        rows = pl.ds(chunk * CHUNK, CHUNK)
        return pltpu.make_async_copy(
            cot_hbm.at[core, 0, rows], upstream.at[rows], up_sem.at[chunk]
        )

    @pl.when(stage == 0)
    def _():
        for chunk in range(chunks):
            entry_copy(chunk).start()

    @pl.when(last_stage)
    def _():
        for chunk in range(chunks):
            up_copy(chunk).start()

    small_pairs = (
        (gain_hbm, gains.at[core]),
        (bias_hbm, biases.at[core]),
        (rates_hbm, rates.at[core]),
        (wkv_hbm.at[0], wkvs.at[core]),
        (state_hbm.at[0], starts.at[core]),
    )
    small_copies = [
        pltpu.make_async_copy(source, target, small_sem.at[0, at])
        for at, (source, target) in enumerate(small_pairs)
    ]
    for copy in small_copies:
        copy.start()

    def in_block(index):
        return w_in_hbm.at[0, :, pl.ds(index * channels, channels)]

    def out_block(index):
        return w_out_hbm.at[0, pl.ds(index * channels, channels), :]

    for index in range(4):
        slot = core * time_blocks + index
        pltpu.make_async_copy(in_block(index), weights.at[slot], weight_sem.at[slot]).start()

    @pl.when(core == 1)
    def _():
        for index in range(hidden_blocks + 1):
            slot = 8 + index
            pltpu.make_async_copy(
                out_block(index), weights.at[slot], weight_sem.at[slot]
            ).start()

    has_previous = jnp.where(stage > 0, 1, 0)
    has_next = jnp.where(stage < stages - 1, 1, 0)
    pl.semaphore_wait(barrier, 1 + count + has_previous + has_next)

    small_remotes = [
        pltpu.make_async_remote_copy(
            src_ref=source,
            dst_ref=target,
            send_sem=small_send.at[at],
            recv_sem=small_sem.at[1, at],
            device_id=partner,
            device_id_type=MESH,
        )
        for at, (source, target) in enumerate(small_pairs)
    ]

    def in_remote(index):
        slot = core * time_blocks + index
        return pltpu.make_async_remote_copy(
            src_ref=in_block(index),
            dst_ref=weights.at[slot],
            send_sem=weight_send.at[slot],
            recv_sem=weight_sem.at[slot],
            device_id=partner,
            device_id_type=MESH,
        )

    def out_remote(index):
        slot = 8 + index
        return pltpu.make_async_remote_copy(
            src_ref=out_block(index),
            dst_ref=weights.at[slot],
            send_sem=weight_send.at[slot],
            recv_sem=weight_sem.at[slot],
            device_id=partner,
            device_id_type=MESH,
        )

    for copy in small_remotes:
        copy.start()
    for index in range(4):
        in_remote(index).start()

    @pl.when(core == 1)
    def _():
        for index in (hidden_blocks, *range(hidden_blocks)):
            out_remote(index).start()

    row_at = lax.broadcasted_iota(jnp.int32, (CHUNK, 2 * CHUNK), 0)
    column_at = lax.broadcasted_iota(jnp.int32, (CHUNK, 2 * CHUNK), 1)
    column_at = jnp.where(column_at >= CHUNK, column_at - CHUNK, column_at)
    triangles[0] = jnp.where(row_at > column_at, 1.0, 0.0).astype(BF16)
    triangles[1] = jnp.where(row_at < column_at, 1.0, 0.0).astype(BF16)
    sums[...] = jnp.zeros_like(sums)
    fin[...] = jnp.zeros_like(fin)

    for copy in small_copies:
        copy.wait()
    for copy in small_remotes:
        copy.wait_recv()

    rate = jnp.exp(wkvs[0, 0:1, :])
    step = jnp.exp(-rate)
    lift = jnp.exp(wkvs[0, 1:2, :])

    def table_rows(index, _):
        start = pl.multiple_of(index * ROWS, ROWS)
        place = (lax.broadcasted_iota(jnp.int32, (ROWS, channels), 0) + start).astype(F32)
        tables[0, pl.ds(start, ROWS), :] = jnp.exp(-(CHUNK - 1.0 - place) * rate)
        tables[1, pl.ds(start, ROWS), :] = jnp.exp(-place * rate)
        return 0

    lax.fori_loop(0, blocks, table_rows, 0)

    for row in range(3):
        carry[row : row + 1] = starts[0, row, core]
    carry[3:4] = starts[1, 0, core]

    def weight_wait(slot):
        pltpu.make_async_copy(weights.at[slot], weights.at[slot], weight_sem.at[slot]).wait()

    def stats(tokens):
        center = tokens - jnp.mean(tokens, axis=-1, keepdims=True)
        spread = jnp.mean(center * center, axis=-1, keepdims=True)
        root = lax.rsqrt(spread + 1e-05)
        return center * root, root

    row_index = lax.broadcasted_iota(jnp.int32, (ROWS, channels), 0)

    def token_mix(kind, source, base, side, slots, carry_row):
        gain, bias = gains[kind], biases[kind]

        def body(index, before):
            start = pl.multiple_of(base + index * ROWS, ROWS)
            rows = pl.ds(start, ROWS)
            unit, _ = stats(source[rows, :].astype(F32))
            normed = unit * gain + bias
            previous[kind, pl.ds(start // ROWS, 1), :] = before
            shifted = jnp.where(
                row_index == 0, jnp.broadcast_to(before, normed.shape), pltpu.roll(normed, 1, 0)
            )
            gap = normed - shifted
            for rate_row, slot in slots:
                early[side, slot, pl.ds(pl.multiple_of(index * ROWS, ROWS), ROWS), :] = (
                    shifted + gap * rates[kind, rate_row]
                ).astype(BF16)
            return normed[ROWS - 1 : ROWS, :]

        carry[carry_row : carry_row + 1] = lax.fori_loop(
            0, blocks, body, carry[carry_row : carry_row + 1], unroll=UNROLL
        )

    def early_copy(chunk):
        rows = pl.ds(pl.multiple_of(chunk * CHUNK, CHUNK), CHUNK)
        side = chunk % 2
        return pltpu.make_async_copy(
            early.at[side], early_hbm.at[:, rows], early_sem.at[side]
        )

    def forward_chunk(chunk, _):
        base = pl.multiple_of(chunk * CHUNK, CHUNK)
        rows = pl.ds(base, CHUNK)
        side = chunk % 2

        @pl.when(chunk >= 2)
        def _():
            early_copy(chunk - 2).wait()

        pltpu.make_async_copy(entry.at[rows], entry.at[rows], entry_sem.at[chunk]).wait()

        token_mix(0, entry, base, side, ((0, T_MIX0), (2, T_MIX2), (1, T_MIX1)), 0)

        for slot in range(3):

            @pl.when(chunk == 0)
            def _():
                weight_wait(slot)

            wide[slot] = nn(early[side, slot], weights[slot])

        def weighted(index, _):
            start = pl.multiple_of(index * ROWS, ROWS)
            local = pl.ds(start, ROWS)
            whole = pl.ds(pl.multiple_of(base + start, ROWS), ROWS)
            value = wide[1, local, :]
            power = jnp.exp(wide[0, local, :])
            wide[0, local, :] = power
            scaled = power * tables[0, local, :]
            pairs[local, pl.ds(0, channels)] = (scaled * value).astype(BF16)
            pairs[local, pl.ds(channels, channels)] = scaled.astype(BF16)
            kept[T_DK, whole, :] = power.astype(BF16)
            kept[T_DV, whole, :] = value.astype(BF16)
            return 0

        lax.fori_loop(0, blocks, weighted, 0)
        wide[3] = nn(triangles[0, :, pl.ds(0, CHUNK)], pairs[pl.ds(0, CHUNK), pl.ds(0, channels)])
        wide[4] = nn(
            triangles[0, :, pl.ds(0, CHUNK)], pairs[pl.ds(0, CHUNK), pl.ds(channels, channels)]
        )
        upper, lower = carry[1:2], carry[2:3]

        def averaged(index, _):
            start = pl.multiple_of(index * ROWS, ROWS)
            local = pl.ds(start, ROWS)
            whole = pl.ds(pl.multiple_of(base + start, ROWS), ROWS)
            place = (row_index + start).astype(F32)
            grown = jnp.exp((CHUNK - place) * rate)
            faded = tables[1, local, :]
            power, value = wide[0, local, :], wide[1, local, :]
            before_upper = grown * wide[3, local, :] + faded * upper
            before_lower = grown * wide[4, local, :] + faded * lower
            now = power * lift
            average = (before_upper + now * value) / (before_lower + now)
            gate = jax.nn.sigmoid(wide[2, local, :])
            states[0, whole, :] = before_upper
            states[1, whole, :] = before_lower
            kept[T_DQ, whole, :] = gate.astype(BF16)
            early[side, T_GATED, local, :] = (gate * average).astype(BF16)
            tail = slice(ROWS - 8, ROWS)
            after_upper = step * before_upper[tail] + power[tail] * value[tail]
            after_lower = step * before_lower[tail] + power[tail]
            carry_next[0:1] = after_upper[7:8]
            carry_next[1:2] = after_lower[7:8]
            return 0

        lax.fori_loop(0, blocks, averaged, 0)
        carry[1:3] = carry_next[0:2]

        @pl.when(chunk == 0)
        def _():
            weight_wait(3)

        mid[rows, :] = (
            entry[rows, :].astype(F32) + nn(early[side, T_GATED], weights[3])
        ).astype(BF16)

        token_mix(1, mid, base, side, ((0, C_MIX0), (1, C_MIX1)), 3)

        for index in range(hidden_blocks):

            @pl.when(chunk == 0)
            def _():
                weight_wait(4 + index)

            pre = nn(early[side, C_MIX0], weights[4 + index])
            kept[C_HID + index, rows, :] = jnp.square(jnp.maximum(pre, 0.0)).astype(BF16)

        @pl.when(chunk == 0)
        def _():
            weight_wait(8 + hidden_blocks)

        early_copy(chunk).start()
        wide[1] = nn(early[side, C_MIX1], weights[8 + hidden_blocks])

        @pl.when(chunk == 0)
        def _():
            for index in range(hidden_blocks):
                weight_wait(8 + index)

        total = nn(kept[C_HID, rows, :], weights[8])
        for index in range(1, hidden_blocks):
            total = total + nn(kept[C_HID + index, rows, :], weights[8 + index])
        wide[0] = total

        def joined(index, _):
            start = pl.multiple_of(index * ROWS, ROWS)
            local = pl.ds(start, ROWS)
            whole = pl.ds(pl.multiple_of(base + start, ROWS), ROWS)
            gate = jax.nn.sigmoid(wide[1, local, :])
            value = wide[0, local, :]
            kept[C_DKV, whole, :] = gate.astype(BF16)
            kept[C_DQ, whole, :] = value.astype(BF16)
            top[whole, :] = (mid[whole, :].astype(F32) + gate * value).astype(BF16)
            return 0

        lax.fori_loop(0, blocks, joined, 0)

        @pl.when(stage < stages - 1)
        def _():
            entry_remote(chunk).start()

        return 0

    def entry_remote(chunk):
        rows = pl.ds(pl.multiple_of(chunk * CHUNK, CHUNK), CHUNK)
        return pltpu.make_async_remote_copy(
            src_ref=top.at[rows],
            dst_ref=entry.at[rows],
            send_sem=entry_send.at[chunk],
            recv_sem=entry_sem.at[chunk],
            device_id={"section": section + 2},
            device_id_type=MESH,
        )

    def up_remote(chunk):
        rows = pl.ds(pl.multiple_of(chunk * CHUNK, CHUNK), CHUNK)
        return pltpu.make_async_remote_copy(
            src_ref=upstream.at[rows],
            dst_ref=upstream.at[rows],
            send_sem=up_send.at[chunk],
            recv_sem=up_sem.at[chunk],
            device_id={"section": section - 2},
            device_id_type=MESH,
        )

    lax.fori_loop(0, chunks, forward_chunk, 0)
    early_copy(chunks - 2).wait()
    early_copy(chunks - 1).wait()

    def mix_back(side, chunk):
        return pltpu.make_async_copy(
            early_hbm.at[C_MIX0 + side, pl.ds(chunk * CHUNK, CHUNK)],
            early.at[side, chunk],
            back_sem.at[side, chunk],
        )

    back_sem, reducing = reducing[0], reducing[1:]
    for side in range(2):
        for chunk in range(chunks):
            mix_back(side, chunk).start()

    fin[0, 0:1] = carry[0:1]
    fin[0, 1:3] = carry[1:3]
    fin[1, 0:1] = carry[3:4]

    def to_owner(index, own_src, other_src, dst):
        own = pltpu.make_async_copy(own_src, dst, out_sem.at[index])
        other = pltpu.make_async_remote_copy(
            src_ref=other_src,
            dst_ref=dst,
            send_sem=out_send.at[index],
            recv_sem=out_recv.at[index],
            device_id=partner,
            device_id_type=MESH,
        )
        return own, other

    outs_copies = to_owner(0, hs.at[core], hs.at[1 - core], outs_hbm.at[core])
    fin_copies = to_owner(1, fin.at[core], fin.at[1 - core], fin_hbm.at[core])
    for copy in outs_copies + fin_copies:
        copy.start()

    carry[0:4] = jnp.zeros((4, channels), F32)

    def norm_back(kind, source, base, mixes, above, target, carry_row):
        gain, bias = gains[kind], biases[kind]

        def body(index, after):
            back = blocks - 1 - index
            local = pl.ds(pl.multiple_of(back * ROWS, ROWS), ROWS)
            start = pl.multiple_of(base + back * ROWS, ROWS)
            rows = pl.ds(start, ROWS)
            unit, root = stats(source[rows, :].astype(F32))
            normed = unit * gain + bias
            before = previous[kind, pl.ds(start // ROWS, 1), :]
            shifted = jnp.where(
                row_index == 0, jnp.broadcast_to(before, normed.shape), pltpu.roll(normed, 1, 0)
            )
            gap = normed - shifted
            straight = jnp.zeros_like(normed)
            total = jnp.zeros_like(normed)
            for rate_row, slot in mixes:
                mix = wide[slot, local, :]
                straight = straight + mix * rates[kind, rate_row]
                total = total + mix
                sums[kind, RATES + rate_row] += folded(mix * gap)
            late = total - straight
            moved = jnp.where(
                row_index == ROWS - 1,
                jnp.broadcast_to(after, late.shape),
                pltpu.roll(late, ROWS - 1, 0),
            )
            d_normed = straight + moved
            sums[kind, GAIN] += folded(d_normed * unit)
            sums[kind, BIAS] += folded(d_normed)
            d_unit = d_normed * gain
            d_tokens = (
                d_unit
                - jnp.mean(d_unit, axis=-1, keepdims=True)
                - unit * jnp.mean(d_unit * unit, axis=-1, keepdims=True)
            ) * root
            target[rows, :] = (above[rows, :].astype(F32) + d_tokens).astype(BF16)
            return late[0:1, :]

        carry[carry_row : carry_row + 1] = lax.fori_loop(
            0, blocks, body, carry[carry_row : carry_row + 1], unroll=UNROLL
        )

    def grad_copies(chunk, kind):
        rows = pl.ds(pl.multiple_of(chunk * CHUNK, CHUNK), CHUNK)
        sources = (upstream.at[rows], kept.at[T_G, rows])
        return to_owner(
            2 + chunk, sources[kind], sources[1 - kind], grads_hbm.at[core, rows]
        )

    def backward_chunk(turn, _):
        chunk = chunks - 1 - turn
        base = pl.multiple_of(chunk * CHUNK, CHUNK)
        rows = pl.ds(base, CHUNK)
        pltpu.make_async_copy(upstream.at[rows], upstream.at[rows], up_sem.at[chunk]).wait()

        def split(index, _):
            whole = pl.ds(pl.multiple_of(base + index * ROWS, ROWS), ROWS)
            above = upstream[whole, :].astype(F32)
            gate = kept[C_DKV, whole, :].astype(F32)
            value = kept[C_DQ, whole, :].astype(F32)
            d_value = above * gate
            kept[C_DKV, whole, :] = d_value.astype(BF16)
            kept[C_DQ, whole, :] = (d_value * value * (1.0 - gate)).astype(BF16)
            return 0

        lax.fori_loop(0, blocks, split, 0)

        for index in range(hidden_blocks):
            d_hidden = nt(kept[C_DKV, rows, :], weights[8 + index])
            slope = jnp.sqrt(kept[C_HID + index, rows, :].astype(F32))
            kept[C_DPRE + index, rows, :] = (d_hidden * (2.0 * slope)).astype(BF16)
        total = nt(kept[C_DPRE, rows, :], weights[4])
        for index in range(1, hidden_blocks):
            total = total + nt(kept[C_DPRE + index, rows, :], weights[4 + index])
        wide[0] = total
        wide[1] = nt(kept[C_DQ, rows, :], weights[8 + hidden_blocks])
        norm_back(1, mid, base, ((0, 0), (1, 1)), upstream, kept.at[T_G], 3)

        wide[0] = nt(kept[T_G, rows, :], weights[3])

        def inputs(index, _):
            start = pl.multiple_of(index * ROWS, ROWS)
            local = pl.ds(start, ROWS)
            whole = pl.ds(pl.multiple_of(base + start, ROWS), ROWS)
            power = kept[T_DK, whole, :].astype(F32)
            value = kept[T_DV, whole, :].astype(F32)
            gate = kept[T_DQ, whole, :].astype(F32)
            now = power * lift
            inverse = 1.0 / (states[1, whole, :] + now)
            average = (states[0, whole, :] + now * value) * inverse
            d_average = wide[0, local, :] * gate
            kept[T_DQ, whole, :] = (d_average * average * (1.0 - gate)).astype(BF16)
            unit = d_average * inverse
            wide[1, local, :] = unit
            wide[2, local, :] = average
            scaled = unit * tables[1, local, :]
            for column, term in ((0, scaled), (channels, -scaled * average)):
                high = term.astype(BF16)
                pairs[local, pl.ds(column, channels)] = high
                pairs[pl.ds(pl.multiple_of(CHUNK + start, ROWS), ROWS), pl.ds(column, channels)] = (
                    term - high.astype(F32)
                ).astype(BF16)
            return 0

        lax.fori_loop(0, blocks, inputs, 0)
        wide[3] = nn(triangles[1], pairs[:, pl.ds(0, channels)])
        wide[4] = nn(triangles[1], pairs[:, pl.ds(channels, channels)])
        alpha_after, beta_after = carry[1:2], carry[2:3]

        def outputs(index, _):
            start = pl.multiple_of((blocks - 1 - index) * ROWS, ROWS)
            local = pl.ds(start, ROWS)
            whole = pl.ds(pl.multiple_of(base + start, ROWS), ROWS)
            place = (row_index + start).astype(F32)
            grown = jnp.exp((place + 1.0) * rate)
            faded = tables[0, local, :]
            alpha = grown * wide[3, local, :] + faded * alpha_after
            beta = grown * wide[4, local, :] + faded * beta_after
            unit, average = wide[1, local, :], wide[2, local, :]
            power = kept[T_DK, whole, :].astype(F32)
            value = kept[T_DV, whole, :].astype(F32)
            weighed = unit * (power * lift)
            own = weighed * (value - average)
            kept[T_DK, whole, :] = (own + power * (alpha * value + beta)).astype(BF16)
            kept[T_DV, whole, :] = (weighed + power * alpha).astype(BF16)
            sums[0, BONUS] += folded(own)
            sums[0, DECAY] += folded(
                alpha * states[0, whole, :] + beta * states[1, whole, :]
            )
            carry_next[0:1] = unit[0:1] + step * alpha[0:1]
            carry_next[1:2] = step * beta[0:1] - unit[0:1] * average[0:1]
            return 0

        lax.fori_loop(0, blocks, outputs, 0)
        carry[1:3] = carry_next[0:2]
        wide[0] = nt(kept[T_DK, rows, :], weights[0])
        wide[1] = nt(kept[T_DQ, rows, :], weights[2])
        wide[2] = nt(kept[T_DV, rows, :], weights[1])
        norm_back(
            0, entry, base, ((0, 0), (1, 1), (2, 2)), kept.at[T_G], upstream, 0
        )

        @pl.when(stage > 0)
        def _():
            up_remote(chunk).start()

        for kind in range(2):

            @pl.when(core == kind)
            def _():
                for copy in grad_copies(chunk, kind):
                    copy.start()

        return 0

    lax.fori_loop(0, chunks, backward_chunk, 0)

    sums[0, DECAY] = sums[0, DECAY] * (-rate * step)
    for kind in range(2):
        for row in range(7):
            totals[kind, row : row + 1] = jnp.sum(sums[kind, row], axis=0, keepdims=True)
        totals[kind, 7:8] = jnp.zeros((1, channels), F32)

    for copy in outs_copies:
        copy.wait()

    @pl.when(stage < stages - 1)
    def _():
        for chunk in range(chunks):
            entry_remote(chunk).wait_send()

    reduce_phase(
        count, channels, pool, early, kept, early_hbm, totals, mix_back, in_hbm, out_hbm, total_hbm, *reducing
    )

    for copy in fin_copies:
        copy.wait()
    for chunk in range(chunks):
        for copy in grad_copies(chunk, 0):
            copy.wait()
    for copy in small_remotes:
        copy.wait_send()
    for index in range(4):
        in_remote(index).wait_send()

    @pl.when(core == 1)
    def _():
        for index in range(hidden_blocks + 1):
            out_remote(index).wait_send()

    @pl.when(stage > 0)
    def _():
        for chunk in range(chunks):
            up_remote(chunk).wait_send()


C_BLOCKS = 9
T_BLOCKS = 4
BLOCKS = C_BLOCKS + T_BLOCKS
PLACES = (8, 9, 0, 1, 2, 10, 3, 11, 4, 5, 6, 12, 7)
PAIRED = 8


def lookup(index, table):
    value = jnp.int32(table[0])
    for at, entry in enumerate(table[1:], 1):
        value = jnp.where(index == at, entry, value)
    return value


def reduce_plan(line, half):
    pieces = (max(16, half // (2 * line)), max(16, half // line))
    sizes = (2 * line * pieces[0], line * pieces[1])
    counts = (-(-PAIRED * half // sizes[0]), -(-(BLOCKS - PAIRED) * half // sizes[1]))
    return pieces, sizes, counts


def ready_times(first, size, count, half):
    made = {place: time for time, place in enumerate(PLACES)}
    times = []
    for group in range(count):
        begin, end = first + group * size, first + (group + 1) * size
        times.append(
            max(made[place] for place in range(BLOCKS) if place * half < end and begin < (place + 1) * half)
        )
    return tuple(times)


COMPUTE = 2
ORDER_OF_FOUR = (
    2000, 1000, 2010, 1010, 2020, 1001, 2030, 2040, 20, 1011, 1002, 2050, 1020, 2060, 2070, 1003,
    21, 1012, 2080, 40, 1021, 2090, 2100, 1004, 22, 1013, 2110, 1022, 41, 10, 2120, 1005,
    1014, 23, 1023, 42, 1006, 11, 1040, 1015, 24, 1024, 43, 1007, 50, 1041, 0, 12,
    1016, 1025, 25, 51, 1042, 1, 30, 1017, 52, 1026, 13, 26, 1043, 2, 53, 1027,
    31, 27, 3, 60, 14, 32, 1044, 4, 1030, 15, 61, 33, 70, 1045, 5, 54,
    1031, 16, 62, 1046, 71, 6, 55, 1047, 1032, 72, 17, 56, 63, 7, 57, 73,
    1033, 34, 44, 64, 35, 74, 45, 65, 75, 36, 46, 1034, 76, 66, 37, 47,
    1035, 77, 67, 1036, 1037,
)


def event_order(line, half):
    _, sizes, counts = reduce_plan(line, half)
    if line == 4 and counts == (8, 5):
        return [(code // 1000, code // 10 % 100, code % 10) for code in ORDER_OF_FOUR]
    firsts = (0, counts[0] * sizes[0])
    steps = [(block, 0, (COMPUTE, block, 0)) for block in range(BLOCKS)]
    for kind in range(2):
        times = ready_times(firsts[kind], sizes[kind], counts[kind], half)
        for group, time in enumerate(times):
            steps += [(time + turn, 1 + kind, (kind, group, turn)) for turn in range(2 * line)]
    return [step for _, _, step in sorted(steps)]


def reduce_phase(
    count,
    channels,
    pool,
    early,
    kept,
    early_hbm,
    totals,
    mix_back,
    in_hbm,
    out_hbm,
    total_hbm,
    small,
    ready_sem,
    back_sem,
    pair_sem,
    pair_send,
    y_sem,
    y_send,
    sum_sem0,
    sum_send0,
    sum_sem1,
    sum_send1,
    spread_sem0,
    spread_send0,
    spread_sem1,
    spread_send1,
    give_sem,
    give_send,
    give_recv,
    small_sem,
    small_send,
):
    section = lax.axis_index("section")
    dp_index = lax.axis_index("dp")
    core = section % 2
    line = count // 2
    z, y = dp_index // 2, dp_index % 2
    half = channels // 2
    pieces, sizes, counts = reduce_plan(line, half)
    firsts = (0, counts[0] * sizes[0])
    partner = {"section": section + 1 - 2 * core}
    across = {"dp": dp_index + 1 - 2 * y}

    def peer(offset):
        return {"dp": lax.rem(dp_index + offset, count)}

    length, chunks = kept.shape[1], early.shape[1] - 2
    starts, _ = pool_plan(count, channels, length, 0)
    mine = pool.at[pl.ds(starts[0], starts[1] - starts[0])]
    theirs = Stack(pool, starts[1], half)
    pair_landing = Stack(pool, starts[2], sizes[0] // 2)
    cross_landing = Stack(pool, starts[3], pieces[1])
    passed = [Stack(pool, starts[4 + kind], (line + 1) * pieces[kind], pieces[kind]) for kind in range(2)]

    def landing(kind, direction, group, step):
        return passed[kind].at[group, step if direction == 0 else line - step]

    right_peer, left_peer = {"dp": dp_index + 2}, {"dp": dp_index - 2}

    def ready(device):
        pl.semaphore_signal(ready_sem, inc=1, device_id=device, device_id_type=MESH)

    ready(partner)
    ready(across)
    pl.when(z < line - 1)(lambda: ready(right_peer))
    pl.when(z > 0)(lambda: ready(left_peer))
    neighbours = 2 + jnp.where(z < line - 1, 1, 0) + jnp.where(z > 0, 1, 0)

    small_pair = pltpu.make_async_remote_copy(
        src_ref=totals.at[1 - core],
        dst_ref=small.at[1],
        send_sem=small_send.at[0],
        recv_sem=small_sem.at[1],
        device_id=partner,
        device_id_type=MESH,
    )

    def small_copy(offset):
        return pltpu.make_async_remote_copy(
            src_ref=small.at[0],
            dst_ref=small.at[1 + offset],
            send_sem=small_send.at[offset],
            recv_sem=small_sem.at[1 + offset],
            device_id=peer(offset),
            device_id_type=MESH,
        )

    def small_start(offset, _):
        small_copy(offset).start()
        return 0

    def small_add(offset, total):
        small_copy(offset).wait()
        return total + small[1 + offset]

    def product(block, which, use):
        columns = pl.ds(pl.multiple_of(which * half, 128), half)
        turn = block - C_BLOCKS
        mixed = (block < 4) | (block == 8)

        @pl.when(mixed)
        def _():
            side = jnp.where(block == 8, 1, 0)
            left = early[side, pl.ds(0, chunks), :, columns].reshape(length, half)
            use(tn(left, kept[jnp.where(block == 8, C_DQ, C_DPRE + block)]))

        @pl.when(~mixed)
        def _():
            left = jnp.where(block < 8, C_HID + block - 4, C_DPRE + turn)
            use(tn(kept[left, :, columns], kept[jnp.where(block < 8, C_DKV, T_DK + turn)]))

    def time_mix_back(turn):
        return pltpu.make_async_copy(
            early_hbm.at[T_MIX0 + turn], kept.at[C_DPRE + turn], back_sem.at[turn]
        )

    def block_rows(block):
        return pl.ds(pl.multiple_of(lookup(block, PLACES) * half, half), half)

    def pair_copy(block):
        return pltpu.make_async_remote_copy(
            src_ref=theirs.at[block % 2],
            dst_ref=mine.at[block_rows(block)],
            send_sem=pair_send.at[block],
            recv_sem=pair_sem.at[block],
            device_id=partner,
            device_id_type=MESH,
        )

    def for_partner(block):
        for side, first in ((0, 0), (1, 8)):

            @pl.when(block == first)
            def _():
                for chunk in range(chunks):
                    mix_back(side, chunk).wait()

        pl.when(block >= C_BLOCKS)(lambda: time_mix_back(block - C_BLOCKS).wait())
        pl.when(block >= 2)(lambda: pair_copy(block - 2).wait_send())

        def store(gradient):
            theirs.at[block % 2][...] = gradient.astype(BF16)

        product(block, 1 - core, store)

        @pl.when(block == 0)
        def _():
            pl.semaphore_wait(ready_sem, neighbours)
            small_pair.start()

        pair_copy(block).start()

    def for_me(block):
        rows = block_rows(block)

        def add(gradient):
            pair_copy(block).wait_recv()
            mine[rows, :] = (gradient + mine[rows, :].astype(F32)).astype(BF16)

        product(block, core, add)
        pl.when(block < 4)(lambda: time_mix_back(block).start())

    blocks_at = tuple(PLACES.index(place) for place in range(BLOCKS))

    def give(kind, group, start):
        size = pieces[kind]
        rows = pl.ds(pl.multiple_of(start, size), size)
        place = start // half if half % sizes[kind] else firsts[kind] // half + group * sizes[kind] // half
        block = lookup(place, blocks_at)
        row = core * half + start - place * half

        def copies(owner, target):
            @pl.when(owner == core)
            def _():
                pltpu.make_async_copy(mine.at[rows], target, give_sem.at[0]).start()

            def remote(device):
                return pltpu.make_async_remote_copy(
                    src_ref=mine.at[rows],
                    dst_ref=target,
                    send_sem=give_send.at[0],
                    recv_sem=give_recv.at[0],
                    device_id=device,
                    device_id_type=MESH,
                )

            @pl.when(owner != core)
            def _():
                remote(partner).start()

            if kind == 0:
                remote({"section": section - core + owner, "dp": dp_index + 1 - 2 * y}).start()

        def to_in(owner, column):
            columns = pl.ds(pl.multiple_of(column * channels, channels), channels)
            copies(owner, in_hbm.at[pl.ds(pl.multiple_of(row, size), size), columns])

        def to_out():
            within = (block - 4) * channels + row
            copies(1, out_hbm.at[pl.ds(pl.multiple_of(within, size), size)])

        of_time = block >= C_BLOCKS
        pl.when((block < 4) | (of_time & (place < BLOCKS)))(
            lambda: to_in(jnp.where(of_time, 0, 1), jnp.where(of_time, block - C_BLOCKS, block))
        )
        pl.when((block >= 4) & ~of_time)(to_out)

    sum_sems = ((sum_sem0, sum_send0), (sum_sem1, sum_send1))
    spread_sems = ((spread_sem0, spread_send0), (spread_sem1, spread_send1))

    def piece_rows(kind, group, index):
        start = firsts[kind] + group * sizes[kind] + index * pieces[kind]
        if kind == 0:
            start = start + y * (sizes[0] // 2)
        return start, pl.ds(pl.multiple_of(start, pieces[kind]), pieces[kind])

    def sum_copy(kind, group, direction, step):
        place = landing(kind, direction, group, step)
        receive, send = sum_sems[kind]
        return pltpu.make_async_remote_copy(
            src_ref=place,
            dst_ref=place,
            send_sem=send.at[group, direction, step],
            recv_sem=receive.at[group, direction, step],
            device_id=(right_peer, left_peer)[direction],
            device_id_type=MESH,
        )

    def spread_copy(kind, group, direction, step, index):
        _, rows = piece_rows(kind, group, index)
        receive, send = spread_sems[kind]
        return pltpu.make_async_remote_copy(
            src_ref=mine.at[rows],
            dst_ref=mine.at[rows],
            send_sem=send.at[group, direction, step],
            recv_sem=receive.at[group, direction, step],
            device_id=(right_peer, left_peer)[direction],
            device_id_type=MESH,
        )

    def passing(kind, group, turn):
        for direction in range(2):
            behind = z if direction == 0 else line - 1 - z
            step = turn - behind
            index = line - 1 - step if direction == 0 else step
            place = landing(kind, direction, group, step)
            _, rows = piece_rows(kind, group, index)

            @pl.when((step >= 0) & (behind == 0) & (step < line - 1))
            def _():
                place[...] = mine[rows, :]
                sum_copy(kind, group, direction, step).start()

            @pl.when((step >= 0) & (behind > 0))
            def _():
                sum_copy(kind, group, direction, step).wait_recv()

                @pl.when(turn < line - 1)
                def _():
                    place[...] = (place[...].astype(F32) + mine[rows, :].astype(F32)).astype(BF16)
                    sum_copy(kind, group, direction, step).start()

    def arrived(kind, group):
        _, rows = piece_rows(kind, group, z)
        total = mine[rows, :].astype(F32)
        from_left = landing(kind, 0, group, jnp.minimum(line - 1 - z, line - 2))
        from_right = landing(kind, 1, group, jnp.minimum(z, line - 2))
        mine[rows, :] = total.astype(BF16)

        @pl.when(z == 0)
        def _():
            mine[rows, :] = (total + from_right[...].astype(F32)).astype(BF16)

        @pl.when(z == line - 1)
        def _():
            mine[rows, :] = (total + from_left[...].astype(F32)).astype(BF16)

        @pl.when((z > 0) & (z < line - 1))
        def _():
            mine[rows, :] = (
                total + from_left[...].astype(F32) + from_right[...].astype(F32)
            ).astype(BF16)

    def finished(kind, group, index):
        start, _ = piece_rows(kind, group, index)
        give(kind, group, start)

    def spread_own(kind, group):
        @pl.when(z < line - 1)
        def _():
            spread_copy(kind, group, 0, 0, z).start()

        @pl.when(z > 0)
        def _():
            spread_copy(kind, group, 1, 0, z).start()

        finished(kind, group, z)

    def spreading(kind, group, hop):
        for direction in range(2):
            index = z - hop if direction == 0 else z + hop
            onward = z < line - 1 if direction == 0 else z > 0
            exists = index >= 0 if direction == 0 else index < line

            @pl.when(exists)
            def _():
                spread_copy(kind, group, direction, hop - 1, index).wait_recv()

                @pl.when(onward)
                def _():
                    spread_copy(kind, group, direction, hop, index).start()

                finished(kind, group, index)

    def over(group):
        start = group * sizes[0] + (1 - y) * (sizes[0] // 2)
        return pltpu.make_async_remote_copy(
            src_ref=mine.at[pl.ds(pl.multiple_of(start, pieces[0]), sizes[0] // 2)],
            dst_ref=pair_landing.at[group],
            send_sem=y_send.at[group],
            recv_sem=y_sem.at[group],
            device_id=across,
            device_id_type=MESH,
        )

    def swap(group):
        _, rows = piece_rows(1, group, z)
        return pltpu.make_async_remote_copy(
            src_ref=mine.at[rows],
            dst_ref=cross_landing.at[group],
            send_sem=y_send.at[counts[0] + group],
            recv_sem=y_sem.at[counts[0] + group],
            device_id=across,
            device_id_type=MESH,
        )

    def event0(group, turn):
        @pl.when(turn == 0)
        def _():
            over(group).start()

        @pl.when(turn == 1)
        def _():
            over(group).wait_recv()

            def add(index, _):
                _, rows = piece_rows(0, group, index)
                local = pl.ds(pl.multiple_of(index * pieces[0], pieces[0]), pieces[0])
                arrived_rows = pair_landing.at[group][local, :]
                mine[rows, :] = (mine[rows, :].astype(F32) + arrived_rows.astype(F32)).astype(BF16)
                return 0

            lax.fori_loop(0, line, add, 0)

        @pl.when((turn >= 1) & (turn <= line))
        def _():
            passing(0, group, turn - 1)

        @pl.when(turn == line)
        def _():
            arrived(0, group)
            spread_own(0, group)

        @pl.when(turn > line)
        def _():
            spreading(0, group, turn - line)

    def event1(group, turn):
        @pl.when(turn < line)
        def _():
            passing(1, group, turn)

        @pl.when(turn == line - 1)
        def _():
            arrived(1, group)
            swap(group).start()

        @pl.when(turn == line)
        def _():
            swap(group).wait()
            _, rows = piece_rows(1, group, z)
            mine[rows, :] = (
                mine[rows, :].astype(F32) + cross_landing[group].astype(F32)
            ).astype(BF16)
            spread_own(1, group)

        @pl.when(turn > line)
        def _():
            spreading(1, group, turn - line)

    spare = firsts[1] + counts[1] * sizes[1] - BLOCKS * half
    if spare:
        mine[pl.ds(BLOCKS * half, spare), :] = jnp.zeros((spare, channels), BF16)
    order = [(COMPUTE, 0, 0)]
    for kind, group, turn in event_order(line, half):
        if kind == COMPUTE:
            order += [(COMPUTE, group + 1, 0)] * (group + 1 < BLOCKS) + [(COMPUTE, group, 1)]
        else:
            order.append((kind, group, turn))
    codes = [kind * 1024 + group * 64 + turn for kind, group, turn in order]
    steps = len(codes)
    words = tuple(a + 4096 * b for a, b in zip(codes[::2], (codes + [0])[1::2], strict=True))

    def take(index, _):
        word = lookup(index // 2, words)
        code = jnp.where(index % 2 == 0, word % 4096, word // 4096)
        kind, group, turn = code // 1024, code // 64 % 16, code % 64

        @pl.when(kind == COMPUTE)
        def _():
            pl.when(turn == 0)(lambda: for_partner(group))
            pl.when(turn == 1)(lambda: for_me(group))

            @pl.when((turn == 1) & (group == BLOCKS // 2))
            def _():
                small_pair.wait()
                small[0] = totals[core] + small[1]
                lax.fori_loop(1, count, small_start, 0)

        pl.when(kind == 0)(lambda: event0(group, turn))
        pl.when(kind == 1)(lambda: event1(group, turn))
        return 0

    lax.fori_loop(0, steps, take, 0)
    small[0] = lax.fori_loop(1, count, small_add, small[0])
    total_copy = pltpu.make_async_copy(small.at[0], total_hbm, small_sem.at[0])
    total_copy.start()

    def over_done(group, _):
        over(group).wait_send()
        return 0

    for block in range(BLOCKS - 2, BLOCKS):
        pair_copy(jnp.int32(block)).wait_send()
    lax.fori_loop(0, counts[0], over_done, 0)
    for kind in range(2):

        def group_done(group, _):
            def step_done(step, _):
                for direction in range(2):
                    behind = z if direction == 0 else line - 1 - z

                    @pl.when(step < line - 1 - behind)
                    def _():
                        sum_copy(kind, group, direction, step).wait_send()

                    @pl.when((step <= behind) & (behind < line - 1))
                    def _():
                        spread_copy(kind, group, direction, step, 0).wait_send()

                return 0

            return lax.fori_loop(0, line - 1, step_done, 0)

        lax.fori_loop(0, counts[kind], group_done, 0)

    def taken(rows, sem):
        if rows:
            ref = mine.at[pl.ds(0, rows)]
            pltpu.make_async_copy(ref, ref, sem.at[0]).wait()

    paired = [PLACES[block] < PAIRED for block in range(BLOCKS)]
    whole = [half // 2 if pair else half for pair in paired]
    by_kind = (range(C_BLOCKS, BLOCKS), range(C_BLOCKS))
    for own in range(2):

        @pl.when(core == own)
        def _():
            local = sum(whole[block] for block in by_kind[own])
            crossed = sum(half // 2 for block in range(BLOCKS) if paired[block])
            other = sum(whole[block] for block in by_kind[1 - own])
            taken(local, give_sem)
            taken(other + crossed, give_send)
            taken(len(by_kind[own]) * channels - local, give_recv)

    total_copy.wait()


def pool_plan(count, channels, length, slots):
    half, line = channels // 2, count // 2
    pieces, sizes, counts = reduce_plan(line, half)
    heights = (
        counts[0] * sizes[0] + counts[1] * sizes[1],
        2 * half,
        counts[0] * sizes[0] // 2,
        counts[1] * pieces[1],
        *[counts[kind] * (line + 1) * pieces[kind] for kind in range(2)],
    )
    starts = [sum(heights[:at]) for at in range(len(heights))]
    return starts, max(sum(heights), slots * channels + 3 * length)


def chain(sections, count, x, cotangent, w_in, w_out, gain, bias, rates, wkv, state):
    length, channels = x.shape[2:]
    hidden_blocks = w_in.shape[2] // channels
    chunks = length // CHUNK
    anywhere = pl.BlockSpec(memory_space=pl.ANY)
    dma = pltpu.SemaphoreType.DMA
    slots = 9 + hidden_blocks
    line = count // 2
    _, _, counts = reduce_plan(line, channels // 2)
    hops = [dma((counts[kind], 2, line - 1)) for kind in range(2)]
    _, pool_rows = pool_plan(count, channels, length, slots)
    return pl.pallas_call(
        functools.partial(chain_kernel, sections, length, channels, hidden_blocks, count),
        out_shape=(
            jax.ShapeDtypeStruct((2, length, channels), BF16),
            jax.ShapeDtypeStruct((2, length, channels), BF16),
            jax.ShapeDtypeStruct((2, 8, channels), F32),
            jax.ShapeDtypeStruct((EARLY, length, channels), BF16),
            jax.ShapeDtypeStruct((channels, 4 * channels), BF16),
            jax.ShapeDtypeStruct(((C_BLOCKS - 4) * channels, channels), BF16),
            jax.ShapeDtypeStruct((8, channels), F32),
        ),
        in_specs=[anywhere] * 9,
        out_specs=(anywhere,) * 7,
        scratch_shapes=[
            pltpu.VMEM((pool_rows, channels), BF16),
            pltpu.VMEM((2, EARLY, CHUNK, channels), BF16),
            pltpu.VMEM((LATE, length, channels), BF16),
            pltpu.VMEM((2, length, channels), F32),
            pltpu.VMEM((length, channels), BF16),
            pltpu.VMEM((5, CHUNK, channels), F32),
            pltpu.VMEM((2 * CHUNK, 2 * channels), BF16),
            pltpu.VMEM((2, CHUNK, channels), F32),
            pltpu.VMEM((2, CHUNK, 2 * CHUNK), BF16),
            pltpu.VMEM((2, 1, channels), F32),
            pltpu.VMEM((2, 1, channels), F32),
            pltpu.VMEM((2, 3, 1, channels), F32),
            pltpu.VMEM((2, 2, channels), F32),
            pltpu.VMEM((2, 3, 2, 1, channels), F32),
            pltpu.VMEM((2, length // ROWS, channels), F32),
            pltpu.VMEM((8, channels), F32),
            pltpu.VMEM((8, channels), F32),
            pltpu.VMEM((2, 8, channels), F32),
            pltpu.VMEM((2, 8, 8, channels), F32),
            pltpu.VMEM((2, 8, channels), F32),
            dma((slots,)),
            dma((slots,)),
            dma((2, 5)),
            dma((5,)),
            dma((chunks,)),
            dma((chunks,)),
            dma((chunks,)),
            dma((chunks,)),
            dma((2 + chunks,)),
            dma((2 + chunks,)),
            dma((2 + chunks,)),
            dma((2,)),
            dma((2, chunks)),
            pltpu.VMEM((count + 1, 8, channels), F32),
            pltpu.SemaphoreType.REGULAR,
            dma((4,)),
            dma((BLOCKS,)),
            dma((BLOCKS,)),
            dma((sum(counts),)),
            dma((sum(counts),)),
            hops[0],
            hops[0],
            hops[1],
            hops[1],
            hops[0],
            hops[0],
            hops[1],
            hops[1],
            dma((1,)),
            dma((1,)),
            dma((1,)),
            dma((count + 1,)),
            dma((count + 1,)),
        ],
        compiler_params=pltpu.CompilerParams(
            collective_id=0, has_side_effects=True, vmem_limit_bytes=VMEM_BYTES
        ),
    )(x, cotangent, w_in, w_out, gain, bias, rates, wkv, state)


def finish_kernel(
    steps,
    in_short,
    out_short,
    outs_in,
    grads_in,
    fin,
    total,
    in_wide,
    out_wide,
    outs,
    grads,
    states,
    normed,
    gain,
    bias,
    rates,
    wkv,
):
    holds_channel_mix = lax.axis_index("section") % 2 == 1
    step = pl.program_id(0)

    @pl.when(step == 0)
    def _():
        for micro in range(2):
            normed[0, micro] = fin[micro, 0:1]
            for row in range(2):
                states[0, row, micro] = fin[micro, 1 + row : 2 + row]
        gain[...] = total[GAIN : GAIN + 1]
        bias[...] = total[BIAS : BIAS + 1]
        for row in range(3):
            rates[row] = total[RATES + row : RATES + row + 1]
        wkv[0] = total[DECAY : DECAY + 2]

    in_wide[...] = in_short[...].astype(F32)
    out_wide[...] = jnp.where(holds_channel_mix, out_short[...].astype(F32), 0.0)
    outs[0, :, 0] = outs_in[...]
    grads[0, :, 0] = grads_in[...]


def finished_outputs(in_short, out_short, outs, grads, fin, total):
    steps = 8
    length, channels = outs.shape[1:]
    whole = pl.BlockSpec(memory_space=pltpu.VMEM)
    kept = pl.BlockSpec((2, length // steps, channels), lambda i: (0, i, 0))
    placed = pl.BlockSpec((1, 2, 1, length // steps, channels), lambda i: (0, 0, 0, i, 0))

    def spec(array):
        rows, columns = array.shape
        return pl.BlockSpec((rows // steps, columns), lambda i: (i, 0))

    def shape(*sizes, dtype=F32):
        return jax.ShapeDtypeStruct(sizes, dtype)

    in_wide, out_wide, *rest = pl.pallas_call(
        functools.partial(finish_kernel, steps),
        grid=(steps,),
        out_shape=(
            shape(*in_short.shape),
            shape(*out_short.shape),
            shape(1, 2, 1, length, channels, dtype=BF16),
            shape(1, 2, 1, length, channels, dtype=BF16),
            shape(1, 2, 2, 1, channels),
            shape(1, 2, 1, channels),
            shape(1, channels),
            shape(1, channels),
            shape(3, 1, channels),
            shape(1, 2, channels),
        ),
        in_specs=[spec(in_short), spec(out_short), kept, kept, whole, whole],
        out_specs=(spec(in_short), spec(out_short), placed, placed) + (whole,) * 6,
        compiler_params=pltpu.CompilerParams(vmem_limit_bytes=VMEM_BYTES),
    )(in_short, out_short, outs, grads, fin, total)
    *rest, rates, wkv = rest
    return in_wide, out_wide, *rest, jnp.swapaxes(rates, 0, 1), wkv


def shards(
    block_input,
    carried_state,
    output_cotangent,
    in_weight,
    out_weight,
    norm_gain,
    norm_bias,
    mix_rates,
    wkv_params,
):
    sections = lax.axis_size("section")
    outs, grads, fin, _, in_short, out_short, total = chain(
        sections,
        lax.axis_size("dp"),
        block_input,
        output_cotangent,
        in_weight,
        out_weight,
        norm_gain,
        norm_bias,
        jnp.swapaxes(mix_rates, 0, 1),
        wkv_params,
        carried_state,
    )
    in_grad, out_grad, outs, grads, states, normed, gain, bias, rates, wkv = finished_outputs(
        in_short, out_short, outs, grads, fin, total
    )
    return outs, states, normed, grads, in_grad[None], out_grad[None], gain, bias, rates, wkv


def solution(mesh):
    return jax.shard_map(
        shards,
        mesh=mesh,
        in_specs=(
            P(None, "dp", None, None),
            P("section", None, None, "dp", None),
            P(None, "dp", None, None),
            P("section", None, None),
            P("section", None, None),
            P("section", None),
            P("section", None),
            P("section", None, None),
            P("section", None, None),
        ),
        out_specs=(
            P("section", None, "dp", None, None),
            P("section", None, None, "dp", None),
            P("section", None, "dp", None),
            P("section", None, "dp", None, None),
            P("section", None, None),
            P("section", None, None),
            P("section", None),
            P("section", None),
            P("section", None, None),
            P("section", None, None),
        ),
        check_vma=False,
    )
```

time: 298 us -> 293 us (0.983)
  Pallas kernels: 297 us -> 292 us
    pallas_call x1 -> x0, Pallas kernels: 154 us -> none  [reduced(): pl.pallas_call(functools.partial(reduce_kernel, count, length, channels),...]
    pallas_call x1, Pallas kernels: 127 us -> 276 us  [chain(): pl.pallas_call(functools.partial(chain_kernel, sections, length, channels...]
where the time goes in v2:
time: 293 us
  Pallas kernels  292 us (100%)
    pallas_call x1, Pallas kernels, chain(): pl.pallas_call(functools.partial(chain_kernel, sections, length, channels...  276 us
    pallas_call x1, Pallas kernels, finished_outputs(): pl.pallas_call(functools.partial(finish_kernel, steps), grid=(steps,), ou...  15.9 us

profile of v2, /device:TPU:0, one launch (start us, length us, event | category | flops | bytes accessed | tf_op | source)
XLA Modules:
  0.0 292.6 jit_solution(10537157835434095778)
XLA Ops:
  0.6 275.8 %shard_map.168 = (bf16[2,1024,768]{2,1,0:T(8,128)(2,1)}, bf16[2,1024,768]{2,1,0:T(8,128)(2,1)}, f32[2,8,768]{2,1,0:T(8,128)}, bf16[6,1024,768]{2,1,0:T(8,128)(2,...) custom-call(bf16[2,1,1024,768]{3,2,1,0:T(8,128)(2,1)} %x_hbm.1, ...), custom_call_target="tpu_custom_call" | custom-call | tf_op jit(solution)/shard_map/pallas_call | solution.py:1284
  276.5 15.9 %shard_map.169 = (f32[768,3072]{1,0:T(8,128)}, f32[3840,768]{1,0:T(8,128)}, bf16[1,2,1,1024,768]{4,3,2,1,0:T(8,128)(2,1)}, bf16[1,2,1,1024,768]{4,3,2,1,0:T(8,12...) custom-call(bf16[768,3072]{1,0:T(8,128)(2,1)} %get-tuple-element.26., ...), custom_call_target="tpu_custom_call" | custom-call | tf_op jit(solution)/shard_map/pallas_call | solution.py:1412

commit v3 on v2

--- a/solution.py
+++ b/solution.py
@@ -153,15 +153,13 @@
 
     @pl.when(stage > 0)
     def _():
-        pl.semaphore_signal(
-            barrier, inc=1, device_id={"section": section - 2}, device_id_type=MESH
-        )
+        for other in (section - 2, section - 1 - 2 * core):
+            pl.semaphore_signal(barrier, inc=1, device_id={"section": other}, device_id_type=MESH)
 
     @pl.when(stage < stages - 1)
     def _():
-        pl.semaphore_signal(
-            barrier, inc=1, device_id={"section": section + 2}, device_id_type=MESH
-        )
+        for other in (section + 2, section + 3 - 2 * core):
+            pl.semaphore_signal(barrier, inc=1, device_id={"section": other}, device_id_type=MESH)
 
     def entry_copy(chunk):
         rows = pl.ds(chunk * CHUNK, CHUNK)
@@ -219,7 +217,7 @@
 
     has_previous = jnp.where(stage > 0, 1, 0)
     has_next = jnp.where(stage < stages - 1, 1, 0)
-    pl.semaphore_wait(barrier, 1 + count + has_previous + has_next)
+    pl.semaphore_wait(barrier, 1 + count + 2 * (has_previous + has_next))
 
     small_remotes = [
         pltpu.make_async_remote_copy(
@@ -695,7 +693,7 @@
             entry_remote(chunk).wait_send()
 
     reduce_phase(
-        count, channels, pool, early, kept, early_hbm, totals, mix_back, in_hbm, out_hbm, total_hbm, *reducing
+        sections, count, channels, pool, early, kept, early_hbm, totals, mix_back, in_hbm, out_hbm, total_hbm, *reducing
     )
 
     for copy in fin_copies:
@@ -724,6 +722,7 @@
 BLOCKS = C_BLOCKS + T_BLOCKS
 PLACES = (8, 9, 0, 1, 2, 10, 3, 11, 4, 5, 6, 12, 7)
 PAIRED = 8
+LENT = 3
 
 
 def lookup(index, table):
@@ -738,6 +737,10 @@
     sizes = (2 * line * pieces[0], line * pieces[1])
     counts = (-(-PAIRED * half // sizes[0]), -(-(BLOCKS - PAIRED) * half // sizes[1]))
     return pieces, sizes, counts
+
+
+def lends(sections, line, half):
+    return sections == 4 and line == 4 and reduce_plan(line, half)[1:] == ((half, half), (8, 5))
 
 
 def ready_times(first, size, count, half):
@@ -752,22 +755,41 @@
 
 
 COMPUTE = 2
-ORDER_OF_FOUR = (
-    2000, 1000, 2010, 1010, 2020, 1001, 2030, 2040, 20, 1011, 1002, 2050, 1020, 2060, 2070, 1003,
-    21, 1012, 2080, 40, 1021, 2090, 2100, 1004, 22, 1013, 2110, 1022, 41, 10, 2120, 1005,
-    1014, 23, 1023, 42, 1006, 11, 1040, 1015, 24, 1024, 43, 1007, 50, 1041, 0, 12,
-    1016, 1025, 25, 51, 1042, 1, 30, 1017, 52, 1026, 13, 26, 1043, 2, 53, 1027,
-    31, 27, 3, 60, 14, 32, 1044, 4, 1030, 15, 61, 33, 70, 1045, 5, 54,
-    1031, 16, 62, 1046, 71, 6, 55, 1047, 1032, 72, 17, 56, 63, 7, 57, 73,
-    1033, 34, 44, 64, 35, 74, 45, 65, 75, 36, 46, 1034, 76, 66, 37, 47,
-    1035, 77, 67, 1036, 1037,
+ORDERS_OF_FOUR = (
+    (
+        2000, 1000, 2010, 1010, 2020, 1001, 2030, 2040, 20, 1011, 1002, 2050, 1020, 2060, 2070, 1003,
+        21, 1012, 2080, 40, 1021, 2090, 1004, 2100, 22, 1013, 2110, 1022, 41, 10, 1005, 2120,
+        1014, 23, 1023, 42, 1006, 11, 1040, 1015, 24, 1024, 43, 1007, 50, 1041, 0, 12,
+        1016, 1025, 25, 51, 1042, 1, 1017, 52, 1026, 13, 26, 1043, 2, 53, 1027, 27,
+        3, 60, 14, 1044, 4, 70, 1030, 15, 61, 1045, 5, 54, 1031, 16, 62, 1046,
+        71, 6, 55, 1047, 1032, 72, 17, 56, 7, 63, 57, 73, 1033, 44, 64, 74,
+        45, 65, 75, 46, 1034, 76, 66, 47, 1035, 77, 67, 1036, 1037,
+    ),
+    (
+        2000, 1000, 2010, 1010, 2020, 1001, 2030, 2040, 20, 1011, 1002, 2050, 1020, 2060, 2070, 1003,
+        21, 1012, 2080, 40, 1021, 2090, 2100, 1004, 22, 1013, 2110, 1022, 41, 10, 2120, 1005,
+        1014, 23, 1023, 42, 1006, 11, 1040, 1015, 24, 1024, 43, 1007, 50, 1041, 0, 12,
+        1016, 1025, 25, 1050, 51, 1042, 1, 30, 1017, 52, 1026, 1051, 13, 26, 1043, 2,
+        53, 1027, 31, 1052, 27, 3, 60, 14, 32, 1044, 4, 1053, 1030, 15, 61, 33,
+        70, 1045, 5, 1054, 54, 1031, 16, 62, 1046, 71, 6, 1055, 55, 1047, 1032, 72,
+        17, 56, 63, 1056, 7, 57, 73, 1033, 34, 44, 64, 1057, 35, 74, 45, 65,
+        75, 36, 46, 1034, 76, 66, 37, 47, 1035, 77, 67, 1036, 1037,
+    ),
+    (
+        2000, 1000, 2010, 1010, 2020, 1001, 2030, 2040, 20, 1011, 1002, 2050, 1020, 2060, 2070, 1003,
+        21, 1012, 2080, 40, 1021, 2090, 2100, 1004, 22, 1013, 2110, 1022, 41, 10, 2120, 1005,
+        1014, 23, 1023, 42, 1006, 11, 1040, 1015, 24, 1024, 43, 1007, 50, 1041, 0, 12,
+        1016, 1025, 25, 51, 1042, 1, 30, 1017, 52, 1026, 13, 26, 1043, 2, 53, 1027,
+        31, 27, 3, 60, 14, 32, 1044, 4, 1030, 15, 61, 33, 70, 1045, 5, 54,
+        1031, 16, 62, 1046, 71, 6, 55, 1047, 1032, 72, 17, 56, 63, 7, 57, 73,
+        1033, 34, 44, 64, 35, 74, 45, 65, 75, 36, 46, 1034, 76, 66, 37, 47,
+        1035, 77, 67, 1036, 1037,
+    ),
 )
 
 
 def event_order(line, half):
     _, sizes, counts = reduce_plan(line, half)
-    if line == 4 and counts == (8, 5):
-        return [(code // 1000, code // 10 % 100, code % 10) for code in ORDER_OF_FOUR]
     firsts = (0, counts[0] * sizes[0])
     steps = [(block, 0, (COMPUTE, block, 0)) for block in range(BLOCKS)]
     for kind in range(2):
@@ -777,7 +799,14 @@
     return [step for _, _, step in sorted(steps)]
 
 
+def stage_orders(sections, line, half):
+    if lends(sections, line, half):
+        return [[(code // 1000, code // 10 % 100, code % 10) for code in order] for order in ORDERS_OF_FOUR]
+    return [event_order(line, half)]
+
+
 def reduce_phase(
+    sections,
     count,
     channels,
     pool,
@@ -804,6 +833,8 @@
     spread_send0,
     spread_sem1,
     spread_send1,
+    lend_sem,
+    lend_send,
     give_sem,
     give_send,
     give_recv,
@@ -818,6 +849,8 @@
     half = channels // 2
     pieces, sizes, counts = reduce_plan(line, half)
     firsts = (0, counts[0] * sizes[0])
+    lent = lends(sections, line, half)
+    lender, borrower = section == 1, section == sections - 1
     partner = {"section": section + 1 - 2 * core}
     across = {"dp": dp_index + 1 - 2 * y}
 
@@ -825,7 +858,7 @@
         return {"dp": lax.rem(dp_index + offset, count)}
 
     length, chunks = kept.shape[1], early.shape[1] - 2
-    starts, _ = pool_plan(count, channels, length, 0)
+    starts, _ = pool_plan(sections, count, channels, length, 0)
     mine = pool.at[pl.ds(starts[0], starts[1] - starts[0])]
     theirs = Stack(pool, starts[1], half)
     pair_landing = Stack(pool, starts[2], sizes[0] // 2)
@@ -845,6 +878,9 @@
     pl.when(z < line - 1)(lambda: ready(right_peer))
     pl.when(z > 0)(lambda: ready(left_peer))
     neighbours = 2 + jnp.where(z < line - 1, 1, 0) + jnp.where(z > 0, 1, 0)
+    if lent:
+        pl.when(borrower)(lambda: ready({"section": section - 2}))
+        neighbours = neighbours + jnp.where(lender, 1, 0)
 
     small_pair = pltpu.make_async_remote_copy(
         src_ref=totals.at[1 - core],
@@ -930,6 +966,16 @@
 
         pair_copy(block).start()
 
+    def lend_copy():
+        return pltpu.make_async_remote_copy(
+            src_ref=mine.at[pl.ds(LENT * half, half)],
+            dst_ref=mine.at[pl.ds(BLOCKS * half, half)],
+            send_sem=lend_send.at[0],
+            recv_sem=lend_sem.at[0],
+            device_id={"section": section + 2},
+            device_id_type=MESH,
+        )
+
     def for_me(block):
         rows = block_rows(block)
 
@@ -938,9 +984,11 @@
             mine[rows, :] = (gradient + mine[rows, :].astype(F32)).astype(BF16)
 
         product(block, core, add)
+        if lent:
+            pl.when(lender & (block == PLACES.index(LENT)))(lambda: lend_copy().start())
         pl.when(block < 4)(lambda: time_mix_back(block).start())
 
-    blocks_at = tuple(PLACES.index(place) for place in range(BLOCKS))
+    blocks_at = tuple(PLACES.index(place) for place in (*range(BLOCKS), LENT))
 
     def give(kind, group, start):
         size = pieces[kind]
@@ -950,7 +998,9 @@
         row = core * half + start - place * half
 
         def copies(owner, target):
-            @pl.when(owner == core)
+            foreign = kind == 1 and lent and group == counts[1]
+
+            @pl.when((owner == core) & ~jnp.bool_(foreign))
             def _():
                 pltpu.make_async_copy(mine.at[rows], target, give_sem.at[0]).start()
 
@@ -964,9 +1014,12 @@
                     device_id_type=MESH,
                 )
 
-            @pl.when(owner != core)
+            @pl.when((owner != core) & ~jnp.bool_(foreign))
             def _():
                 remote(partner).start()
+
+            if kind == 1 and lent:
+                pl.when(foreign)(lambda: remote({"section": section - core + owner - 2}).start())
 
             if kind == 0:
                 remote({"section": section - core + owner, "dp": dp_index + 1 - 2 * y}).start()
@@ -1146,6 +1199,9 @@
             spreading(0, group, turn - line)
 
     def event1(group, turn):
+        if lent:
+            pl.when((turn == 0) & (group == counts[1]))(lambda: lend_copy().wait_recv())
+
         @pl.when(turn < line)
         def _():
             passing(1, group, turn)
@@ -1171,18 +1227,34 @@
     spare = firsts[1] + counts[1] * sizes[1] - BLOCKS * half
     if spare:
         mine[pl.ds(BLOCKS * half, spare), :] = jnp.zeros((spare, channels), BF16)
-    order = [(COMPUTE, 0, 0)]
-    for kind, group, turn in event_order(line, half):
-        if kind == COMPUTE:
-            order += [(COMPUTE, group + 1, 0)] * (group + 1 < BLOCKS) + [(COMPUTE, group, 1)]
-        else:
-            order.append((kind, group, turn))
-    codes = [kind * 1024 + group * 64 + turn for kind, group, turn in order]
-    steps = len(codes)
-    words = tuple(a + 4096 * b for a, b in zip(codes[::2], (codes + [0])[1::2], strict=True))
+    tables = []
+    for events in stage_orders(sections, line, half):
+        order = [(COMPUTE, 0, 0)]
+        for kind, group, turn in events:
+            if kind == COMPUTE:
+                order += [(COMPUTE, group + 1, 0)] * (group + 1 < BLOCKS) + [(COMPUTE, group, 1)]
+            else:
+                order.append((kind, group, turn))
+        tables.append([kind * 1024 + group * 64 + turn for kind, group, turn in order])
+    most = max(len(table) for table in tables)
+    packed = []
+    for table in tables:
+        filled = table + [0] * (most + most % 2 - len(table))
+        packed.append(tuple(a + 4096 * b for a, b in zip(filled[::2], filled[1::2], strict=True)))
+
+    def mine_of(values):
+        if len(values) == 1:
+            return values[0]
+        if len(set(values)) == 1:
+            return jnp.int32(values[0])
+        return jnp.where(lender, values[0], jnp.where(borrower, values[1], values[2]))
+
+    steps = mine_of([len(table) for table in tables])
 
     def take(index, _):
-        word = lookup(index // 2, words)
+        word = jnp.int32(0)
+        for at, values in enumerate(zip(*packed, strict=True)):
+            word = jnp.where(index // 2 == at, mine_of(values), word)
         code = jnp.where(index % 2 == 0, word % 4096, word // 4096)
         kind, group, turn = code // 1024, code // 64 % 16, code % 64
 
@@ -1206,8 +1278,13 @@
     total_copy = pltpu.make_async_copy(small.at[0], total_hbm, small_sem.at[0])
     total_copy.start()
 
+    def summed_here(kind, group):
+        if not lent:
+            return group >= 0
+        return (borrower | (group != counts[1])) if kind else (~lender | (group != LENT))
+
     def over_done(group, _):
-        over(group).wait_send()
+        pl.when(summed_here(0, group))(lambda: over(group).wait_send())
         return 0
 
     for block in range(BLOCKS - 2, BLOCKS):
@@ -1220,11 +1297,11 @@
                 for direction in range(2):
                     behind = z if direction == 0 else line - 1 - z
 
-                    @pl.when(step < line - 1 - behind)
+                    @pl.when((step < line - 1 - behind) & summed_here(kind, group))
                     def _():
                         sum_copy(kind, group, direction, step).wait_send()
 
-                    @pl.when((step <= behind) & (behind < line - 1))
+                    @pl.when((step <= behind) & (behind < line - 1) & summed_here(kind, group))
                     def _():
                         spread_copy(kind, group, direction, step, 0).wait_send()
 
@@ -1232,7 +1309,10 @@
 
             return lax.fori_loop(0, line - 1, step_done, 0)
 
-        lax.fori_loop(0, counts[kind], group_done, 0)
+        lax.fori_loop(0, counts[kind] + kind * lent, group_done, 0)
+
+    if lent:
+        pl.when(lender)(lambda: lend_copy().wait_send())
 
     def taken(rows, sem):
         if rows:
@@ -1243,22 +1323,30 @@
     whole = [half // 2 if pair else half for pair in paired]
     by_kind = (range(C_BLOCKS, BLOCKS), range(C_BLOCKS))
     for own in range(2):
-
-        @pl.when(core == own)
-        def _():
+        for last in range(2):
             local = sum(whole[block] for block in by_kind[own])
             crossed = sum(half // 2 for block in range(BLOCKS) if paired[block])
             other = sum(whole[block] for block in by_kind[1 - own])
-            taken(local, give_sem)
-            taken(other + crossed, give_send)
-            taken(len(by_kind[own]) * channels - local, give_recv)
+            if lent and own and last:
+                other += half
+            elif lent and own:
+                crossed -= half // 2
+                local -= whole[PLACES.index(LENT)]
+            received = len(by_kind[own]) * channels - local
+
+            @pl.when((core == own) & ((section >= 2) == bool(last)))
+            def _(local=local, sent=other + crossed, received=received):
+                taken(local, give_sem)
+                taken(sent, give_send)
+                taken(received, give_recv)
 
     total_copy.wait()
 
 
-def pool_plan(count, channels, length, slots):
+def pool_plan(sections, count, channels, length, slots):
     half, line = channels // 2, count // 2
     pieces, sizes, counts = reduce_plan(line, half)
+    counts = (counts[0], counts[1] + lends(sections, line, half))
     heights = (
         counts[0] * sizes[0] + counts[1] * sizes[1],
         2 * half,
@@ -1279,8 +1367,9 @@
     slots = 9 + hidden_blocks
     line = count // 2
     _, _, counts = reduce_plan(line, channels // 2)
+    counts = (counts[0], counts[1] + lends(sections, line, channels // 2))
     hops = [dma((counts[kind], 2, line - 1)) for kind in range(2)]
-    _, pool_rows = pool_plan(count, channels, length, slots)
+    _, pool_rows = pool_plan(sections, count, channels, length, slots)
     return pl.pallas_call(
         functools.partial(chain_kernel, sections, length, channels, hidden_blocks, count),
         out_shape=(
@@ -1346,6 +1435,8 @@
             dma((1,)),
             dma((1,)),
             dma((1,)),
+            dma((1,)),
+            dma((1,)),
             dma((count + 1,)),
             dma((count + 1,)),
         ],
@@ -1356,7 +1447,6 @@
 
 
 def finish_kernel(
-    steps,
     in_short,
     out_short,
     outs_in,
@@ -1373,45 +1463,115 @@
     bias,
     rates,
     wkv,
+    in_held,
+    out_held,
+    in_made,
+    out_made,
+    tokens_held,
+    load_sem,
+    store_sem,
 ):
     holds_channel_mix = lax.axis_index("section") % 2 == 1
-    step = pl.program_id(0)
-
-    @pl.when(step == 0)
-    def _():
-        for micro in range(2):
-            normed[0, micro] = fin[micro, 0:1]
-            for row in range(2):
-                states[0, row, micro] = fin[micro, 1 + row : 2 + row]
-        gain[...] = total[GAIN : GAIN + 1]
-        bias[...] = total[BIAS : BIAS + 1]
-        for row in range(3):
-            rates[row] = total[RATES + row : RATES + row + 1]
-        wkv[0] = total[DECAY : DECAY + 2]
-
-    in_wide[...] = in_short[...].astype(F32)
-    out_wide[...] = jnp.where(holds_channel_mix, out_short[...].astype(F32), 0.0)
-    outs[0, :, 0] = outs_in[...]
-    grads[0, :, 0] = grads_in[...]
+    sources, targets = (in_short, out_short), (in_wide, out_wide)
+    held, made = (in_held, out_held), (in_made, out_made)
+    parts = 8
+    jobs = [(which, part) for part in range(parts) for which in range(2)]
+
+    def rows_of(which, part):
+        tall = sources[which].shape[0] // parts
+        return pl.ds(part * tall, tall)
+
+    def load(which, part):
+        rows = rows_of(which, part)
+        return pltpu.make_async_copy(
+            sources[which].at[rows], held[which].at[rows], load_sem.at[which, part]
+        )
+
+    def store(which, part):
+        rows = rows_of(which, part)
+        return pltpu.make_async_copy(
+            made[which].at[rows], targets[which].at[rows], store_sem.at[which, part]
+        )
+
+    def start(which, part):
+        if which:
+            pl.when(holds_channel_mix)(lambda: load(which, part).start())
+        else:
+            load(which, part).start()
+
+    token_loads = [
+        pltpu.make_async_copy(source, tokens_held.at[at], load_sem.at[2, at])
+        for at, source in enumerate((outs_in, grads_in))
+    ]
+    token_stores = [
+        pltpu.make_async_copy(tokens_held.at[at], target.at[0, :, 0], store_sem.at[2, at])
+        for at, target in enumerate((outs, grads))
+    ]
+    ahead = 6
+    for job in jobs[:2]:
+        start(*job)
+    for copy in token_loads:
+        copy.start()
+    for job in jobs[2:ahead]:
+        start(*job)
+    for micro in range(2):
+        normed[0, micro] = fin[micro, 0:1]
+        for row in range(2):
+            states[0, row, micro] = fin[micro, 1 + row : 2 + row]
+    gain[...] = total[GAIN : GAIN + 1]
+    bias[...] = total[BIAS : BIAS + 1]
+    for row in range(3):
+        rates[row] = total[RATES + row : RATES + row + 1]
+    wkv[0] = total[DECAY : DECAY + 2]
+    for at, (which, part) in enumerate(jobs):
+        tall = sources[which].shape[0] // parts
+        step = 32 if which == 0 else 96
+
+        def widen(index, _):
+            rows = pl.ds(pl.multiple_of(part * tall + index * step, step), step)
+            made[which][rows, :] = held[which][rows, :].astype(F32)
+            return 0
+
+        def clear(index, _):
+            rows = pl.ds(pl.multiple_of(part * tall + index * step, step), step)
+            made[which][rows, :] = jnp.zeros((step, made[which].shape[1]), F32)
+            return 0
+
+        def widened():
+            load(which, part).wait()
+            lax.fori_loop(0, tall // step, widen, 0)
+
+        if which:
+            pl.when(holds_channel_mix)(widened)
+
+            @pl.when(~holds_channel_mix)
+            def _():
+                lax.fori_loop(0, tall // step, clear, 0)
+
+        else:
+            widened()
+        if at + ahead < len(jobs):
+            start(*jobs[at + ahead])
+        store(which, part).start()
+        if at < 2:
+            token_loads[at].wait()
+            token_stores[at].start()
+    for job in jobs:
+        store(*job).wait()
+    for copy in token_stores:
+        copy.wait()
 
 
 def finished_outputs(in_short, out_short, outs, grads, fin, total):
-    steps = 8
     length, channels = outs.shape[1:]
     whole = pl.BlockSpec(memory_space=pltpu.VMEM)
-    kept = pl.BlockSpec((2, length // steps, channels), lambda i: (0, i, 0))
-    placed = pl.BlockSpec((1, 2, 1, length // steps, channels), lambda i: (0, 0, 0, i, 0))
-
-    def spec(array):
-        rows, columns = array.shape
-        return pl.BlockSpec((rows // steps, columns), lambda i: (i, 0))
+    anywhere = pl.BlockSpec(memory_space=pl.ANY)
 
     def shape(*sizes, dtype=F32):
         return jax.ShapeDtypeStruct(sizes, dtype)
 
     in_wide, out_wide, *rest = pl.pallas_call(
-        functools.partial(finish_kernel, steps),
-        grid=(steps,),
+        finish_kernel,
         out_shape=(
             shape(*in_short.shape),
             shape(*out_short.shape),
@@ -1424,8 +1584,17 @@
             shape(3, 1, channels),
             shape(1, 2, channels),
         ),
-        in_specs=[spec(in_short), spec(out_short), kept, kept, whole, whole],
-        out_specs=(spec(in_short), spec(out_short), placed, placed) + (whole,) * 6,
+        in_specs=[anywhere] * 4 + [whole] * 2,
+        out_specs=(anywhere,) * 4 + (whole,) * 6,
+        scratch_shapes=[
+            pltpu.VMEM(in_short.shape, BF16),
+            pltpu.VMEM(out_short.shape, BF16),
+            pltpu.VMEM(in_short.shape, F32),
+            pltpu.VMEM(out_short.shape, F32),
+            pltpu.VMEM((2, 2, length, channels), BF16),
+            pltpu.SemaphoreType.DMA((3, 8)),
+            pltpu.SemaphoreType.DMA((3, 8)),
+        ],
         compiler_params=pltpu.CompilerParams(vmem_limit_bytes=VMEM_BYTES),
     )(in_short, out_short, outs, grads, fin, total)
     *rest, rates, wkv = rest

time: 293 us -> 290 us (0.990)
  Pallas kernels: 292 us -> 287 us
where the time goes in v3:
time: 290 us; the launch traced here: 288 us
  Pallas kernels  287 us (99%)
    pallas_call x1, Pallas kernels, chain(): pl.pallas_call(functools.partial(chain_kernel, sections, length, channels...  273 us
    pallas_call x1, Pallas kernels, finished_outputs(): pl.pallas_call(finish_kernel, out_shape=(shape(*in_short.shape), shape(*o...  13.9 us

profile of v3, /device:TPU:0, one launch (start us, length us, event | category | flops | bytes accessed | tf_op | source)
XLA Modules:
  0.0 287.6 jit_solution(10133963511428278831)
XLA Ops:
  0.6 272.9 %shard_map.168 = (bf16[2,1024,768]{2,1,0:T(8,128)(2,1)}, bf16[2,1024,768]{2,1,0:T(8,128)(2,1)}, f32[2,8,768]{2,1,0:T(8,128)}, bf16[6,1024,768]{2,1,0:T(8,128)(2,...) custom-call(bf16[2,1,1024,768]{3,2,1,0:T(8,128)(2,1)} %x_hbm.1, ...), custom_call_target="tpu_custom_call" | custom-call | tf_op jit(solution)/shard_map/pallas_call | solution.py:1373
  273.6 13.9 %shard_map.169 = (f32[768,3072]{1,0:T(8,128)}, f32[3840,768]{1,0:T(8,128)}, bf16[1,2,1,1024,768]{4,3,2,1,0:T(8,128)(2,1)}, bf16[1,2,1,1024,768]{4,3,2,1,0:T(8,12...) custom-call(bf16[768,3072]{1,0:T(8,128)(2,1)} %get-tuple-element.26., ...), custom_call_target="tpu_custom_call" | custom-call | tf_op jit(solution)/shard_map/pallas_call | solution.py:1573

commit v4 on v3

--- a/solution.py
+++ b/solution.py
@@ -11,8 +11,9 @@
 F32 = jnp.float32
 BF16 = jnp.bfloat16
 CHUNK = 256
-ROWS = 32
-UNROLL = 4
+ROWS = 64
+UNROLL = 2
+TALL = 64
 VMEM_BYTES = (64 << 20) - (128 << 10)
 
 T_MIX0, T_MIX2, T_MIX1, T_GATED, C_MIX0, C_MIX1 = 0, 1, 2, 3, 4, 5
@@ -131,6 +132,7 @@
     partner = {"section": section + 1 - 2 * core}
     chunks = length // CHUNK
     blocks = CHUNK // ROWS
+    tall_blocks = CHUNK // TALL
     time_blocks = 4
     last_stage = stage == stages - 1
     weights = Stack(pool, 0, channels)
@@ -303,6 +305,7 @@
         return center * root, root
 
     row_index = lax.broadcasted_iota(jnp.int32, (ROWS, channels), 0)
+    tall_index = lax.broadcasted_iota(jnp.int32, (TALL, channels), 0)
 
     def token_mix(kind, source, base, side, slots, carry_row):
         gain, bias = gains[kind], biases[kind]
@@ -356,9 +359,9 @@
             wide[slot] = nn(early[side, slot], weights[slot])
 
         def weighted(index, _):
-            start = pl.multiple_of(index * ROWS, ROWS)
-            local = pl.ds(start, ROWS)
-            whole = pl.ds(pl.multiple_of(base + start, ROWS), ROWS)
+            start = pl.multiple_of(index * TALL, TALL)
+            local = pl.ds(start, TALL)
+            whole = pl.ds(pl.multiple_of(base + start, TALL), TALL)
             value = wide[1, local, :]
             power = jnp.exp(wide[0, local, :])
             wide[0, local, :] = power
@@ -369,7 +372,7 @@
             kept[T_DV, whole, :] = value.astype(BF16)
             return 0
 
-        lax.fori_loop(0, blocks, weighted, 0)
+        lax.fori_loop(0, tall_blocks, weighted, 0)
         wide[3] = nn(triangles[0, :, pl.ds(0, CHUNK)], pairs[pl.ds(0, CHUNK), pl.ds(0, channels)])
         wide[4] = nn(
             triangles[0, :, pl.ds(0, CHUNK)], pairs[pl.ds(0, CHUNK), pl.ds(channels, channels)]
@@ -377,10 +380,10 @@
         upper, lower = carry[1:2], carry[2:3]
 
         def averaged(index, _):
-            start = pl.multiple_of(index * ROWS, ROWS)
-            local = pl.ds(start, ROWS)
-            whole = pl.ds(pl.multiple_of(base + start, ROWS), ROWS)
-            place = (row_index + start).astype(F32)
+            start = pl.multiple_of(index * TALL, TALL)
+            local = pl.ds(start, TALL)
+            whole = pl.ds(pl.multiple_of(base + start, TALL), TALL)
+            place = (tall_index + start).astype(F32)
             grown = jnp.exp((CHUNK - place) * rate)
             faded = tables[1, local, :]
             power, value = wide[0, local, :], wide[1, local, :]
@@ -393,14 +396,14 @@
             states[1, whole, :] = before_lower
             kept[T_DQ, whole, :] = gate.astype(BF16)
             early[side, T_GATED, local, :] = (gate * average).astype(BF16)
-            tail = slice(ROWS - 8, ROWS)
+            tail = slice(TALL - 8, TALL)
             after_upper = step * before_upper[tail] + power[tail] * value[tail]
             after_lower = step * before_lower[tail] + power[tail]
             carry_next[0:1] = after_upper[7:8]
             carry_next[1:2] = after_lower[7:8]
             return 0
 
-        lax.fori_loop(0, blocks, averaged, 0)
+        lax.fori_loop(0, tall_blocks, averaged, 0)
         carry[1:3] = carry_next[0:2]
 
         @pl.when(chunk == 0)
@@ -440,9 +443,9 @@
         wide[0] = total
 
         def joined(index, _):
-            start = pl.multiple_of(index * ROWS, ROWS)
-            local = pl.ds(start, ROWS)
-            whole = pl.ds(pl.multiple_of(base + start, ROWS), ROWS)
+            start = pl.multiple_of(index * TALL, TALL)
+            local = pl.ds(start, TALL)
+            whole = pl.ds(pl.multiple_of(base + start, TALL), TALL)
             gate = jax.nn.sigmoid(wide[1, local, :])
             value = wide[0, local, :]
             kept[C_DKV, whole, :] = gate.astype(BF16)
@@ -450,7 +453,7 @@
             top[whole, :] = (mid[whole, :].astype(F32) + gate * value).astype(BF16)
             return 0
 
-        lax.fori_loop(0, blocks, joined, 0)
+        lax.fori_loop(0, tall_blocks, joined, 0)
 
         @pl.when(stage < stages - 1)
         def _():
@@ -577,7 +580,7 @@
         pltpu.make_async_copy(upstream.at[rows], upstream.at[rows], up_sem.at[chunk]).wait()
 
         def split(index, _):
-            whole = pl.ds(pl.multiple_of(base + index * ROWS, ROWS), ROWS)
+            whole = pl.ds(pl.multiple_of(base + index * TALL, TALL), TALL)
             above = upstream[whole, :].astype(F32)
             gate = kept[C_DKV, whole, :].astype(F32)
             value = kept[C_DQ, whole, :].astype(F32)
@@ -586,7 +589,7 @@
             kept[C_DQ, whole, :] = (d_value * value * (1.0 - gate)).astype(BF16)
             return 0
 
-        lax.fori_loop(0, blocks, split, 0)
+        lax.fori_loop(0, tall_blocks, split, 0)
 
         for index in range(hidden_blocks):
             d_hidden = nt(kept[C_DKV, rows, :], weights[8 + index])
@@ -602,9 +605,9 @@
         wide[0] = nt(kept[T_G, rows, :], weights[3])
 
         def inputs(index, _):
-            start = pl.multiple_of(index * ROWS, ROWS)
-            local = pl.ds(start, ROWS)
-            whole = pl.ds(pl.multiple_of(base + start, ROWS), ROWS)
+            start = pl.multiple_of(index * TALL, TALL)
+            local = pl.ds(start, TALL)
+            whole = pl.ds(pl.multiple_of(base + start, TALL), TALL)
             power = kept[T_DK, whole, :].astype(F32)
             value = kept[T_DV, whole, :].astype(F32)
             gate = kept[T_DQ, whole, :].astype(F32)
@@ -620,21 +623,21 @@
             for column, term in ((0, scaled), (channels, -scaled * average)):
                 high = term.astype(BF16)
                 pairs[local, pl.ds(column, channels)] = high
-                pairs[pl.ds(pl.multiple_of(CHUNK + start, ROWS), ROWS), pl.ds(column, channels)] = (
+                pairs[pl.ds(pl.multiple_of(CHUNK + start, TALL), TALL), pl.ds(column, channels)] = (
                     term - high.astype(F32)
                 ).astype(BF16)
             return 0
 
-        lax.fori_loop(0, blocks, inputs, 0)
+        lax.fori_loop(0, tall_blocks, inputs, 0)
         wide[3] = nn(triangles[1], pairs[:, pl.ds(0, channels)])
         wide[4] = nn(triangles[1], pairs[:, pl.ds(channels, channels)])
         alpha_after, beta_after = carry[1:2], carry[2:3]
 
         def outputs(index, _):
-            start = pl.multiple_of((blocks - 1 - index) * ROWS, ROWS)
-            local = pl.ds(start, ROWS)
-            whole = pl.ds(pl.multiple_of(base + start, ROWS), ROWS)
-            place = (row_index + start).astype(F32)
+            start = pl.multiple_of((tall_blocks - 1 - index) * TALL, TALL)
+            local = pl.ds(start, TALL)
+            whole = pl.ds(pl.multiple_of(base + start, TALL), TALL)
+            place = (tall_index + start).astype(F32)
             grown = jnp.exp((place + 1.0) * rate)
             faded = tables[0, local, :]
             alpha = grown * wide[3, local, :] + faded * alpha_after
@@ -654,7 +657,7 @@
             carry_next[1:2] = step * beta[0:1] - unit[0:1] * average[0:1]
             return 0
 
-        lax.fori_loop(0, blocks, outputs, 0)
+        lax.fori_loop(0, tall_blocks, outputs, 0)
         carry[1:3] = carry_next[0:2]
         wide[0] = nt(kept[T_DK, rows, :], weights[0])
         wide[1] = nt(kept[T_DQ, rows, :], weights[2])

time: 290 us -> 289 us (level)
  no operation moved by 1% of the time
where the time goes in v4:
time: 289 us; the launch traced here: 287 us
  Pallas kernels  286 us (99%)
    pallas_call x1, Pallas kernels, chain(): pl.pallas_call(functools.partial(chain_kernel, sections, length, channels...  272 us
    pallas_call x1, Pallas kernels, finished_outputs(): pl.pallas_call(finish_kernel, out_shape=(shape(*in_short.shape), shape(*o...  13.9 us

profile of v4, /device:TPU:0, one launch (start us, length us, event | category | flops | bytes accessed | tf_op | source)
XLA Modules:
  0.0 286.7 jit_solution(16049362099446175563)
XLA Ops:
  0.6 272.0 %shard_map.168 = (bf16[2,1024,768]{2,1,0:T(8,128)(2,1)}, bf16[2,1024,768]{2,1,0:T(8,128)(2,1)}, f32[2,8,768]{2,1,0:T(8,128)}, bf16[6,1024,768]{2,1,0:T(8,128)(2,...) custom-call(bf16[2,1,1024,768]{3,2,1,0:T(8,128)(2,1)} %x_hbm.1, ...), custom_call_target="tpu_custom_call" | custom-call | tf_op jit(solution)/shard_map/pallas_call | solution.py:1376
  272.7 13.9 %shard_map.169 = (f32[768,3072]{1,0:T(8,128)}, f32[3840,768]{1,0:T(8,128)}, bf16[1,2,1,1024,768]{4,3,2,1,0:T(8,128)(2,1)}, bf16[1,2,1,1024,768]{4,3,2,1,0:T(8,12...) custom-call(bf16[768,3072]{1,0:T(8,128)(2,1)} %get-tuple-element.26., ...), custom_call_target="tpu_custom_call" | custom-call | tf_op jit(solution)/shard_map/pallas_call | solution.py:1576

commit v5 on v4

--- a/solution.py
+++ b/solution.py
@@ -205,18 +205,19 @@
     def out_block(index):
         return w_out_hbm.at[0, pl.ds(index * channels, channels), :]
 
-    for index in range(4):
-        slot = core * time_blocks + index
-        pltpu.make_async_copy(in_block(index), weights.at[slot], weight_sem.at[slot]).start()
-
-    @pl.when(core == 1)
-    def _():
+    def load_in():
+        for index in range(4):
+            slot = core * time_blocks + index
+            pltpu.make_async_copy(in_block(index), weights.at[slot], weight_sem.at[slot]).start()
+
+    def load_out():
         for index in range(hidden_blocks + 1):
             slot = 8 + index
             pltpu.make_async_copy(
                 out_block(index), weights.at[slot], weight_sem.at[slot]
             ).start()
 
+    pl.when(core == 0)(load_in)
     has_previous = jnp.where(stage > 0, 1, 0)
     has_next = jnp.where(stage < stages - 1, 1, 0)
     pl.semaphore_wait(barrier, 1 + count + 2 * (has_previous + has_next))
@@ -264,6 +265,8 @@
     def _():
         for index in (hidden_blocks, *range(hidden_blocks)):
             out_remote(index).start()
+        load_in()
+        load_out()
 
     row_at = lax.broadcasted_iota(jnp.int32, (CHUNK, 2 * CHUNK), 0)
     column_at = lax.broadcasted_iota(jnp.int32, (CHUNK, 2 * CHUNK), 1)

time: 289 us -> 289 us (level)
  no operation moved by 1% of the time
where the time goes in v5:
time: 289 us; the launch traced here: 287 us
  Pallas kernels  286 us (99%)
    pallas_call x1, Pallas kernels, chain(): pl.pallas_call(functools.partial(chain_kernel, sections, length, channels...  272 us
    pallas_call x1, Pallas kernels, finished_outputs(): pl.pallas_call(finish_kernel, out_shape=(shape(*in_short.shape), shape(*o...  13.9 us

profile of v5, /device:TPU:0, one launch (start us, length us, event | category | flops | bytes accessed | tf_op | source)
XLA Modules:
  0.0 286.7 jit_solution(10586935390979847858)
XLA Ops:
  0.6 272.0 %shard_map.168 = (bf16[2,1024,768]{2,1,0:T(8,128)(2,1)}, bf16[2,1024,768]{2,1,0:T(8,128)(2,1)}, f32[2,8,768]{2,1,0:T(8,128)}, bf16[6,1024,768]{2,1,0:T(8,128)(2,...) custom-call(bf16[2,1,1024,768]{3,2,1,0:T(8,128)(2,1)} %x_hbm.1, ...), custom_call_target="tpu_custom_call" | custom-call | tf_op jit(solution)/shard_map/pallas_call | solution.py:1379
  272.6 13.9 %shard_map.169 = (f32[768,3072]{1,0:T(8,128)}, f32[3840,768]{1,0:T(8,128)}, bf16[1,2,1,1024,768]{4,3,2,1,0:T(8,128)(2,1)}, bf16[1,2,1,1024,768]{4,3,2,1,0:T(8,12...) custom-call(bf16[768,3072]{1,0:T(8,128)(2,1)} %get-tuple-element.26., ...), custom_call_target="tpu_custom_call" | custom-call | tf_op jit(solution)/shard_map/pallas_call | solution.py:1579
